TPU v7x, 32 devices: a whole 2x2x4 slice. The times are simulated.
32 devices in a mesh: dp: 8 (over z, core), fsdp: 4 (over y, x).
Axes of the slice: x: 2, y: 2, z: 4, core: 2. Of those that a mesh axis runs over, the one named last changes fastest.
Arguments:
- node_feat: bfloat16 [32768, 256], P(('dp', 'fsdp')), may hold values from -3 to 3
- out_cot: bfloat16 [32768, 256], P(('dp', 'fsdp')), may hold values from -3 to 3
- node_type: int32 [32768], P(('dp', 'fsdp')), may hold values from 0 to 3
- node_count: int32 [32], P(('dp', 'fsdp')), may hold values from 256 to 1024, as said below
- edge_src: int32 [256, 1024], P(('dp', 'fsdp')), may hold values from 0 to 1023, as said below
- edge_dst: int32 [256, 1024], P(('dp', 'fsdp')), may hold values from 0 to 1023, as said below
- edge_time: int32 [256, 1024], P(('dp', 'fsdp')), may hold values from 0 to 239
- edge_count: int32 [256], P(('dp', 'fsdp')), may hold values from 128 to 1024, as said below
- type_weight: float32 [1024, 1024], P('fsdp'), may hold values from -0.26516504 to 0.26516504
- type_first: float32 [1024, 1024], P('fsdp'), may hold values from -32 to 32
- type_second: float32 [1024, 1024], P('fsdp'), may hold values from 4.096 to 16.384
- type_avg: float32 [1024, 1024], P('fsdp'), may hold values from -0.26516504 to 0.26516504
- edge_weight: float32 [256, 768], P('fsdp'), may hold values from -0.26516504 to 0.26516504
- edge_first: float32 [256, 768], P('fsdp'), may hold values from -128 to 128
- edge_second: float32 [256, 768], P('fsdp'), may hold values from 45.8752 to 183.5008
- edge_avg: float32 [256, 768], P('fsdp'), may hold values from -0.26516504 to 0.26516504
- norm_params: float32 [8, 256], P(None, 'fsdp')
- norm_first: float32 [8, 256], P(None, 'fsdp'), may hold values from -48 to 48
- norm_second: float32 [8, 256], P(None, 'fsdp'), may hold values from 7.3728 to 29.4912
- norm_avg: float32 [8, 256], P(None, 'fsdp')
- mix_params: float32 [68], replicated, may hold values from 0.25 to 1.5
- mix_first: float32 [68], replicated, may hold values from -384 to 384
- mix_second: float32 [68], replicated, may hold values from 461.37344 to 1887.4368
- mix_avg: float32 [68], replicated, may hold values from 0.25 to 1.5
Outputs:
- layer_out: bfloat16 [32768, 256], P(('dp', 'fsdp'))
- input_grad: bfloat16 [32768, 256], P(('dp', 'fsdp'))
- new_type_weight: float32 [1024, 1024], P('fsdp')
- new_type_first: float32 [1024, 1024], P('fsdp')
- new_type_second: float32 [1024, 1024], P('fsdp')
- new_type_avg: float32 [1024, 1024], P('fsdp')
- new_edge_weight: float32 [256, 768], P('fsdp')
- new_edge_first: float32 [256, 768], P('fsdp')
- new_edge_second: float32 [256, 768], P('fsdp')
- new_edge_avg: float32 [256, 768], P('fsdp')
- new_norm_params: float32 [8, 256], P(None, 'fsdp')
- new_norm_first: float32 [8, 256], P(None, 'fsdp')
- new_norm_second: float32 [8, 256], P(None, 'fsdp')
- new_norm_avg: float32 [8, 256], P(None, 'fsdp')
- new_mix_params: float32 [68], replicated
- new_mix_first: float32 [68], replicated
- new_mix_second: float32 [68], replicated
- new_mix_avg: float32 [68], replicated
Inputs may be any that keep to these rules, and one draw needn't show every extreme that they name: `node_count`: each subgraph holds at least 256 live nodes in its first slots, and in every draw one subgraph fills all 1024 slots. `edge_count`: the first that many slots of a relation's row are counted; every live node is the target and the source of some counted edge; in every draw one row is full. `edge_src`: every entry is a live node of its own subgraph. `edge_dst`: every entry is a live node of its own subgraph.
All inputs are finite; a program needn't handle non-finite values.
Results may differ from a plain program's by a relative error of at most 0.012.
The roundings to bfloat16 on the way count: a program that leaves them out, or rounds other values in their place, can miss the bound.
Values may be sent and summed in bfloat16 or wider, within the bound.
No kernel may reach another device: no remote copies, remote signals or barrier semaphores. Data moves between devices by JAX's collectives and lax.ppermute only.
A program may use at most 256 MiB of HBM per device.

v0:
```python
import jax
import jax.numpy as jnp
from jax import lax
from jax.sharding import PartitionSpec as P

D = 256
H = 8
DK = 32
TYPES = 4
REL = 8
TB = 240
STEP = 10


beta_one = 0.9
beta_two = 0.999
adam_eps = 1e-08
decay_rate = 0.01
ema_keep = 0.7
norm_eps = 1e-05
rate_type = 0.2
rate_edge = 0.2
rate_norm = 0.6
rate_mix = 0.6


def time_table():
    steps = lax.broadcasted_iota(jnp.int32, (TB, D), 0).astype(jnp.float32)
    column = lax.broadcasted_iota(jnp.int32, (TB, D), 1)
    freq = jnp.exp(-jnp.log(10000.0) * (2 * (column // 2)).astype(jnp.float32) / D)
    angle = steps * freq
    return jnp.where(column % 2 == 0, jnp.sin(angle), jnp.cos(angle))


def exact_gelu(values):
    return jax.nn.gelu(values, approximate=False)


def spread_types(onehot_low, values):
    row_count = values.shape[0]
    return (onehot_low[:, :, None] * values[:, None, :]).reshape(row_count, TYPES * values.shape[1])


def pick_types(onehot, wide):
    row_count = wide.shape[0]
    return jnp.sum(wide.reshape(row_count, TYPES, -1) * onehot[:, :, None], axis=1)


def contract_rows(left, right):
    return lax.dot_general(
        left, right, (((0,), (0,)), ((), ())), preferred_element_type=jnp.float32
    )


def exact_rows(left, right):
    return lax.dot_general(
        left,
        right,
        (((0,), (0,)), ((), ())),
        precision=lax.Precision.HIGHEST,
        preferred_element_type=jnp.float32,
    )


def against_cols(left, right):
    return lax.dot_general(
        left, right, (((1,), (1,)), ((), ())), preferred_element_type=jnp.float32
    )


def adam_step(param, first, second, avg, grad, rate):
    first_new = beta_one * first + (1.0 - beta_one) * grad
    second_new = beta_two * second + (1.0 - beta_two) * grad * grad
    first_hat = first_new / (1.0 - beta_one**STEP)
    second_hat = second_new / (1.0 - beta_two**STEP)
    param_new = param - rate * (first_hat / (jnp.sqrt(second_hat) + adam_eps) + decay_rate * param)
    avg_new = ema_keep * avg + (1.0 - ema_keep) * param_new
    return (param_new, first_new, second_new, avg_new)


def shards(
    node_feat,
    out_cot,
    node_type,
    node_count,
    edge_src,
    edge_dst,
    edge_time,
    edge_count,
    type_weight,
    type_first,
    type_second,
    type_avg,
    edge_weight,
    edge_first,
    edge_second,
    edge_avg,
    norm_params,
    norm_first,
    norm_second,
    norm_avg,
    mix_params,
    mix_first,
    mix_second,
    mix_avg,
):
    node_total = node_feat.shape[0]
    edge_slots = edge_src.shape[1]
    score_scale = DK ** (-0.5)
    typed_w, edge_w, norm_w = (
        lax.all_gather(type_weight.astype(jnp.bfloat16), "fsdp", axis=0, tiled=True),
        lax.all_gather(edge_weight.astype(jnp.bfloat16), "fsdp", axis=0, tiled=True),
        lax.all_gather(norm_params.astype(jnp.bfloat16), "fsdp", axis=1, tiled=True),
    )
    norm_full = norm_w.astype(jnp.float32)
    mix_full = lax.optimization_barrier(mix_params.astype(jnp.bfloat16)).astype(jnp.float32)
    onehot = (node_type[:, None] == jnp.arange(TYPES, dtype=jnp.int32)[None, :]).astype(jnp.float32)
    onehot_low = onehot.astype(jnp.bfloat16)
    live_mask = (jnp.arange(node_total, dtype=jnp.int32) < node_count[0]).astype(jnp.float32)
    feat_full = node_feat.astype(jnp.float32)
    typed_feat = spread_types(onehot_low, node_feat)
    qkv_node = jnp.dot(typed_feat, typed_w[:, : 3 * D], preferred_element_type=jnp.float32)
    query_node = qkv_node[:, :D]
    keyval = qkv_node[:, D:]
    emb_low = time_table().astype(jnp.bfloat16)
    rte_low = jnp.dot(
        emb_low, edge_w[:, REL * 2 * DK :], preferred_element_type=jnp.float32
    ).astype(jnp.bfloat16)
    kv_types = typed_w[:, D : 3 * D].reshape(TYPES, D, 2 * D)
    time_kv = jnp.einsum(
        "td,sde->ste", rte_low, kv_types, preferred_element_type=jnp.float32
    ).reshape(TYPES * TB, 2 * D)
    rel_blocks = edge_w[:, : REL * 2 * DK].reshape(H, DK, REL, 2, DK)
    rel_prior = mix_full[: REL * H].reshape(REL, H)
    skip_logit = mix_full[REL * H :]
    denom_sum = jnp.zeros((node_total, H), jnp.float32)
    numer_sum = jnp.zeros((node_total, D), jnp.float32)
    kept_edges = []
    for relation in range(REL):
        source = edge_src[relation]
        target = edge_dst[relation]
        bucket = node_type[source] * TB + edge_time[relation]
        valid_edge = (jnp.arange(edge_slots, dtype=jnp.int32) < edge_count[relation]).astype(
            jnp.float32
        )
        kv_edge = (keyval[source] + time_kv[bucket]).astype(jnp.bfloat16)
        key_edge = kv_edge[:, :D].reshape(edge_slots, H, DK)
        val_edge = kv_edge[:, D:].reshape(edge_slots, H, DK)
        key_att = jnp.einsum(
            "ehi,hij->ehj",
            key_edge,
            rel_blocks[:, :, relation, 0, :],
            preferred_element_type=jnp.float32,
        )
        message = jnp.einsum(
            "ehi,hij->ehj",
            val_edge,
            rel_blocks[:, :, relation, 1, :],
            preferred_element_type=jnp.float32,
        )
        q_target = query_node[target].reshape(edge_slots, H, DK)
        raw_score = jnp.sum(key_att * q_target, axis=2)
        weight = valid_edge[:, None] * jnp.exp(
            raw_score * rel_prior[relation][None, :] * score_scale
        )
        denom_sum = denom_sum + jax.ops.segment_sum(weight, target, num_segments=node_total)
        numer_sum = numer_sum + jax.ops.segment_sum(
            (weight[:, :, None] * message).reshape(edge_slots, D), target, num_segments=node_total
        )
        kept_edges.append(
            (
                source,
                target,
                bucket,
                key_edge,
                val_edge,
                key_att,
                message,
                q_target,
                raw_score,
                weight,
            )
        )
    den_safe = denom_sum + 1.0 - live_mask[:, None]
    den_wide = jnp.repeat(den_safe, DK, axis=1)
    agg_node = numer_sum / den_wide
    act_node, gelu_back = jax.vjp(exact_gelu, agg_node)
    act_low = act_node.astype(jnp.bfloat16)
    typed_act = spread_types(onehot_low, act_low)
    trans_node = jnp.dot(typed_act, typed_w[:, 3 * D :], preferred_element_type=jnp.float32)
    alpha_node = jax.nn.sigmoid(jnp.sum(onehot * skip_logit[None, :], axis=1))[:, None]
    resid = alpha_node * trans_node + (1.0 - alpha_node) * feat_full
    mean_node = jnp.mean(resid, axis=1, keepdims=True)
    centered = resid - mean_node
    var_node = jnp.mean(centered * centered, axis=1, keepdims=True)
    inv_std = lax.rsqrt(var_node + norm_eps)
    normed = centered * inv_std
    gain_node = jnp.dot(onehot, norm_full[:TYPES], precision=lax.Precision.HIGHEST)
    bias_node = jnp.dot(onehot, norm_full[TYPES:], precision=lax.Precision.HIGHEST)
    layer_out = (live_mask[:, None] * (normed * gain_node + bias_node)).astype(jnp.bfloat16)
    grad_out = live_mask[:, None] * out_cot.astype(jnp.float32)
    grad_gain = exact_rows(onehot, grad_out * normed)
    grad_bias = exact_rows(onehot, grad_out)
    grad_normed = grad_out * gain_node
    grad_resid = inv_std * (
        grad_normed
        - jnp.mean(grad_normed, axis=1, keepdims=True)
        - normed * jnp.mean(grad_normed * normed, axis=1, keepdims=True)
    )
    dtrans_low = (alpha_node * grad_resid).astype(jnp.bfloat16)
    skip_part = (1.0 - alpha_node) * grad_resid
    grad_alpha = jnp.sum(grad_resid * (trans_node - feat_full), axis=1)
    grad_skip = exact_rows(
        onehot, (grad_alpha * alpha_node[:, 0] * (1.0 - alpha_node[:, 0]))[:, None]
    )[:, 0]
    grad_outproj = contract_rows(typed_act, dtrans_low)
    grad_act = pick_types(onehot, against_cols(dtrans_low, typed_w[:, 3 * D :]))
    grad_agg = gelu_back(grad_act)[0]
    grad_numer = grad_agg / den_wide
    grad_denom = -jnp.sum((grad_agg * agg_node).reshape(node_total, H, DK), axis=2) / den_safe
    dq_sum = jnp.zeros((node_total, D), jnp.float32)
    dkv_sum = jnp.zeros((node_total, 2 * D), jnp.float32)
    dtime_sum = jnp.zeros((TYPES * TB, 2 * D), jnp.float32)
    rel_grads = []
    prior_grads = []
    for relation in range(REL):
        (
            source,
            target,
            bucket,
            key_edge,
            val_edge,
            key_att,
            message,
            q_target,
            raw_score,
            weight,
        ) = kept_edges[relation]
        dnum_edge = grad_numer[target].reshape(edge_slots, H, DK)
        grad_weight = jnp.sum(dnum_edge * message, axis=2) + grad_denom[target]
        grad_score = grad_weight * weight
        prior_grads.append(jnp.sum(grad_score * raw_score, axis=0) * score_scale)
        scaled_score = grad_score * rel_prior[relation][None, :] * score_scale
        dkey_att = (scaled_score[:, :, None] * q_target).astype(jnp.bfloat16)
        dmessage = (weight[:, :, None] * dnum_edge).astype(jnp.bfloat16)
        dq_sum = dq_sum + jax.ops.segment_sum(
            (scaled_score[:, :, None] * key_att).reshape(edge_slots, D),
            target,
            num_segments=node_total,
        )
        dkey_edge = jnp.einsum(
            "ehj,hij->ehi",
            dkey_att,
            rel_blocks[:, :, relation, 0, :],
            preferred_element_type=jnp.float32,
        )
        dval_edge = jnp.einsum(
            "ehj,hij->ehi",
            dmessage,
            rel_blocks[:, :, relation, 1, :],
            preferred_element_type=jnp.float32,
        )
        grad_att = jnp.einsum(
            "ehi,ehj->hij", key_edge, dkey_att, preferred_element_type=jnp.float32
        )
        grad_msg = jnp.einsum(
            "ehi,ehj->hij", val_edge, dmessage, preferred_element_type=jnp.float32
        )
        rel_grads.append(jnp.stack([grad_att, grad_msg], axis=2))
        dkv_edge = jnp.concatenate(
            [dkey_edge.reshape(edge_slots, D), dval_edge.reshape(edge_slots, D)], axis=1
        )
        dkv_sum = dkv_sum + jax.ops.segment_sum(dkv_edge, source, num_segments=node_total)
        dtime_sum = dtime_sum + jax.ops.segment_sum(dkv_edge, bucket, num_segments=TYPES * TB)
    dqkv_low = jnp.concatenate([dq_sum, dkv_sum], axis=1).astype(jnp.bfloat16)
    grad_qkv = contract_rows(typed_feat, dqkv_low)
    dtime_low = dtime_sum.astype(jnp.bfloat16).reshape(TYPES, TB, 2 * D)
    grad_time_kv = jnp.einsum(
        "td,ste->sde", rte_low, dtime_low, preferred_element_type=jnp.float32
    ).reshape(TYPES * D, 2 * D)
    grad_qkv = jnp.concatenate([grad_qkv[:, :D], grad_qkv[:, D:] + grad_time_kv], axis=1)
    drte_low = jnp.einsum(
        "ste,sde->td", dtime_low, kv_types, preferred_element_type=jnp.float32
    ).astype(jnp.bfloat16)
    grad_time_w = contract_rows(emb_low, drte_low)
    proj_part = pick_types(onehot, against_cols(dqkv_low, typed_w[:, : 3 * D]))
    input_grad = (proj_part + skip_part).astype(jnp.bfloat16)
    grad_type = jnp.concatenate([grad_qkv, grad_outproj], axis=1)
    grad_edge = jnp.concatenate(
        [jnp.stack(rel_grads, axis=2).reshape(D, REL * 2 * DK), grad_time_w], axis=1
    )
    grad_norm = jnp.concatenate([grad_gain, grad_bias], axis=0)
    grad_mix = jnp.concatenate([jnp.stack(prior_grads, axis=0).reshape(REL * H), grad_skip], axis=0)
    total_type, total_edge, total_norm, total_mix = lax.psum(
        (grad_type, grad_edge, grad_norm, grad_mix), ("dp", "fsdp")
    )
    fsdp_rank = lax.axis_index("fsdp")
    part_type = lax.dynamic_slice_in_dim(
        total_type, fsdp_rank * type_weight.shape[0], type_weight.shape[0], 0
    )
    part_edge = lax.dynamic_slice_in_dim(
        total_edge, fsdp_rank * edge_weight.shape[0], edge_weight.shape[0], 0
    )
    part_norm = lax.dynamic_slice_in_dim(
        total_norm, fsdp_rank * norm_params.shape[1], norm_params.shape[1], 1
    )
    type_new = adam_step(type_weight, type_first, type_second, type_avg, part_type, rate_type)
    edge_new = adam_step(edge_weight, edge_first, edge_second, edge_avg, part_edge, rate_edge)
    norm_new = adam_step(norm_params, norm_first, norm_second, norm_avg, part_norm, rate_norm)
    mix_new = adam_step(mix_params, mix_first, mix_second, mix_avg, total_mix, rate_mix)
    return (
        layer_out,
        input_grad,
        type_new[0],
        type_new[1],
        type_new[2],
        type_new[3],
        edge_new[0],
        edge_new[1],
        edge_new[2],
        edge_new[3],
        norm_new[0],
        norm_new[1],
        norm_new[2],
        norm_new[3],
        mix_new[0],
        mix_new[1],
        mix_new[2],
        mix_new[3],
    )


def solution(mesh):
    placed = (
        P(("dp", "fsdp"), None),
        P(("dp", "fsdp"), None),
        P(("dp", "fsdp")),
        P(("dp", "fsdp")),
        P(("dp", "fsdp"), None),
        P(("dp", "fsdp"), None),
        P(("dp", "fsdp"), None),
        P(("dp", "fsdp")),
        P("fsdp", None),
        P("fsdp", None),
        P("fsdp", None),
        P("fsdp", None),
        P("fsdp", None),
        P("fsdp", None),
        P("fsdp", None),
        P("fsdp", None),
        P(None, "fsdp"),
        P(None, "fsdp"),
        P(None, "fsdp"),
        P(None, "fsdp"),
        P(),
        P(),
        P(),
        P(),
    )
    return jax.shard_map(
        shards,
        mesh=mesh,
        in_specs=placed,
        out_specs=(
            P(("dp", "fsdp"), None),
            P(("dp", "fsdp"), None),
            P("fsdp", None),
            P("fsdp", None),
            P("fsdp", None),
            P("fsdp", None),
            P("fsdp", None),
            P("fsdp", None),
            P("fsdp", None),
            P("fsdp", None),
            P(None, "fsdp"),
            P(None, "fsdp"),
            P(None, "fsdp"),
            P(None, "fsdp"),
            P(),
            P(),
            P(),
            P(),
        ),
        check_vma=False,
    )
```

profile of v0, /device:TPU:0, one launch (start us, length us, event | category | flops | bytes accessed | tf_op | source)
XLA Modules:
  0.0 1221.8 jit_solution(4087820819571141902)
XLA Ops:
  53.9 11.0 all_gather.10
  112.9 8.0 all-gather
  172.7 4.9 gather_fusion.24
  185.3 4.9 gather_fusion.6
  242.4 5.1 gather_fusion.10
  366.9 5.1 gather_fusion.27
  386.6 7.5 scatter_custom_fusion.1
  394.1 7.2 scatter_custom_fusion.9
  401.3 7.5 scatter_custom_fusion
  408.8 7.2 scatter_custom_fusion.8
  416.0 7.7 scatter_custom_fusion.3
  423.7 7.2 scatter_custom_fusion.11
  430.9 7.5 scatter_custom_fusion.5
  438.5 7.2 scatter_custom_fusion.13
  462.1 6.5 scatter_fusion.3
  468.7 6.2 scatter_fusion.4
  475.1 6.5 scatter_custom_fusion.15
  481.6 6.2 scatter_fusion.5
  492.6 7.6 scatter_custom_fusion.7
  501.9 6.9 scatter_fusion
  510.2 6.9 scatter_fusion.1
  518.5 7.0 scatter_fusion.2
  736.0 8.8 scatter_custom_fusion.33
  744.8 8.7 scatter_custom_fusion.32
  757.4 8.8 scatter_custom_fusion.35
  766.2 10.2 scatter_custom_fusion.34
  780.3 8.9 scatter_custom_fusion.37
  789.2 10.2 scatter_custom_fusion.36
  803.3 8.6 scatter_custom_fusion.39
  811.9 10.5 scatter_custom_fusion.38
  856.0 7.7 scatter_custom_fusion.23
  873.5 7.6 scatter_custom_fusion.17
  885.9 7.5 scatter_custom_fusion.16
  903.3 7.7 scatter_custom_fusion.19
  920.8 7.5 scatter_custom_fusion.21
  928.3 8.6 scatter_custom_fusion.31
  936.9 9.3 scatter_custom_fusion.29
  946.2 8.6 scatter_custom_fusion.27
  954.8 8.9 scatter_custom_fusion.25
  963.7 8.2 scatter_custom_fusion.24
  976.3 7.1 scatter_fusion.6
  984.8 6.9 scatter_fusion.7
  993.1 7.0 scatter_fusion.8
  1005.5 9.9 scatter_custom_fusion.26
  1019.6 9.7 scatter_custom_fusion.28
  1033.5 9.9 scatter_custom_fusion.30
  1066.1 40.2 %all-reduce = (f32[8,256]{1,0:T(8,128)S(1)}, f32[68]{0:T(128)S(1)}) all-reduce(f32[8,256]{1,0:T(8,128)S(1)} %pad_maximum_fusion.29, f32[68]{0:T(128)S(1)} %pad_maximum_fusion.30), channel_id=1, replica_groups=mesh['dp'=8,'fsdp'=4] {'dp','fsdp'}, use_global_device_ids=true, to_apply=%region_66.67 | all-reduce | flops 2116 | bytes 16928 | tf_op jit(solution)/shard_map/psum | solution.py:294
  1107.6 94.1 %all-reduce.4.cloned.1.call-done = (f32[1024,1024]{0,1:T(8,128)}, f32[256,768]{1,0:T(8,128)}) async-done(((f32[1024,1024]{0,1:T(8,128)}, f32[256,768]{1,0:T(8,128)}), (f32[1024,1024]{0,1:T(8,128)}, f32[256,768]{1,0:T(8,128)})) %all-reduce.4.cloned.1.call-update) | async-done | bytes 4980752 | tf_op jit(solution)/shard_map/psum | solution.py:294
  (971 shorter events, 710.4 us)
Async XLA Ops:
  7.2 131.9 %all-gather.3.cloned.1.call-start = ((), (), s32[]{:S(2)}) async-start(), calls=%async_computation | async-start | bytes 2621440 | tf_op jit(solution)/shard_map/all_gather | solution.py:111
  9.5 1192.2 %all-reduce.4.cloned.1.call-start = ((), (), s32[]{:S(2)}) async-start(), calls=%async_computation.1 | async-start | bytes 9961472 | tf_op jit(solution)/shard_map/psum | solution.py:294
  48.8 16.4 %copy-start.84 = (bf16[1024,256]{1,0:T(8,128)(2,1)S(1)}, bf16[1024,256]{1,0:T(8,128)(2,1)}, u32[]{:S(2)}) copy-start(bf16[1024,256]{1,0:T(8,128)(2,1)} %param.24) | copy-start | bytes 1572868
  71.2 67.9 %copy-start.82 = (bf16[128,8,4,256]{3,1,2,0:T(8,128)(2,1)}, bf16[128,8,4,256]{3,1,2,0:T(8,128)(2,1)S(1)}, u32[]{:S(2)}) copy-start(bf16[128,8,4,256]{3,1,2,0:T(8,128)(2,1)S(1)} %copy.781) | copy-start | bytes 6291460
  78.1 23.9 %copy-start.127 = (bf16[8,32,1,1,32]{4,3,2,1,0:T(2,128)(2,1)S(1)}, bf16[8,32,1,1,32]{4,3,2,1,0:T(2,128)(2,1)}, u32[]{:S(2)}) copy-start(bf16[8,32,1,1,32]{4,3,2,1,0:T(2,128)(2,1)} %get-tuple-element.160) | copy-start | bytes 49156
  78.1 25.8 %copy-start.126 = (bf16[8,32,1,1,32]{4,3,2,1,0:T(2,128)(2,1)S(1)}, bf16[8,32,1,1,32]{4,3,2,1,0:T(2,128)(2,1)}, u32[]{:S(2)}) copy-start(bf16[8,32,1,1,32]{4,3,2,1,0:T(2,128)(2,1)} %get-tuple-element.159) | copy-start | bytes 49156
  78.1 26.6 %copy-start.125 = (bf16[8,32,1,1,32]{4,3,2,1,0:T(2,128)(2,1)S(1)}, bf16[8,32,1,1,32]{4,3,2,1,0:T(2,128)(2,1)}, u32[]{:S(2)}) copy-start(bf16[8,32,1,1,32]{4,3,2,1,0:T(2,128)(2,1)} %get-tuple-element.158) | copy-start | bytes 49156
  78.1 28.6 %copy-start.124 = (bf16[8,32,1,1,32]{4,3,2,1,0:T(2,128)(2,1)S(1)}, bf16[8,32,1,1,32]{4,3,2,1,0:T(2,128)(2,1)}, u32[]{:S(2)}) copy-start(bf16[8,32,1,1,32]{4,3,2,1,0:T(2,128)(2,1)} %get-tuple-element.157) | copy-start | bytes 49156
  78.1 29.3 %copy-start.123 = (bf16[8,32,1,1,32]{4,3,2,1,0:T(2,128)(2,1)S(1)}, bf16[8,32,1,1,32]{4,3,2,1,0:T(2,128)(2,1)}, u32[]{:S(2)}) copy-start(bf16[8,32,1,1,32]{4,3,2,1,0:T(2,128)(2,1)} %get-tuple-element.156) | copy-start | bytes 49156
  78.1 31.9 %copy-start.122 = (bf16[8,32,1,1,32]{4,3,2,1,0:T(2,128)(2,1)S(1)}, bf16[8,32,1,1,32]{4,3,2,1,0:T(2,128)(2,1)}, u32[]{:S(2)}) copy-start(bf16[8,32,1,1,32]{4,3,2,1,0:T(2,128)(2,1)} %get-tuple-element.155) | copy-start | bytes 49156
  79.9 33.0 %copy-start.240 = (f32[8,64]{1,0:T(8,128)S(1)}, f32[8,64]{1,0:T(8,128)}, u32[]{:S(2)}) copy-start(f32[8,64]{1,0:T(8,128)} %param.40) | copy-start | bytes 6148
  110.0 27.8 %copy-start.152 = (f32[1024]{0:T(1024)}, f32[1024]{0:T(1024)S(1)}, u32[]{:S(2)}) copy-start(f32[1024]{0:T(1024)S(1)} %fusion.156) | copy-start | bytes 12292
  111.0 13.2 %copy-start.191 = (f32[1024]{0:T(1024)}, f32[1024]{0:T(1024)S(1)}, u32[]{:S(2)}) copy-start(f32[1024]{0:T(1024)S(1)} %select_reduce_fusion) | copy-start | bytes 12292
  112.8 25.0 %copy-start.16 = (bf16[1024,256]{0,1:T(8,128)(2,1)}, bf16[1024,256]{0,1:T(8,128)(2,1)S(1)}, u32[]{:S(2)}) copy-start(bf16[1024,256]{0,1:T(8,128)(2,1)S(1)} %copy.665) | copy-start | bytes 1572868
  124.2 8.0 copy-start.230
  124.2 8.0 copy-start.242
  124.2 8.0 copy-start.243
  124.2 8.0 copy-start.244
  124.2 8.0 copy-start.245
  124.2 8.0 copy-start.246
  124.3 8.0 copy-start.247
  126.8 10.4 copy-start.164
  133.6 61.5 %copy-start.177 = (s32[1024]{0:T(1024)}, s32[1024]{0:T(1024)S(1)}, u32[]{:S(2)}) copy-start(s32[1024]{0:T(1024)S(1)} %get-tuple-element.317) | copy-start | bytes 12292
  133.6 90.0 %copy-start.175 = (s32[1024]{0:T(1024)}, s32[1024]{0:T(1024)S(1)}, u32[]{:S(2)}) copy-start(s32[1024]{0:T(1024)S(1)} %get-tuple-element.318) | copy-start | bytes 12292
  134.2 118.2 %copy-start.179 = (s32[1024]{0:T(1024)}, s32[1024]{0:T(1024)S(1)}, u32[]{:S(2)}) copy-start(s32[1024]{0:T(1024)S(1)} %get-tuple-element.316) | copy-start | bytes 12292
  134.2 146.8 %copy-start.181 = (s32[1024]{0:T(1024)}, s32[1024]{0:T(1024)S(1)}, u32[]{:S(2)}) copy-start(s32[1024]{0:T(1024)S(1)} %get-tuple-element.315) | copy-start | bytes 12292
  195.1 9.3 copy-start.34
  223.6 9.3 copy-start.37
  252.4 9.4 copy-start.40
  281.0 9.3 copy-start.49
  309.6 9.3 copy-start.43
  338.2 9.4 copy-start.52
  366.9 9.7 copy-start.46
  408.8 36.8 %copy-start.233 = (s32[1024]{0:T(1024)S(1)}, s32[1024]{0:T(1024)}, u32[]{:S(2)}) copy-start(s32[1024]{0:T(1024)} %get-tuple-element.303) | copy-start | bytes 12292
  459.9 8.7 copy-start.149
  460.0 8.6 copy-start.100
  492.6 9.3 copy-start.61
  936.9 9.3 copy-start.21
  954.8 8.9 copy-start.22
  1063.6 42.8 %copy-start.277 = (f32[68]{0:T(128)S(1)}, f32[68]{0:T(128)}, u32[]{:S(2)}) copy-start(f32[68]{0:T(128)} %param.44) | copy-start | bytes 820
  1063.6 42.8 %copy-start.278 = (f32[68]{0:T(128)S(1)}, f32[68]{0:T(128)}, u32[]{:S(2)}) copy-start(f32[68]{0:T(128)} %param.47) | copy-start | bytes 820
  1063.6 42.7 %copy-start.279 = (f32[68]{0:T(128)S(1)}, f32[68]{0:T(128)}, u32[]{:S(2)}) copy-start(f32[68]{0:T(128)} %param.45) | copy-start | bytes 820
  1063.6 42.7 %copy-start.280 = (f32[68]{0:T(128)S(1)}, f32[68]{0:T(128)}, u32[]{:S(2)}) copy-start(f32[68]{0:T(128)} %param.46) | copy-start | bytes 820
  1063.6 43.3 %copy-start.241 = (f32[8,64]{1,0:T(8,128)S(1)}, f32[8,64]{1,0:T(8,128)}, u32[]{:S(2)}) copy-start(f32[8,64]{1,0:T(8,128)} %param.40) | copy-start | bytes 6148
  1063.6 43.3 %copy-start.261 = (f32[8,64]{1,0:T(8,128)S(1)}, f32[8,64]{1,0:T(8,128)}, u32[]{:S(2)}) copy-start(f32[8,64]{1,0:T(8,128)} %param.43) | copy-start | bytes 6148
  1063.6 43.3 %copy-start.262 = (f32[8,64]{1,0:T(8,128)S(1)}, f32[8,64]{1,0:T(8,128)}, u32[]{:S(2)}) copy-start(f32[8,64]{1,0:T(8,128)} %param.41) | copy-start | bytes 6148
  1063.6 43.3 %copy-start.263 = (f32[8,64]{1,0:T(8,128)S(1)}, f32[8,64]{1,0:T(8,128)}, u32[]{:S(2)}) copy-start(f32[8,64]{1,0:T(8,128)} %param.42) | copy-start | bytes 6148
  1064.1 137.6 %copy-start.59 = (f32[256,1024]{0,1:T(8,128)S(1)}, f32[256,1024]{0,1:T(8,128)}, u32[]{:S(2)}) copy-start(f32[256,1024]{0,1:T(8,128)} %copy.731) | copy-start | bytes 3145732
  (238 other events, 864.7 us)
Sparse Core Ops, SparseCore 0:
  10.5 38.0 all-gather.2
  1055.0 146.6 all-reduce.3
where the time goes:
time: 1240 us; the launch traced here: 1220 us
  other arithmetic  488 us (39%)
  local copies, waits for them, and re-layouts  464 us (37%)
  matrix products  98.9 us (8%)
  waiting for transfers between devices  94.1 us (8%)
  blocking collectives  59.2 us (5%)
  between operations  18.2 us (1%)
    psum x1, waiting for transfers between devices, shards(): lax.psum((grad_type, grad_edge, grad_norm, grad_mix), ('dp', 'fsdp'))  94.1 us
    gather x16, local copies, waits for them, and re-layouts, shards(): kv_edge = (keyval[source] + time_kv[bucket]).astype(jnp.bfloat16)  78.6 us
    scatter-add x8, other arithmetic, shards(): jax.ops.segment_sum(dkv_edge, bucket, num_segments=TYPES * TB)  74.8 us
    scatter-add x8, other arithmetic, shards(): jax.ops.segment_sum(dkv_edge, source, num_segments=node_total)  73.2 us
    scatter-add x8, other arithmetic, shards(): jax.ops.segment_sum((scaled_score[:, :, None] * key_att).reshape(edge_slo...  59 us
    scatter-add x8, other arithmetic, shards(): jax.ops.segment_sum((weight[:, :, None] * message).reshape(edge_slots, D)...  58.7 us
    unnamed x599, local copies, waits for them, and re-layouts  58.1 us
    gather x16, local copies, waits for them, and re-layouts, shards(): q_target = query_node[target].reshape(edge_slots, H, DK)  54.9 us
  transfers between devices with their start and end apart: 2, of which 1 were waited for; matrix products, arithmetic and copies ran while one was open for 10% of the time, Pallas kernels for 0%

commit v1 on v0

v1 whole, which is shorter than its diff:
```python
import functools

import jax
import jax.numpy as jnp
import numpy as np
from jax import lax
from jax.experimental import pallas as pl
from jax.experimental.pallas import tpu as pltpu
from jax.sharding import PartitionSpec as P

D, H, DK, TYPES, REL, TB = 256, 8, 32, 4, 8, 240
N = 1024
EC = 512
SUB = 256
NSUB = EC // SUB
NC = 256
bf16 = jnp.bfloat16
f32 = jnp.float32
norm_eps = 1e-5
STEP = 10
beta_one = 0.9
beta_two = 0.999
adam_eps = 1e-08
decay_rate = 0.01
ema_keep = 0.7
rates = (0.2, 0.2, 0.6, 0.6)


def nn(a, b):
    return jnp.dot(a, b, preferred_element_type=f32)


def nt(a, b):
    return lax.dot_general(a, b, (((1,), (1,)), ((), ())), preferred_element_type=f32)


def one_hot_rows(row, count):
    wide = row.shape[1]
    base = lax.broadcasted_iota(jnp.int32, (256, wide), 0).astype(bf16)
    one, zero = jnp.ones((), bf16), jnp.zeros((), bf16)
    return jnp.concatenate(
        [jnp.where(base == (row - 256 * g).astype(bf16), one, zero) for g in range(count // 256)], axis=0
    )


def head_sum(x):
    return jnp.sum(x.reshape(H, DK, x.shape[1]), axis=1)


def head_wide(x):
    return jnp.broadcast_to(x[:, None, :], (H, DK, x.shape[1])).reshape(D, x.shape[1])


def hi_lo(x):
    high = x.astype(bf16).astype(f32)
    return jnp.concatenate([high, x - high], axis=0).astype(bf16)


def eye():
    return (
        lax.broadcasted_iota(jnp.int32, (256, 256), 0) == lax.broadcasted_iota(jnp.int32, (256, 256), 1)
    ).astype(f32).astype(bf16)


def pick(masks, wide):
    out = wide[0] * masks[0:1]
    for s in range(1, TYPES):
        out = jnp.where(masks[s:s + 1] > 0, wide[s], out)
    return out


def kernel(
    blocks,
    place_ref, live_ref, cnt_ref, skip_ref,
    kinds_ref, kinds8_ref, src_ref, dst_ref, tim_ref,
    feat_ref, cot_ref, mu_ref, emb_ref, own_ref, *rest,
):
    near_refs, far_refs, rest = rest[:blocks - 1], rest[blocks - 1:2 * blocks - 2], rest[2 * blocks - 2:]
    (
        out_ref, ig_ref, keep_ref, send_ref,
        lst_r, lst_o, lst_c,
        wpk, gpack, gout, gnorm_acc, gskip_acc,
        bkt, wt, xcat, kvt, tkvt, qt, rte,
        bda, bdat, bdm, bdmt, ga, gm, dmu,
        kve, qe, katt, msg, wexp, raws,
        num, dnum, dq, dkv, dtkv, skp,
    ) = rest
    trows, erows = TYPES * D // blocks, D // blocks
    part = trows + erows
    half = part // 2
    me, core = place_ref[0], place_ref[1]

    wpk[pl.ds(pl.multiple_of(me * part, 16), part), :] = own_ref[...]
    for m in range(1, blocks):
        base = jnp.bitwise_xor(me, m) * part
        wpk[pl.ds(pl.multiple_of(base + core * half, 16), half), :] = near_refs[m - 1][...]
        wpk[pl.ds(pl.multiple_of(base + (1 - core) * half, 16), half), :] = far_refs[m - 1][...]

    def rows_at(pieces):
        return pieces[0] if len(pieces) == 1 else jnp.concatenate(pieces, axis=0)

    def type_part(s, c0, c1):
        lo, hi = s * D // trows, max((s + 1) * D // trows, s * D // trows + 1)
        return rows_at([
            wpk[f * part + max(s * D - f * trows, 0):f * part + min((s + 1) * D - f * trows, trows), c0:c1]
            for f in range(lo, hi)
        ])

    def edge_part(c0, c1):
        return rows_at([wpk[f * part + trows:(f + 1) * part, c0:c1] for f in range(blocks)])

    def norm_part():
        wide = D // blocks
        full = jnp.concatenate(
            [wpk[f * part + trows:f * part + trows + 16, 768:768 + wide].astype(f32) for f in range(blocks)], axis=1
        )
        return full.astype(bf16)

    def put_type(s, value):
        lo, hi = s * D // trows, max((s + 1) * D // trows, s * D // trows + 1)
        for f in range(lo, hi):
            a, b = max(s * D, f * trows), min((s + 1) * D, (f + 1) * trows)
            gpack[f * part + a - f * trows:f * part + b - f * trows, :] = value[a - s * D:b - s * D].astype(bf16)

    def put_edge(c0, value):
        for f in range(blocks):
            gpack[f * part + trows:(f + 1) * part, c0:c0 + value.shape[1]] = value[f * erows:(f + 1) * erows].astype(bf16)

    ident = eye()
    def per_rel(r, k):
        c = cnt_ref[r]
        def one(j, k):
            lst_r[k] = r
            lst_o[k] = j
            lst_c[k] = c - j * SUB
            return k + 1
        return lax.fori_loop(0, (c + SUB - 1) // SUB, one, k)
    total = lax.fori_loop(0, REL, per_rel, 0)
    for extra in range(NSUB - 1):
        lst_r[total + extra] = 0
        lst_o[total + extra] = 0
        lst_c[total + extra] = 0
    chunks = (total + NSUB - 1) // NSUB

    src = src_ref[...]
    for j in range(N // 128):
        idx = src[:, j * 128:(j + 1) * 128]
        low = jnp.bitwise_and(idx, 127)
        high = jnp.right_shift(idx, 7)
        acc = jnp.zeros((8, 128), jnp.int32)
        for k in range(N // 128):
            row = jnp.broadcast_to(kinds8_ref[k:k + 1, :], (8, 128))
            acc = jnp.where(high == k, jnp.take_along_axis(row, low, axis=1), acc)
        bkt[:, j * 128:(j + 1) * 128] = acc * 256 + tim_ref[:, j * 128:(j + 1) * 128]

    lane = lax.broadcasted_iota(jnp.int32, (D, 128), 1)
    rowi = lax.broadcasted_iota(jnp.int32, (D, 128), 0)
    on_diag = (lane // DK) == (rowi // DK) % 4
    for p in range(4):
        x = edge_part(p * 128, (p + 1) * 128).astype(f32)
        rolled = [x if k == 0 else pltpu.roll(x, 32 * k, 1) for k in range(4)]
        for g in range(4):
            r, m = 2 * p + g // 2, g % 2
            t = jnp.concatenate([rolled[(h % 4 - g) % 4][h * 32:(h + 1) * 32] for h in range(H)], axis=0)
            t = jnp.where(on_diag, t, 0.0)
            z = jnp.zeros((128, 128), f32)
            full = jnp.concatenate(
                [jnp.concatenate([t[:128], z], axis=1), jnp.concatenate([z, t[128:]], axis=1)], axis=0
            ).astype(bf16)
            (bdm if m else bda)[r] = full
            (bdmt if m else bdat)[r] = nt(ident, full).astype(bf16)

    for cb in range(4):
        for s in range(4):
            wt[cb * 256:(cb + 1) * 256, s * 256:(s + 1) * 256] = nt(
                ident, type_part(s, cb * 256, (cb + 1) * 256)
            ).astype(bf16)
    kinds = kinds_ref[...]
    masks = (lax.broadcasted_iota(jnp.int32, (8, N), 0) == kinds).astype(f32)
    featt = nt(ident, feat_ref[...])
    for s in range(TYPES):
        xcat[s * D:(s + 1) * D, :] = (featt * masks[s:s + 1]).astype(bf16)
    qt[...] = nn(wt[:D, :], xcat[...]).astype(bf16)
    kvt[...] = nn(wt[D:3 * D, :], xcat[...]).astype(bf16)
    wet = nt(ident, edge_part(512, 768)).astype(bf16)
    rte[...] = nt(wet, emb_ref[...]).astype(bf16)
    for s in range(TYPES):
        tkvt[:, s * 256:(s + 1) * 256] = nn(wt[D:3 * D, s * 256:(s + 1) * 256], rte[...]).astype(bf16)

    num[...] = jnp.zeros_like(num)
    dq[...] = jnp.zeros_like(dq)
    dkv[...] = jnp.zeros_like(dkv)
    dtkv[...] = jnp.zeros_like(dtkv)
    ga[...] = jnp.zeros_like(ga)
    gm[...] = jnp.zeros_like(gm)
    dmu[...] = jnp.zeros_like(dmu)

    def rows_of(ref, c):
        return jnp.concatenate(
            [ref[pl.ds(lst_r[c * NSUB + k], 1), pl.ds(pl.multiple_of(lst_o[c * NSUB + k] * SUB, SUB), SUB)] for k in range(NSUB)],
            axis=1,
        )

    def mu_of(c):
        return jnp.concatenate([mu_ref[lst_r[c * NSUB + k // 2]] for k in range(2 * NSUB)], axis=1)

    def forward(c, _):
        at = pl.ds(pl.multiple_of(c * EC, EC), EC)
        ohs = one_hot_rows(rows_of(src_ref, c), N)
        ohb = one_hot_rows(rows_of(bkt, c), N)
        ohd = one_hot_rows(rows_of(dst_ref, c), N)
        kv_e = (nn(kvt[...], ohs) + nn(tkvt[...], ohb)).astype(bf16)
        kve[:, at] = kv_e
        q_e = nn(qt[...], ohd)
        qe[:, at] = q_e.astype(bf16)
        ks, ms = [], []
        for k in range(NSUB):
            r = lst_r[c * NSUB + k]
            ks.append(nn(bdat[r], kv_e[:D, k * SUB:(k + 1) * SUB]))
            ms.append(nn(bdmt[r], kv_e[D:, k * SUB:(k + 1) * SUB]))
        ka = jnp.concatenate(ks, axis=1)
        me = jnp.concatenate(ms, axis=1)
        katt[:, at] = ka.astype(bf16)
        msg[:, at] = me.astype(bf16)
        raw = head_sum(ka * q_e)
        raws[:, at] = raw
        lanes = lax.broadcasted_iota(jnp.int32, (H, SUB), 1)
        valid = jnp.concatenate([lanes < lst_c[c * NSUB + k] for k in range(NSUB)], axis=1)
        w = jnp.where(valid, jnp.exp(raw * mu_of(c)), 0.0)
        wexp[:, at] = w
        wm = (head_wide(w) * me).astype(bf16)
        num[...] += nt(jnp.concatenate([wm, hi_lo(w)], axis=0), ohd)
        return 0

    lax.fori_loop(0, chunks, forward, 0)

    nwt = nt(ident, norm_part())
    gnorm_acc[...] = jnp.zeros_like(gnorm_acc)
    gskip_acc[...] = jnp.zeros_like(gskip_acc)
    gout[...] = jnp.zeros((TYPES * D, D), f32)

    def nodes(c, _):
        at = pl.ds(pl.multiple_of(c * NC, NC), NC)
        mk = (lax.broadcasted_iota(jnp.int32, (8, NC), 0) == kinds_ref[:, at]).astype(f32)
        live = (lax.broadcasted_iota(jnp.int32, (1, NC), 1) + c * NC < live_ref[0]).astype(f32)
        den = num[D:D + H, at] + num[D + H:, at] + (1.0 - live)
        denw = head_wide(den)
        agg = num[:D, at] / denw
        phi = 0.5 * (1.0 + lax.erf(agg * (0.5 ** 0.5)))
        act = (agg * phi).astype(bf16).astype(f32)
        acat = jnp.concatenate([(act * mk[s:s + 1]).astype(bf16) for s in range(TYPES)], axis=0)
        trans = nn(wt[3 * D:, :], acat)
        skip = jnp.zeros((1, NC), f32)
        for s in range(TYPES):
            skip = skip + mk[s:s + 1] * skip_ref[s]
        alpha = 1.0 / (1.0 + jnp.exp(-skip))
        ft = nt(ident, feat_ref[at, :])
        res = alpha * trans + (1.0 - alpha) * ft
        mean = jnp.mean(res, axis=0, keepdims=True)
        cen = res - mean
        inv = lax.rsqrt(jnp.mean(cen * cen, axis=0, keepdims=True) + norm_eps)
        nrm = cen * inv
        gain = nwt[:, 0:1] * mk[0:1]
        bias = nwt[:, 4:5] * mk[0:1]
        for s in range(1, TYPES):
            gain = gain + nwt[:, s:s + 1] * mk[s:s + 1]
            bias = bias + nwt[:, 4 + s:5 + s] * mk[s:s + 1]
        out_ref[at, :] = (live * (nrm * gain + bias)).T.astype(bf16)
        dy = live * nt(ident, cot_ref[at, :])
        oh16 = jnp.concatenate([mk, jnp.zeros((8, NC), f32)], axis=0).astype(bf16)
        dyn = dy * nrm
        dyn_hi = dyn.astype(bf16)
        dyn_lo = (dyn - dyn_hi.astype(f32)).astype(bf16)
        gnorm_acc[0:4, :] += (nt(oh16, dyn_hi) + nt(oh16, dyn_lo))[0:4]
        gnorm_acc[4:8, :] += nt(oh16, dy.astype(bf16))[0:4]
        dn = dy * gain
        dres = inv * (dn - jnp.mean(dn, axis=0, keepdims=True) - nrm * jnp.mean(dn * nrm, axis=0, keepdims=True))
        dtr = (alpha * dres).astype(bf16)
        skp[:, at] = (1.0 - alpha) * dres
        dal = jnp.sum(dres * (trans - ft), axis=0, keepdims=True) * alpha * (1.0 - alpha)
        gskip_acc[...] += jnp.broadcast_to(jnp.sum(mk * dal, axis=1, keepdims=True), (8, 128))
        gout[...] += nt(acat, dtr)
        dact = pick(mk, [nn(type_part(s, 3 * D, 4 * D), dtr) for s in range(TYPES)])
        dagg = dact * (phi + agg * (jnp.exp(-0.5 * agg * agg) * (0.5 / np.pi) ** 0.5))
        dnum[0:D, at] = (dagg / denw).astype(bf16)
        dnum[D:, at] = hi_lo(-head_sum(dagg * agg) / den)
        return 0

    lax.fori_loop(0, N // NC, nodes, 0)

    def backward(c, _):
        at = pl.ds(pl.multiple_of(c * EC, EC), EC)
        ohs = one_hot_rows(rows_of(src_ref, c), N)
        ohb = one_hot_rows(rows_of(bkt, c), N)
        ohd = one_hot_rows(rows_of(dst_ref, c), N)
        dn_all = nn(dnum[...], ohd)
        dn_e = dn_all[:D]
        w = wexp[:, at]
        dw = head_sum(dn_e * msg[:, at].astype(f32)) + dn_all[D:D + H] + dn_all[D + H:]
        ds = dw * w
        dsr = ds * raws[:, at]
        ss = head_wide(ds * mu_of(c))
        dka = (ss * qe[:, at].astype(f32)).astype(bf16)
        dms = (head_wide(w) * dn_e).astype(bf16)
        dq[...] += nt((ss * katt[:, at].astype(f32)).astype(bf16), ohd)
        ds_, = ([],)
        for k in range(NSUB):
            r = lst_r[c * NSUB + k]
            sl = slice(k * SUB, (k + 1) * SUB)
            ds_.append(jnp.concatenate([nn(bda[r], dka[:, sl]), nn(bdm[r], dms[:, sl])], axis=0).astype(bf16))
            at_k = pl.ds(pl.multiple_of(c * EC + k * SUB, SUB), SUB)
            gak = nt(kve[0:D, at_k], dka[:, sl])
            gmk = nt(kve[D:, at_k], dms[:, sl])
            ga[r, 0:128] += gak[0:128, 0:128]
            ga[r, 128:] += gak[128:, 128:]
            gm[r, 0:128] += gmk[0:128, 0:128]
            gm[r, 128:] += gmk[128:, 128:]
            dmu[r] += dsr[:, k * SUB:k * SUB + 128] + dsr[:, k * SUB + 128:(k + 1) * SUB]
        dkve = jnp.concatenate(ds_, axis=1)
        dkv[...] += nt(dkve, ohs)
        dtkv[...] += nt(dkve, ohb)
        return 0

    lax.fori_loop(0, chunks, backward, 0)

    dqkv = jnp.concatenate([dq[...].astype(bf16), dkv[...].astype(bf16)], axis=0)
    dt = dtkv[...].astype(bf16)
    for s in range(TYPES):
        g = nt(xcat[s * D:(s + 1) * D, :], dqkv)
        g_kv = g[:, D:] + nt(rte[...], dt[:, s * 256:(s + 1) * 256])
        put_type(s, jnp.concatenate([g[:, :D], g_kv, gout[s * D:(s + 1) * D, :]], axis=1))
    drte = nn(type_part(0, D, 3 * D), dt[:, 0:256])
    for s in range(1, TYPES):
        drte = drte + nn(type_part(s, D, 3 * D), dt[:, s * 256:(s + 1) * 256])
    embt = nt(ident, emb_ref[...]).astype(bf16)
    put_edge(512, nt(embt, drte.astype(bf16)))
    for c in range(N // NC):
        at = slice(c * NC, (c + 1) * NC)
        proj = pick(masks[:, at], [nn(type_part(s, 0, 3 * D), dqkv[:, at]) for s in range(TYPES)])
        ig_ref[at, :] = (proj + skp[:, at]).T.astype(bf16)
    for p in range(4):
        acc = jnp.zeros((D, 128), f32)
        for g in range(4):
            r, m = 2 * p + g // 2, g % 2
            t = jnp.where(on_diag, (gm if m else ga)[r], 0.0)
            rolled = [t if k == 0 else pltpu.roll(t, 32 * k, 1) for k in range(4)]
            acc = acc + jnp.concatenate([rolled[(g - h % 4) % 4][h * 32:(h + 1) * 32] for h in range(H)], axis=0)
        put_edge(p * 128, acc)
    gmu = jnp.sum(dmu[...], axis=2) * DK ** (-0.5)
    gnorm = gnorm_acc[...]
    wide = D // blocks
    for f in range(blocks):
        small = jnp.concatenate(
            [
                jnp.concatenate([gnorm[:, f * wide:(f + 1) * wide], jnp.zeros((8, 256 - wide), f32)], axis=1),
                jnp.concatenate([gmu, jnp.zeros((8, 248), f32)], axis=1),
                jnp.concatenate([gskip_acc[...], jnp.zeros((8, 128), f32)], axis=1),
                jnp.zeros((erows - 24, 256), f32),
            ],
            axis=0,
        )
        gpack[f * part + trows:(f + 1) * part, 768:] = small.astype(bf16)
    for m in range(blocks):
        base = jnp.bitwise_xor(me, m) * part
        keep_ref[m] = gpack[pl.ds(pl.multiple_of(base + core * half, 16), half), :]
        send_ref[m] = gpack[pl.ds(pl.multiple_of(base + (1 - core) * half, 16), half), :]


def emb_table():
    steps = np.arange(TB, dtype=np.float32)[:, None]
    col = np.arange(D)
    freq = np.exp(-np.log(np.float32(10000.0)) * (2 * (col // 2)).astype(np.float32) / np.float32(D)).astype(np.float32)
    angle = steps * freq[None]
    tab = np.where(col[None] % 2 == 0, np.sin(angle), np.cos(angle)).astype(np.float32)
    return np.concatenate([tab, np.zeros((256 - TB, D), np.float32)], axis=0)


def run_block(blocks, place, live, cnt, skip, kinds, src, dst, tim, feat, cot, mu, own, near, far):
    S = jax.ShapeDtypeStruct
    smem = pl.BlockSpec(memory_space=pltpu.SMEM)
    vmem = pl.BlockSpec(memory_space=pltpu.VMEM)
    V = pltpu.VMEM
    part = (TYPES * D + D) // blocks
    return pl.pallas_call(
        functools.partial(kernel, blocks),
        out_shape=(
            S((N, D), bf16), S((N, D), bf16),
            S((blocks, part // 2, 1024), bf16), S((blocks, part // 2, 1024), bf16),
        ),
        in_specs=[smem] * 4 + [vmem] * (10 + 2 * (blocks - 1)),
        out_specs=[vmem] * 4,
        scratch_shapes=[
            pltpu.SMEM((40,), jnp.int32), pltpu.SMEM((40,), jnp.int32), pltpu.SMEM((40,), jnp.int32),
            V((blocks * part, 1024), bf16), V((blocks * part, 1024), bf16), V((TYPES * D, D), f32),
            V((8, D), f32), V((8, 128), f32),
            V((8, N), jnp.int32), V((1024, 1024), bf16), V((1024, N), bf16), V((512, N), bf16), V((512, 1024), bf16),
            V((D, N), bf16), V((D, 256), bf16),
            V((8, 256, 256), bf16), V((8, 256, 256), bf16), V((8, 256, 256), bf16), V((8, 256, 256), bf16),
            V((8, 256, 128), f32), V((8, 256, 128), f32), V((8, 8, 128), f32),
            V((512, 8192), bf16), V((D, 8192), bf16), V((D, 8192), bf16), V((D, 8192), bf16), V((8, 8192), f32), V((8, 8192), f32),
            V((D + 16, N), f32), V((D + 16, N), bf16), V((D, N), f32), V((512, N), f32), V((512, 1024), f32), V((D, N), f32),
        ],
        compiler_params=pltpu.CompilerParams(vmem_limit_bytes=63 << 20),
        name="layer",
    )(
        place, live, cnt, skip, kinds.reshape(1, N), kinds.reshape(8, 128), src, dst, tim,
        feat, cot, mu, jnp.asarray(emb_table(), bf16), own, *near, *far,
    )


def tree(terms):
    while len(terms) > 1:
        terms = [terms[i] + terms[i + 1] for i in range(0, len(terms), 2)]
    return terms[0]


def add_core_kernel(blocks, keep_ref, got_ref, *outs):
    for m in range(blocks):
        outs[m][...] = (keep_ref[m].astype(f32) + got_ref[m].astype(f32)).astype(bf16)


def add_core(blocks, keep, got):
    rows = keep.shape[1]
    return pl.pallas_call(
        functools.partial(add_core_kernel, blocks),
        out_shape=[jax.ShapeDtypeStruct((rows, 1024), bf16)] * blocks,
        name="add_core",
    )(keep, got)


def add_parts_kernel(lines, zi_ref, *refs):
    ins, outs = refs[:-lines], refs[-lines:]
    total = tree([r[...].astype(f32) for r in ins]).astype(bf16)
    wide = 1024 // lines
    pieces = [total[:, j * wide:(j + 1) * wide] for j in range(lines)]
    for k in range(lines):
        want = jnp.bitwise_xor(zi_ref[0], k)
        for j in range(lines):
            @pl.when(want == j)
            def _():
                outs[k][...] = pieces[j]


def add_parts(lines, zi, terms):
    rows = terms[0].shape[0]
    return pl.pallas_call(
        functools.partial(add_parts_kernel, lines),
        out_shape=[jax.ShapeDtypeStruct((rows, 1024 // lines), bf16)] * lines,
        in_specs=[pl.BlockSpec(memory_space=pltpu.SMEM)] + [pl.BlockSpec(memory_space=pltpu.VMEM)] * len(terms),
        name="add_parts",
    )(zi, *terms)


def add_lines_kernel(*refs):
    refs[-1][...] = tree([r[...].astype(f32) for r in refs[:-1]]).astype(bf16)


def add_lines(terms):
    return pl.pallas_call(
        add_lines_kernel, out_shape=jax.ShapeDtypeStruct(terms[0].shape, bf16), name="add_lines"
    )(*terms)


def adam(param, first, second, avg, grad, rate):
    first_new = beta_one * first + (1.0 - beta_one) * grad
    second_new = beta_two * second + (1.0 - beta_two) * grad * grad
    first_hat = first_new / (1.0 - beta_one**STEP)
    second_hat = second_new / (1.0 - beta_two**STEP)
    param_new = param - rate * (first_hat / (jnp.sqrt(second_hat) + adam_eps) + decay_rate * param)
    avg_new = ema_keep * avg + (1.0 - ema_keep) * param_new
    return (param_new, first_new, second_new, avg_new)


def update_kernel(lines, trows, erows, place_ref, *refs):
    pieces, refs = refs[:2 * lines], refs[2 * lines:]
    states, outs, gsum = refs[:16], refs[16:32], refs[32]
    core, zi = place_ref[1], place_ref[2]
    half = (trows + erows) // 2
    wide = 1024 // lines
    for side in range(2):
        at = pl.ds(pl.multiple_of(jnp.bitwise_xor(core, side) * half, 16), half)
        for k in range(lines):
            want = jnp.bitwise_xor(zi, k)
            for j in range(lines):
                @pl.when(want == j)
                def _():
                    gsum[at, j * wide:(j + 1) * wide] = pieces[side * lines + k][...]
    nwide = states[8].shape[1]
    grads = (
        gsum[0:trows, :].astype(f32),
        gsum[trows:trows + erows, 0:768].astype(f32),
        gsum[trows:trows + 16, 768:768 + nwide].astype(f32)[0:8],
    )
    for i in range(3):
        new = adam(*[states[4 * i + j][...] for j in range(4)], grads[i], rates[i])
        for j in range(4):
            outs[4 * i + j][...] = new[j]
    mix = gsum[trows:trows + 32, 768:896].astype(f32)
    lanes = lax.broadcasted_iota(jnp.int32, (8, 128), 1)
    grad_mu = jnp.where(lanes < 8, mix[8:16], 0.0)
    grad_skip = jnp.where(lanes < 8, mix[16:24], 0.0)
    grad_mix = jnp.concatenate([grad_mu, grad_skip], axis=0)
    new = adam(*[states[12 + j][...] for j in range(4)], grad_mix, rates[3])
    for j in range(4):
        outs[12 + j][...] = new[j]


def update(lines, place, pieces, states):
    trows, erows = states[0].shape[0], states[4].shape[0]
    return pl.pallas_call(
        functools.partial(update_kernel, lines, trows, erows),
        out_shape=[jax.ShapeDtypeStruct(x.shape, f32) for x in states],
        in_specs=[pl.BlockSpec(memory_space=pltpu.SMEM)]
        + [pl.BlockSpec(memory_space=pltpu.VMEM)] * (len(pieces) + 16),
        scratch_shapes=[pltpu.VMEM((trows + erows, 1024), bf16)],
        compiler_params=pltpu.CompilerParams(vmem_limit_bytes=40 << 20),
        name="update",
    )(place, *pieces, *states)


def wide_mix(mix):
    mu = jnp.pad(mix[:64].reshape(8, 8), ((0, 0), (0, 120)))
    skip = jnp.pad(jnp.broadcast_to(mix[64:, None], (4, 128)), ((0, 4), (0, 0)))
    return jnp.concatenate([mu, skip], axis=0)


def narrow_mix(wide):
    return jnp.concatenate([wide[:8, :8].reshape(64), wide[8:12, 0]], axis=0)


def shards(dp, fsdp, *args):
    (
        node_feat, out_cot, node_type, node_count, edge_src, edge_dst, edge_time, edge_count,
        type_weight, type_first, type_second, type_avg,
        edge_weight, edge_first, edge_second, edge_avg,
        norm_params, norm_first, norm_second, norm_avg,
        mix_params, mix_first, mix_second, mix_avg,
    ) = args
    lines = dp // 2
    dp_at, fsdp_at = lax.axis_index("dp"), lax.axis_index("fsdp")
    core, zi = dp_at % 2, dp_at // 2
    place = jnp.stack([fsdp_at, core, zi]).astype(jnp.int32)

    def swap(x, axis, mask):
        size = dp if axis == "dp" else fsdp
        return lax.ppermute(x, axis, [(i, i ^ mask) for i in range(size)])

    trows, erows = type_weight.shape[0], edge_weight.shape[0]
    nwide = norm_params.shape[1]
    half = (trows + erows) // 2
    corner = jnp.pad(norm_params, ((0, erows - 8), (0, 256 - nwide)))
    own = jnp.concatenate([type_weight, jnp.concatenate([edge_weight, corner], axis=1)], axis=0).astype(bf16)
    mine = lax.dynamic_slice_in_dim(own, core * half, half, 0)
    near = [swap(mine, "fsdp", m) for m in range(1, fsdp)]
    far = [swap(x, "dp", 1) for x in near]
    mix = lax.optimization_barrier(mix_params.astype(bf16)).astype(f32)
    mu = jnp.broadcast_to((mix[:64] * DK ** (-0.5)).reshape(REL, H, 1), (REL, H, 128))
    layer_out, input_grad, keep, send = run_block(
        fsdp, place, node_count, edge_count, mix[64:], node_type, edge_src, edge_dst, edge_time,
        node_feat, out_cot, mu, own, near, far,
    )
    sums = add_core(fsdp, keep, swap(send, "dp", 1))
    pieces = add_parts(lines, place[2:], [sums[0]] + [swap(sums[m], "fsdp", m) for m in range(1, fsdp)])
    total = add_lines([pieces[0]] + [swap(pieces[k], "dp", 2 * k) for k in range(1, lines)])
    totals = [total] + [swap(total, "dp", 2 * k) for k in range(1, lines)]
    others = [swap(x, "dp", 1) for x in totals]
    states = [
        type_weight, type_first, type_second, type_avg,
        edge_weight, edge_first, edge_second, edge_avg,
        norm_params, norm_first, norm_second, norm_avg,
    ] + [wide_mix(x) for x in (mix_params, mix_first, mix_second, mix_avg)]
    new = update(lines, place, totals + others, states)
    return (layer_out, input_grad, *new[:12], *[narrow_mix(x) for x in new[12:]])


def solution(mesh):
    whole = P(("dp", "fsdp"), None)
    flat = P(("dp", "fsdp"))
    state = [P("fsdp", None)] * 8 + [P(None, "fsdp")] * 4 + [P()] * 4
    return jax.shard_map(
        functools.partial(shards, mesh.shape["dp"], mesh.shape["fsdp"]),
        mesh=mesh,
        in_specs=tuple([whole, whole, flat, flat, whole, whole, whole, flat] + state),
        out_specs=tuple([whole, whole] + state),
        check_vma=False,
    )
```

time: 1240 us -> 186 us (0.15); the launches traced: 1220 us -> 188 us
  other arithmetic: 488 us -> 10.3 us
  local copies, waits for them, and re-layouts: 464 us -> 20 us
  matrix products: 98.9 us -> 0 us
  Pallas kernels: 0 us -> 66.3 us
  blocking collectives: 59.2 us -> 0 us
  waiting for transfers between devices: 94.1 us -> 36.2 us
  starting transfers between devices: 0.08 us -> 53.6 us
  between operations: 18.2 us -> 1.49 us
    scatter-add x40 -> x0, other arithmetic: 320 us -> none  [the longest x8 74.8 us: shards(): jax.ops.segment_sum(dkv_edge, bucket, num_segments=TYPES * TB)]
    gather x72 -> x0, local copies, waits for them, and re-layouts: 263 us -> none  [the longest x16 78.6 us: shards(): kv_edge = (keyval[source] + time_kv[bucket]).astype(jnp.bfloat16)]
    dot_general x63 -> x0, matrix products: 98.9 us -> none  [the longest x8 20.1 us: shards(): jnp.einsum('ehi,hij->ehj', val_edge, rel_blocks[:, :, relation, 1, :], pr...]
    psum x1 -> x0, waiting for transfers between devices: 94.1 us -> none  [shards(): lax.psum((grad_type, grad_edge, grad_norm, grad_mix), ('dp', 'fsdp'))]
    reshape x38 -> x8, local copies, waits for them, and re-layouts: 87.6 us -> 5.03 us  [the longest x4 4.72 us: wide_mix(): mu = jnp.pad(mix[:64].reshape(8, 8), ((0, 0), (0, 120)))]
    pallas_call x0 -> x5, Pallas kernels: none -> 66.3 us  [the longest x1 55.2 us: run_block(): pl.pallas_call(functools.partial(kernel, blocks), out_shape=(S((N, D), bf...]
    ppermute x0 -> x20, starting transfers between devices: none -> 53.6 us  [swap(): return lax.ppermute(x, axis, [(i, i ^ mask) for i in range(size)])]
    unnamed x599 -> x48, local copies, waits for them, and re-layouts: 58.1 us -> 9.9 us
  transfers between devices with their start and end apart: 2 -> 20, of which waited for: 1 -> 11; matrix products, arithmetic and copies ran while one was open for 10% -> 7% of each run, Pallas kernels for 0% -> 0%
where the time goes in v1:
time: 186 us; the launch traced here: 188 us
  Pallas kernels  66.3 us (36%)
  starting transfers between devices  53.6 us (29%)
  waiting for transfers between devices  36.2 us (19%)
  local copies, waits for them, and re-layouts  20 us (11%)
  other arithmetic  10.3 us (6%)
    pallas_call x1, Pallas kernels, run_block(): pl.pallas_call(functools.partial(kernel, blocks), out_shape=(S((N, D), bf...  55.2 us
    ppermute x20, starting transfers between devices, swap(): return lax.ppermute(x, axis, [(i, i ^ mask) for i in range(size)])  53.6 us
    ppermute x20, waiting for transfers between devices, swap(): return lax.ppermute(x, axis, [(i, i ^ mask) for i in range(size)])  36.2 us
    unnamed x48, local copies, waits for them, and re-layouts  9.9 us
    reshape x4, local copies, waits for them, and re-layouts, wide_mix(): mu = jnp.pad(mix[:64].reshape(8, 8), ((0, 0), (0, 120)))  4.72 us
    concatenate x8, other arithmetic, wide_mix(): return jnp.concatenate([mu, skip], axis=0)  4.41 us
    pallas_call x1, Pallas kernels, update(): pl.pallas_call(functools.partial(update_kernel, lines, trows, erows), out...  4.07 us
  transfers between devices with their start and end apart: 20, of which 11 were waited for; matrix products, arithmetic and copies ran while one was open for 7% of the time, Pallas kernels for 0%

profile of v1, /device:TPU:0, one launch (start us, length us, event | category | flops | bytes accessed | tf_op | source)
XLA Modules:
  0.0 187.9 jit_solution(17669044975889860828)
XLA Ops:
  0.7 0.7 convert.14
  1.4 0.9 convert.13
  2.3 1.3 convert.12
  3.7 4.0 %collective-permute-start.2 = (bf16[160,1024]{1,0:T(8,128)(2,1)S(1)}, bf16[160,1024]{1,0:T(8,128)(2,1)S(1)}, u32[]{:S(2)}, u32[]{:S(2)}) collective-permute-start(bf16[160,1024]{1,0:T(8,128)(2,1)S(1)} %constant_dynamic-slice_fusion), channel_id=1, source_target_pairs={{0,3},{1,2},{2,1},{3,0},{4,7},{5,6},{6,5},{7,4},{8,11},{9,10},{10,... | collective-permute-start | bytes 983048 | tf_op jit(solution)/shard_map/ppermute | solution.py:546
  9.6 6.7 %collective-permute-done.2.rest_2_ = bf16[160,1024]{1,0:T(8,128)(2,1)S(1)} collective-permute-done((bf16[160,1024]{1,0:T(8,128)(2,1)S(1)}, bf16[160,1024]{1,0:T(8,128)(2,1)S(1)}, u32[]{:S(2)}, u32[]{:S(2)}) %collective-permute-start.2) | collective-permute-done | bytes 327712 | tf_op jit(solution)/shard_map/ppermute | solution.py:546
  16.3 6.1 %collective-permute-done.1.rest_1_ = bf16[160,1024]{1,0:T(8,128)(2,1)S(1)} collective-permute-done((bf16[160,1024]{1,0:T(8,128)(2,1)S(1)}, bf16[160,1024]{1,0:T(8,128)(2,1)S(1)}, u32[]{:S(2)}, u32[]{:S(2)}) %collective-permute-start.1) | collective-permute-done | bytes 327712 | tf_op jit(solution)/shard_map/ppermute | solution.py:546
  25.3 0.7 broadcast_in_dim.2.mu_ref
  25.9 55.2 %layer.1 = (bf16[1024,256]{1,0:T(8,128)(2,1)}, bf16[1024,256]{1,0:T(8,128)(2,1)}, bf16[4,160,1024]{2,1,0:T(8,128)(2,1)}, bf16[4,160,1024]{2,1,0:T(8,128)(2,1)}) custom-call(s32[3]{0:T(128)} %pad_add_fusion.place_ref, s32[1]{0:T(128)S(6)} %copy.43.live_ref, s32[8]{0:T(128)} %cnt_ref.1, f32[4]{0:T(128)} %slice.54.skip_ref, s32[1,1024]{1,0:T(1,128)} %bitcast.9, ...), custom_call_target="tpu_custom_call" | custom-call | tf_op jit(solution)/shard_map/layer/pallas_call | solution.py:384
  81.1 27.0 %collective-permute-start.6 = (bf16[4,160,1024]{2,1,0:T(8,128)(2,1)}, bf16[4,160,1024]{2,1,0:T(8,128)(2,1)S(1)}, u32[]{:S(2)}, u32[]{:S(2)}) collective-permute-start(bf16[4,160,1024]{2,1,0:T(8,128)(2,1)} %get-tuple-element.49), channel_id=1, source_target_pairs={{0,4},{4,0},{8,12},{12,8},{16,20},{20,16},{24,28},{28,24},{1,5},{5... | collective-permute-start | bytes 3932168 | tf_op jit(solution)/shard_map/ppermute | solution.py:546
  108.1 0.7 slice.57
  108.9 0.7 slice.61
  109.6 0.7 slice.63
  110.3 0.7 reshape.80
  111.1 1.3 reshape.83
  112.4 1.3 reshape.82
  114.5 1.1 copy-done.16
  115.5 3.0 %add_core.1 = (bf16[160,1024]{1,0:T(8,128)(2,1)}, bf16[160,1024]{1,0:T(8,128)(2,1)}, bf16[160,1024]{1,0:T(8,128)(2,1)}, bf16[160,1024]{1,0:T(8,128)(2,1)}) custom-call(bf16[4,160,1024]{2,1,0:T(8,128)(2,1)} %get-tuple-element.48.keep_ref, bf16[4,160,1024]{2,1,0:T(8,128)(2,1)} %copy-done.16), custom_call_target="tpu_custom_call" | custom-call | tf_op jit(solution)/shard_map/add_core/pallas_call | solution.py:424
  118.6 6.8 %collective-permute-start.8 = (bf16[160,1024]{1,0:T(8,128)(2,1)}, bf16[160,1024]{1,0:T(8,128)(2,1)}, u32[]{:S(2)}, u32[]{:S(2)}) collective-permute-start(bf16[160,1024]{1,0:T(8,128)(2,1)} %get-tuple-element.52), channel_id=1, source_target_pairs={{0,2},{1,3},{2,0},{3,1},{4,6},{5,7},{6,4},{7,5},{8,10},{9,11},{10,... | collective-permute-start | bytes 983048 | tf_op jit(solution)/shard_map/ppermute | solution.py:546
  125.5 0.8 select_maximum_fusion.refs_23_
  126.3 3.2 %collective-permute-done.7.refs_1_ = bf16[160,1024]{1,0:T(8,128)(2,1)} collective-permute-done((bf16[160,1024]{1,0:T(8,128)(2,1)}, bf16[160,1024]{1,0:T(8,128)(2,1)}, u32[]{:S(2)}, u32[]{:S(2)}) %collective-permute-start.7) | collective-permute-done | bytes 327712 | tf_op jit(solution)/shard_map/ppermute | solution.py:546
  129.5 10.9 %collective-permute-done.8.refs_2_ = bf16[160,1024]{1,0:T(8,128)(2,1)} collective-permute-done((bf16[160,1024]{1,0:T(8,128)(2,1)}, bf16[160,1024]{1,0:T(8,128)(2,1)}, u32[]{:S(2)}, u32[]{:S(2)}) %collective-permute-start.8) | collective-permute-done | bytes 327712 | tf_op jit(solution)/shard_map/ppermute | solution.py:546
  140.4 2.4 %add_parts.1 = (bf16[160,256]{1,0:T(8,128)(2,1)}, bf16[160,256]{1,0:T(8,128)(2,1)}, bf16[160,256]{1,0:T(8,128)(2,1)}, bf16[160,256]{1,0:T(8,128)(2,1)}) custom-call(s32[1]{0:T(128)} %bitcast.2.zi_ref, bf16[160,1024]{1,0:T(8,128)(2,1)} %get-tuple-element.50.refs_0_, bf16[160,1024]{1,0:T(8,128)(2,1)} %collective-permute-done.7.refs_1_, ...), custom_call_target="tpu_custom_call" | custom-call | tf_op jit(solution)/shard_map/add_parts/pallas_call | solution.py:446
  142.8 7.5 %collective-permute-start.10 = (bf16[160,256]{1,0:T(8,128)(2,1)}, bf16[160,256]{1,0:T(8,128)(2,1)}, u32[]{:S(2)}, u32[]{:S(2)}) collective-permute-start(bf16[160,256]{1,0:T(8,128)(2,1)} %get-tuple-element.55), channel_id=1, source_target_pairs={{0,8},{4,12},{8,0},{12,4},{16,24},{20,28},{24,16},{28,20},{1,9},{5... | collective-permute-start | bytes 245768 | tf_op jit(solution)/shard_map/ppermute | solution.py:546
  150.3 2.4 %collective-permute-start.12 = (bf16[160,256]{1,0:T(8,128)(2,1)}, bf16[160,256]{1,0:T(8,128)(2,1)}, u32[]{:S(2)}, u32[]{:S(2)}) collective-permute-start(bf16[160,256]{1,0:T(8,128)(2,1)} %get-tuple-element.57), channel_id=1, source_target_pairs={{0,24},{4,28},{8,16},{12,20},{16,8},{20,12},{24,0},{28,4},{1,25},{... | collective-permute-start | bytes 245768 | tf_op jit(solution)/shard_map/ppermute | solution.py:546
  152.7 1.4 select_maximum_fusion.1.refs_22_
  154.0 1.2 slice.59
  155.3 1.3 reshape.81
  156.6 1.9 %collective-permute-done.11.refs_2_ = bf16[160,256]{1,0:T(8,128)(2,1)} collective-permute-done((bf16[160,256]{1,0:T(8,128)(2,1)}, bf16[160,256]{1,0:T(8,128)(2,1)}, u32[]{:S(2)}, u32[]{:S(2)}) %collective-permute-start.11) | collective-permute-done | bytes 81952 | tf_op jit(solution)/shard_map/ppermute | solution.py:546
  158.5 1.7 add_lines.1.refs_0_
  160.2 1.2 collective-permute-start.15
  161.4 2.3 %collective-permute-start.14 = (bf16[160,256]{1,0:T(8,128)(2,1)}, bf16[160,256]{1,0:T(8,128)(2,1)S(1)}, u32[]{:S(2)}, u32[]{:S(2)}) collective-permute-start(bf16[160,256]{1,0:T(8,128)(2,1)} %add_lines.1.refs_0_), channel_id=1, source_target_pairs={{0,16},{4,20},{8,24},{12,28},{16,0},{20,4},{24,8},{28,12},{1,17},{... | collective-permute-start | bytes 245768 | tf_op jit(solution)/shard_map/ppermute | solution.py:546
  163.7 0.9 collective-permute-start.13
  164.6 0.7 pad_select_fusion.2
  165.3 2.3 %collective-permute-done.15.refs_3_ = bf16[160,256]{1,0:T(8,128)(2,1)S(1)} collective-permute-done((bf16[160,256]{1,0:T(8,128)(2,1)}, bf16[160,256]{1,0:T(8,128)(2,1)S(1)}, u32[]{:S(2)}, u32[]{:S(2)}) %collective-permute-start.15) | collective-permute-done | bytes 81952 | tf_op jit(solution)/shard_map/ppermute | solution.py:546
  167.6 3.7 %collective-permute-done.14.refs_2_ = bf16[160,256]{1,0:T(8,128)(2,1)S(1)} collective-permute-done((bf16[160,256]{1,0:T(8,128)(2,1)}, bf16[160,256]{1,0:T(8,128)(2,1)S(1)}, u32[]{:S(2)}, u32[]{:S(2)}) %collective-permute-start.14) | collective-permute-done | bytes 81952 | tf_op jit(solution)/shard_map/ppermute | solution.py:546
  171.8 0.8 select_maximum_fusion.2.refs_21_
  172.8 1.2 copy-done.3
  174.0 0.9 copy-done.5
  174.9 0.9 copy-done.7
  175.8 0.9 copy-done.8
  176.8 0.7 copy-done.9
  177.5 0.7 copy-done.10
  178.1 0.7 copy-done.11
  178.8 0.7 copy-done.12
  179.5 0.7 copy-done.13
  180.2 0.7 copy-done.14
  180.9 4.1 %update.1 = (f32[256,1024]{1,0:T(8,128)}, f32[256,1024]{1,0:T(8,128)}, f32[256,1024]{1,0:T(8,128)}, f32[256,1024]{1,0:T(8,128)}, f32[64,768]{1,0:T(8,128)}, /*in...) custom-call(s32[3]{0:T(128)S(1)} %copy-done.11, ...), custom_call_target="tpu_custom_call" | custom-call | tf_op jit(solution)/shard_map/update/pallas_call | solution.py:510
  185.6 0.6 pad_maximum_fusion.1
  (87 shorter events, 8.1 us)
Async XLA Ops:
  3.6 4.7 %copy-start.23 = (f32[68]{0:T(128)S(1)}, f32[68]{0:T(128)}, u32[]{:S(2)}) copy-start(f32[68]{0:T(128)} %param.45) | copy-start | bytes 820
  3.7 22.3 %copy-start.15 = (bf16[320,1024]{1,0:T(8,128)(2,1)}, bf16[320,1024]{1,0:T(8,128)(2,1)S(1)}, u32[]{:S(2)}) copy-start(bf16[320,1024]{1,0:T(8,128)(2,1)S(1)} %fusion.4.own_ref) | copy-start | bytes 1966084
  3.7 12.5 %collective-permute-start.2 = (bf16[160,1024]{1,0:T(8,128)(2,1)S(1)}, bf16[160,1024]{1,0:T(8,128)(2,1)S(1)}, u32[]{:S(2)}, u32[]{:S(2)}) collective-permute-start(bf16[160,1024]{1,0:T(8,128)(2,1)S(1)} %constant_dynamic-slice_fusion), channel_id=1, source_target_pairs={{0,3},{1,2},{2,1},{3,0},{4,7},{5,6},{6,5},{7,4},{8,11},{9,10},{10,... | collective-permute-start | bytes 983048 | tf_op jit(solution)/shard_map/ppermute | solution.py:546
  7.7 14.7 %collective-permute-start.1 = (bf16[160,1024]{1,0:T(8,128)(2,1)S(1)}, bf16[160,1024]{1,0:T(8,128)(2,1)S(1)}, u32[]{:S(2)}, u32[]{:S(2)}) collective-permute-start(bf16[160,1024]{1,0:T(8,128)(2,1)S(1)} %constant_dynamic-slice_fusion), channel_id=1, source_target_pairs={{0,2},{1,3},{2,0},{3,1},{4,6},{5,7},{6,4},{7,5},{8,10},{9,11},{10,... | collective-permute-start | bytes 983048 | tf_op jit(solution)/shard_map/ppermute | solution.py:546
  8.2 14.5 %collective-permute-start = (bf16[160,1024]{1,0:T(8,128)(2,1)S(1)}, bf16[160,1024]{1,0:T(8,128)(2,1)S(1)}, u32[]{:S(2)}, u32[]{:S(2)}) collective-permute-start(bf16[160,1024]{1,0:T(8,128)(2,1)S(1)} %constant_dynamic-slice_fusion), channel_id=1, source_target_pairs={{0,1},{1,0},{2,3},{3,2},{4,5},{5,4},{6,7},{7,6},{8,9},{9,8},{10,11... | collective-permute-start | bytes 983048 | tf_op jit(solution)/shard_map/ppermute | solution.py:546
  16.3 9.7 %copy-start.17 = (bf16[160,1024]{1,0:T(8,128)(2,1)}, bf16[160,1024]{1,0:T(8,128)(2,1)S(1)}, u32[]{:S(2)}) copy-start(bf16[160,1024]{1,0:T(8,128)(2,1)S(1)} %collective-permute-done.2.rest_2_) | copy-start | bytes 983044
  16.3 7.3 %collective-permute-start.5 = (bf16[160,1024]{1,0:T(8,128)(2,1)S(1)}, bf16[160,1024]{1,0:T(8,128)(2,1)S(1)}, u32[]{:S(2)}, u32[]{:S(2)}) collective-permute-start(bf16[160,1024]{1,0:T(8,128)(2,1)S(1)} %collective-permute-done.2.rest_2_), channel_id=1, source_target_pairs={{0,4},{4,0},{8,12},{12,8},{16,20},{20,16},{24,28},{28,24},{1,5},{5... | collective-permute-start | bytes 983048 | tf_op jit(solution)/shard_map/ppermute | solution.py:546
  22.4 1.2 copy-start.18
  22.4 1.6 collective-permute-start.4
  22.7 1.3 copy-start.19
  22.7 1.8 collective-permute-start.3
  23.6 0.9 copy-start.20
  24.1 0.7 copy-start.21
  24.5 0.7 copy-start.22
  81.1 33.3 %collective-permute-start.6 = (bf16[4,160,1024]{2,1,0:T(8,128)(2,1)}, bf16[4,160,1024]{2,1,0:T(8,128)(2,1)S(1)}, u32[]{:S(2)}, u32[]{:S(2)}) collective-permute-start(bf16[4,160,1024]{2,1,0:T(8,128)(2,1)} %get-tuple-element.49), channel_id=1, source_target_pairs={{0,4},{4,0},{8,12},{12,8},{16,20},{20,16},{24,28},{28,24},{1,5},{5... | collective-permute-start | bytes 3932168 | tf_op jit(solution)/shard_map/ppermute | solution.py:546
  114.5 1.1 copy-start.16
  115.5 57.2 %copy-start.1 = (f32[256,1024]{1,0:T(8,128)S(1)}, f32[256,1024]{1,0:T(8,128)}, u32[]{:S(2)}) copy-start(f32[256,1024]{1,0:T(8,128)} %refs_9_.1) | copy-start | bytes 3145732
  115.5 57.2 %copy-start.2 = (f32[256,1024]{1,0:T(8,128)S(1)}, f32[256,1024]{1,0:T(8,128)}, u32[]{:S(2)}) copy-start(f32[256,1024]{1,0:T(8,128)} %refs_10_.1) | copy-start | bytes 3145732
  118.5 54.2 %copy-start = (f32[256,1024]{1,0:T(8,128)S(1)}, f32[256,1024]{1,0:T(8,128)}, u32[]{:S(2)}) copy-start(f32[256,1024]{1,0:T(8,128)} %refs_8_.1) | copy-start | bytes 3145732
  118.5 54.2 %copy-start.4 = (f32[64,768]{1,0:T(8,128)S(1)}, f32[64,768]{1,0:T(8,128)}, u32[]{:S(2)}) copy-start(f32[64,768]{1,0:T(8,128)} %refs_12_.1) | copy-start | bytes 589828
  118.5 54.2 %copy-start.6 = (f32[64,768]{1,0:T(8,128)S(1)}, f32[64,768]{1,0:T(8,128)}, u32[]{:S(2)}) copy-start(f32[64,768]{1,0:T(8,128)} %refs_13_.1) | copy-start | bytes 589828
  118.5 11.0 %collective-permute-start.7 = (bf16[160,1024]{1,0:T(8,128)(2,1)}, bf16[160,1024]{1,0:T(8,128)(2,1)}, u32[]{:S(2)}, u32[]{:S(2)}) collective-permute-start(bf16[160,1024]{1,0:T(8,128)(2,1)} %get-tuple-element.51), channel_id=1, source_target_pairs={{0,1},{1,0},{2,3},{3,2},{4,5},{5,4},{6,7},{7,6},{8,9},{9,8},{10,11... | collective-permute-start | bytes 983048 | tf_op jit(solution)/shard_map/ppermute | solution.py:546
  118.6 21.8 %collective-permute-start.8 = (bf16[160,1024]{1,0:T(8,128)(2,1)}, bf16[160,1024]{1,0:T(8,128)(2,1)}, u32[]{:S(2)}, u32[]{:S(2)}) collective-permute-start(bf16[160,1024]{1,0:T(8,128)(2,1)} %get-tuple-element.52), channel_id=1, source_target_pairs={{0,2},{1,3},{2,0},{3,1},{4,6},{5,7},{6,4},{7,5},{8,10},{9,11},{10,... | collective-permute-start | bytes 983048 | tf_op jit(solution)/shard_map/ppermute | solution.py:546
  125.4 14.9 %collective-permute-start.9 = (bf16[160,1024]{1,0:T(8,128)(2,1)}, bf16[160,1024]{1,0:T(8,128)(2,1)}, u32[]{:S(2)}, u32[]{:S(2)}) collective-permute-start(bf16[160,1024]{1,0:T(8,128)(2,1)} %get-tuple-element.53), channel_id=1, source_target_pairs={{0,3},{1,2},{2,1},{3,0},{4,7},{5,6},{6,5},{7,4},{8,11},{9,10},{10,... | collective-permute-start | bytes 983048 | tf_op jit(solution)/shard_map/ppermute | solution.py:546
  142.8 13.8 %collective-permute-start.10 = (bf16[160,256]{1,0:T(8,128)(2,1)}, bf16[160,256]{1,0:T(8,128)(2,1)}, u32[]{:S(2)}, u32[]{:S(2)}) collective-permute-start(bf16[160,256]{1,0:T(8,128)(2,1)} %get-tuple-element.55), channel_id=1, source_target_pairs={{0,8},{4,12},{8,0},{12,4},{16,24},{20,28},{24,16},{28,20},{1,9},{5... | collective-permute-start | bytes 245768 | tf_op jit(solution)/shard_map/ppermute | solution.py:546
  150.3 8.2 %collective-permute-start.11 = (bf16[160,256]{1,0:T(8,128)(2,1)}, bf16[160,256]{1,0:T(8,128)(2,1)}, u32[]{:S(2)}, u32[]{:S(2)}) collective-permute-start(bf16[160,256]{1,0:T(8,128)(2,1)} %get-tuple-element.56), channel_id=1, source_target_pairs={{0,16},{4,20},{8,24},{12,28},{16,0},{20,4},{24,8},{28,12},{1,17},{... | collective-permute-start | bytes 245768 | tf_op jit(solution)/shard_map/ppermute | solution.py:546
  150.3 8.2 %collective-permute-start.12 = (bf16[160,256]{1,0:T(8,128)(2,1)}, bf16[160,256]{1,0:T(8,128)(2,1)}, u32[]{:S(2)}, u32[]{:S(2)}) collective-permute-start(bf16[160,256]{1,0:T(8,128)(2,1)} %get-tuple-element.57), channel_id=1, source_target_pairs={{0,24},{4,28},{8,16},{12,20},{16,8},{20,12},{24,0},{28,4},{1,25},{... | collective-permute-start | bytes 245768 | tf_op jit(solution)/shard_map/ppermute | solution.py:546
  160.2 7.4 %collective-permute-start.15 = (bf16[160,256]{1,0:T(8,128)(2,1)}, bf16[160,256]{1,0:T(8,128)(2,1)S(1)}, u32[]{:S(2)}, u32[]{:S(2)}) collective-permute-start(bf16[160,256]{1,0:T(8,128)(2,1)} %add_lines.1.refs_0_), channel_id=1, source_target_pairs={{0,24},{4,28},{8,16},{12,20},{16,8},{20,12},{24,0},{28,4},{1,25},{... | collective-permute-start | bytes 245768 | tf_op jit(solution)/shard_map/ppermute | solution.py:546
  161.4 9.9 %collective-permute-start.14 = (bf16[160,256]{1,0:T(8,128)(2,1)}, bf16[160,256]{1,0:T(8,128)(2,1)S(1)}, u32[]{:S(2)}, u32[]{:S(2)}) collective-permute-start(bf16[160,256]{1,0:T(8,128)(2,1)} %add_lines.1.refs_0_), channel_id=1, source_target_pairs={{0,16},{4,20},{8,24},{12,28},{16,0},{20,4},{24,8},{28,12},{1,17},{... | collective-permute-start | bytes 245768 | tf_op jit(solution)/shard_map/ppermute | solution.py:546
  163.7 7.6 %collective-permute-start.13 = (bf16[160,256]{1,0:T(8,128)(2,1)}, bf16[160,256]{1,0:T(8,128)(2,1)S(1)}, u32[]{:S(2)}, u32[]{:S(2)}) collective-permute-start(bf16[160,256]{1,0:T(8,128)(2,1)} %add_lines.1.refs_0_), channel_id=1, source_target_pairs={{0,8},{4,12},{8,0},{12,4},{16,24},{20,28},{24,16},{28,20},{1,9},{5... | collective-permute-start | bytes 245768 | tf_op jit(solution)/shard_map/ppermute | solution.py:546
  165.3 7.3 %collective-permute-start.16 = (bf16[160,256]{1,0:T(8,128)(2,1)}, bf16[160,256]{1,0:T(8,128)(2,1)S(1)}, u32[]{:S(2)}, u32[]{:S(2)}) collective-permute-start(bf16[160,256]{1,0:T(8,128)(2,1)} %add_lines.1.refs_0_), channel_id=1, source_target_pairs={{0,4},{4,0},{8,12},{12,8},{16,20},{20,16},{24,28},{28,24},{1,5},{5... | collective-permute-start | bytes 245768 | tf_op jit(solution)/shard_map/ppermute | solution.py:546
  167.6 5.0 %collective-permute-start.19 = (bf16[160,256]{1,0:T(8,128)(2,1)S(1)}, bf16[160,256]{1,0:T(8,128)(2,1)S(1)}, u32[]{:S(2)}, u32[]{:S(2)}) collective-permute-start(bf16[160,256]{1,0:T(8,128)(2,1)S(1)} %collective-permute-done.15.refs_3_), channel_id=1, source_target_pairs={{0,4},{4,0},{8,12},{12,8},{16,20},{20,16},{24,28},{28,24},{1,5},{5... | collective-permute-start | bytes 245768 | tf_op jit(solution)/shard_map/ppermute | solution.py:546
  171.3 1.3 collective-permute-start.18
  171.3 1.4 collective-permute-start.17
  172.8 1.2 copy-start.3
  174.0 0.9 copy-start.5
  174.9 0.9 copy-start.7
  175.8 0.9 copy-start.8
  176.8 0.7 copy-start.9
  177.5 0.7 copy-start.10
  178.1 0.7 copy-start.11
  178.8 0.7 copy-start.12
  179.5 0.7 copy-start.13
  180.2 0.7 copy-start.14

commit v2 on v1

v2 whole, which is shorter than its diff:
```python
import functools

import jax
import jax.numpy as jnp
import numpy as np
from jax import lax
from jax.experimental import pallas as pl
from jax.experimental.pallas import tpu as pltpu
from jax.sharding import PartitionSpec as P

D, H, DK, TYPES, REL, TB = 256, 8, 32, 4, 8, 240
N = 1024
SLOTS = 1024
EC = 512
SUB = 128
NSUB = EC // SUB
NC = 256
EDGES = REL * SLOTS + EC
bf16 = jnp.bfloat16
f32 = jnp.float32
norm_eps = 1e-5
STEP = 10
beta_one = 0.9
beta_two = 0.999
adam_eps = 1e-08
decay_rate = 0.01
ema_keep = 0.7
rates = (0.2, 0.2, 0.6, 0.6)
score_scale = DK ** (-0.5)

SMEM = pl.BlockSpec(memory_space=pltpu.SMEM)
VMEM = pl.BlockSpec(memory_space=pltpu.VMEM)
ANY = pl.BlockSpec(memory_space=pl.ANY)
S = jax.ShapeDtypeStruct
V = pltpu.VMEM
MIB = 1 << 20
SOURCE, TARGET, TIME, TYPE, BUCKET = range(5)
LAYER_VMEM = 60 * MIB
GROUP = 4
WIDE = 1024 // GROUP


def nn(a, b):
    return jnp.dot(a, b, preferred_element_type=f32)


def nt(a, b):
    return lax.dot_general(a, b, (((1,), (1,)), ((), ())), preferred_element_type=f32)


def one_hot_rows(row, count):
    wide = row.shape[1]
    base = lax.broadcasted_iota(jnp.int32, (256, wide), 0).astype(bf16)
    one, zero = jnp.ones((), bf16), jnp.zeros((), bf16)
    return jnp.concatenate(
        [jnp.where(base == (row - 256 * g).astype(bf16), one, zero) for g in range(count // 256)], axis=0
    )


def head_sum(x):
    return jnp.sum(x.reshape(H, DK, x.shape[1]), axis=1)


def head_wide(x):
    return jnp.broadcast_to(x[:, None, :], (H, DK, x.shape[1])).reshape(D, x.shape[1])


def hi_lo(x):
    high = x.astype(bf16).astype(f32)
    return jnp.concatenate([high, x - high], axis=0).astype(bf16)


def eye():
    return (
        lax.broadcasted_iota(jnp.int32, (256, 256), 0) == lax.broadcasted_iota(jnp.int32, (256, 256), 1)
    ).astype(f32).astype(bf16)


def pick(masks, wide):
    out = wide[0] * masks[0:1]
    for s in range(1, TYPES):
        out = jnp.where(masks[s:s + 1] > 0, wide[s], out)
    return out


def stack(pieces):
    return pieces[0] if len(pieces) == 1 else jnp.concatenate(pieces, axis=0)


class Layout:
    def __init__(self, blocks):
        self.blocks = blocks
        self.trows, self.erows = TYPES * D // blocks, D // blocks
        self.part = self.trows + self.erows
        self.half = self.part // 2
        self.wide = D // blocks

    def type_rows(self, s):
        for f in range(self.blocks):
            a, b = max(s * D, f * self.trows), min((s + 1) * D, (f + 1) * self.trows)
            if a < b:
                yield f, f * self.part + a - f * self.trows, f * self.part + b - f * self.trows, a - s * D, b - s * D

    def get_type(self, ref, s, c0, c1):
        return stack([ref[a:b, c0:c1] for _, a, b, _, _ in self.type_rows(s)])

    def get_edge(self, ref, c0, c1):
        return stack([ref[f * self.part + self.trows:(f + 1) * self.part, c0:c1] for f in range(self.blocks)])

    def get_norm(self, ref):
        rows = [f * self.part + self.trows for f in range(self.blocks)]
        return jnp.concatenate([ref[a:a + 16, 768:768 + self.wide].astype(f32) for a in rows], axis=1).astype(bf16)

    def weight_copies(self, me, core, own, near, far, wpk, sems):
        out = [pltpu.make_async_copy(own, wpk.at[pl.ds(pl.multiple_of(me * self.part, 16), self.part)], sems.at[0])]
        for m in range(1, self.blocks):
            base = jnp.bitwise_xor(me, m) * self.part
            for i, (ref, side) in enumerate(((near[m - 1], core), (far[m - 1], 1 - core))):
                at = pl.ds(pl.multiple_of(base + side * self.half, 16), self.half)
                out.append(pltpu.make_async_copy(ref, wpk.at[at], sems.at[2 * m - 1 + i]))
        return out


def position():
    return lax.axis_index("fsdp"), lax.rem(lax.axis_index("dp"), 2), lax.div(lax.axis_index("dp"), 2)


def list_blocks(cnt_ref, lst_r, lst_o, lst_c):
    def put(k, r, j, c):
        lst_r[k] = r
        lst_o[k] = j
        lst_c[k] = c - j * SUB

    def pairs(r, k):
        c = cnt_ref[r]

        def one(j, k):
            put(k, r, 2 * j, c)
            put(k + 1, r, 2 * j + 1, c)
            return k + 2
        return lax.fori_loop(0, (c + SUB - 1) // SUB // 2, one, k)

    def odd(r, k):
        c = cnt_ref[r]
        blocks = (c + SUB - 1) // SUB
        put(k, r, jnp.minimum(blocks, SLOTS // SUB) - 1, c)
        return k + lax.rem(blocks, 2)
    paired = lax.fori_loop(0, REL, pairs, 0)
    total = lax.fori_loop(0, REL, odd, paired)
    for extra in range(2 * NSUB):
        put(total + extra, 0, 0, 0)
    return paired // NSUB, (total + NSUB - 1) // NSUB


def rows_of(ref, lst_r, lst_o, c):
    pieces = []
    for k in range(NSUB):
        r, j = lst_r[c * NSUB + k], lst_o[c * NSUB + k]
        pair = ref[pl.ds(r, 1), pl.ds(pl.multiple_of(lax.div(j, 2) * 2 * SUB, 2 * SUB), 2 * SUB)]
        pieces.append(jnp.where(lax.rem(j, 2) == 0, pair[:, :SUB], pair[:, SUB:]))
    return jnp.concatenate(pieces, axis=1)


def place(c):
    return pl.ds(pl.multiple_of(c * EC, EC), EC)


LISTS = [pltpu.SMEM((REL * SLOTS // SUB + 2 * NSUB,), jnp.int32)] * 3


def pack_half_kernel(lay, type_ref, edge_ref, norm_ref, mine_ref, buf, sems):
    _, core, _ = position()
    rest = lay.half - lay.erows
    for side in range(2):
        @pl.when(core == side)
        def _():
            rows = lay.half if side == 0 else rest
            first = pltpu.make_async_copy(
                type_ref.at[pl.ds(side * lay.half, rows)], buf.at[pl.ds(0, rows)], sems.at[0]
            )
            first.start()
            if side == 1:
                second = pltpu.make_async_copy(edge_ref, buf.at[pl.ds(rest, lay.erows), pl.ds(0, 768)], sems.at[1])
                second.start()
                corner = jnp.concatenate([norm_ref[...], jnp.zeros((8, 256 - lay.wide), f32)], axis=1)
                buf[rest:, 768:] = jnp.concatenate([corner, jnp.zeros((lay.erows - 8, 256), f32)], axis=0)
                second.wait()
            first.wait()
    mine_ref[...] = buf[...].astype(bf16)


def pack_half(lay, type_weight, edge_weight, norm_params):
    return pl.pallas_call(
        functools.partial(pack_half_kernel, lay),
        out_shape=S((lay.half, 1024), bf16),
        in_specs=[ANY, ANY, VMEM],
        scratch_shapes=[V((lay.half, 1024), f32), pltpu.SemaphoreType.DMA((2,))],
        compiler_params=pltpu.CompilerParams(vmem_limit_bytes=63 * MIB),
        name="pack_half",
    )(type_weight, edge_weight, norm_params)


def pack_kernel(lay, type_ref, edge_ref, norm_ref, own_ref):
    own_ref[0:lay.trows, :] = type_ref[...].astype(bf16)
    own_ref[lay.trows:, 0:768] = edge_ref[...].astype(bf16)
    corner = jnp.concatenate([norm_ref[...], jnp.zeros((8, 256 - lay.wide), f32)], axis=1)
    own_ref[lay.trows:, 768:] = jnp.concatenate([corner, jnp.zeros((lay.erows - 8, 256), f32)], axis=0).astype(bf16)


def pack(lay, type_weight, edge_weight, norm_params):
    return pl.pallas_call(
        functools.partial(pack_kernel, lay),
        out_shape=S((lay.part, 1024), bf16),
        compiler_params=pltpu.CompilerParams(vmem_limit_bytes=63 * MIB),
        name="pack",
    )(type_weight, edge_weight, norm_params)


def before_kernel(cnt_ref, kinds_ref, src_ref, dst_ref, tim_ref, feat_ref, idx_ref, xg_ref, typ_ref, lst_r, lst_o, lst_c):
    _, chunks = list_blocks(cnt_ref, lst_r, lst_o, lst_c)
    src = src_ref[...]
    for j in range(SLOTS // 128):
        idx = src[:, j * 128:(j + 1) * 128]
        low = jnp.bitwise_and(idx, 127)
        high = jnp.right_shift(idx, 7)
        acc = jnp.zeros((8, 128), jnp.int32)
        for k in range(N // 128):
            row = jnp.broadcast_to(kinds_ref[:, k * 128:(k + 1) * 128], (8, 128))
            acc = jnp.where(high == k, jnp.take_along_axis(row, low, axis=1), acc)
        typ_ref[:, j * 128:(j + 1) * 128] = acc
    ft = nt(eye(), feat_ref[...]).astype(bf16)

    def one(c, _):
        src, dst, tim, typ = [rows_of(ref, lst_r, lst_o, c) for ref in (src_ref, dst_ref, tim_ref, typ_ref)]
        idx_ref[pl.ds(pl.multiple_of(c * 8, 8), 8), :] = jnp.concatenate(
            [src, dst, tim, typ, typ * 256 + tim, src, src, src], axis=0
        )
        xg_ref[:, place(c)] = nn(ft, one_hot_rows(src, N)).astype(bf16)
        return 0

    lax.fori_loop(0, chunks, one, 0)


def before(cnt, kinds, src, dst, tim, feat):
    return pl.pallas_call(
        before_kernel,
        out_shape=(S((EDGES // EC * 8, EC), jnp.int32), S((D, EDGES), bf16)),
        in_specs=[SMEM] + [VMEM] * 5,
        scratch_shapes=[V((REL, SLOTS), jnp.int32)] + LISTS,
        compiler_params=pltpu.CompilerParams(vmem_limit_bytes=63 * MIB),
        cost_estimate=pl.CostEstimate(flops=2 * D * N * EDGES, bytes_accessed=6 * MIB, transcendentals=0),
        name="before",
    )(cnt, kinds, src, dst, tim, feat)


def layer_kernel(lay, *refs):
    nb = lay.blocks - 1
    (
        live_ref, cnt_ref, kinds_ref, mix_ref, idx_ref, emb_ref, cot_hbm, feat_hbm, own_ref,
    ) = refs[:9]
    near, far, xg_hbm = refs[9:9 + nb], refs[9 + nb:9 + 2 * nb], refs[9 + 2 * nb]
    (
        out_ref, dqkv_ref, skp_ref, keep_ref, send_ref,
        lst_r, lst_o, lst_c,
        wpk, gpack, gout, gnorm, gskip, xg, outs, low, cot_ref, feat_ref,
        wt, xcat, qt, rte, dn_buf, dkve_buf, mu,
        bda, bdat, bdm, bdmt, ga, gm, dmu,
        kve, qe, msg, wexp, raws,
        num, dnum, dqkv, dtkv, skp,
        wsem, xsem, osem, gsem,
    ) = refs[10 + 2 * nb:]
    me, core, zi = position()
    zi = lax.rem(zi, GROUP)
    feat_copy = pltpu.make_async_copy(feat_hbm, feat_ref, xsem.at[1])
    feat_copy.start()
    weights = lay.weight_copies(me, core, own_ref, near, far, wpk, wsem)
    for copy in weights:
        copy.start()
    xg_copy = pltpu.make_async_copy(xg_hbm, xg, xsem.at[0])
    xg_copy.start()
    cot_copy = pltpu.make_async_copy(cot_hbm, cot_ref, xsem.at[2])

    ident = eye()
    whole, chunks = list_blocks(cnt_ref, lst_r, lst_o, lst_c)

    def row(c, k):
        return idx_ref[pl.ds(pl.multiple_of(c * 8, 8), 8), :][k:k + 1]

    for ref in (num, dqkv, dtkv, ga, gm, dmu, gnorm, gskip, gout):
        ref[...] = jnp.zeros_like(ref)
    dkve_buf[...] = jnp.zeros_like(dkve_buf)

    mix = jnp.broadcast_to(mix_ref[...].astype(bf16).astype(f32), (8, 68))
    lanes68 = lax.broadcasted_iota(jnp.int32, (8, 68), 1)
    line68 = lax.broadcasted_iota(jnp.int32, (8, 68), 0)

    def column(first):
        return jnp.sum(jnp.where(lanes68 == first + line68, mix, 0.0), axis=1, keepdims=True)

    for r in range(REL):
        mu[r] = jnp.broadcast_to(column(r * H) * score_scale, (H, 128))
    skip_col = column(REL * H)

    kinds = kinds_ref[...]
    masks = (lax.broadcasted_iota(jnp.int32, (8, N), 0) == kinds).astype(f32)
    feat_copy.wait()
    featt = nt(ident, feat_ref[...])
    for s in range(TYPES):
        xcat[s * D:(s + 1) * D, :] = (featt * masks[s:s + 1]).astype(bf16)
    for copy in weights:
        copy.wait()
    cot_copy.start()

    lane = lax.broadcasted_iota(jnp.int32, (D, 128), 1)
    rowi = lax.broadcasted_iota(jnp.int32, (D, 128), 0)
    on_diag = (lane // DK) == (rowi // DK) % 4
    zeros = jnp.zeros((128, 128), f32)
    for p in range(4):
        x = lay.get_edge(wpk, p * 128, (p + 1) * 128).astype(f32)
        rolled = [x if k == 0 else pltpu.roll(x, 32 * k, 1) for k in range(4)]
        for g in range(4):
            r, m = 2 * p + g // 2, g % 2
            t = jnp.concatenate([rolled[(h % 4 - g) % 4][h * 32:(h + 1) * 32] for h in range(H)], axis=0)
            t = jnp.where(on_diag, t, 0.0)
            for ref, a, b in (
                (bdm if m else bda, t[:128], t[128:]), (bdmt if m else bdat, t[:128].T, t[128:].T)
            ):
                ref[r] = jnp.concatenate(
                    [jnp.concatenate([a, zeros], axis=1), jnp.concatenate([zeros, b], axis=1)], axis=0
                ).astype(bf16)

    for cb in range(4):
        for s in range(4):
            wt[cb * 256:(cb + 1) * 256, s * 256:(s + 1) * 256] = nt(
                ident, lay.get_type(wpk, s, cb * 256, (cb + 1) * 256)
            ).astype(bf16)
    qt[...] = nn(wt[:D, :], xcat[...]).astype(bf16)
    wet = nt(ident, lay.get_edge(wpk, 512, 768)).astype(bf16)
    rte[...] = nt(wet, emb_ref[...]).astype(bf16)

    def mu_of(c):
        return jnp.concatenate([mu[lst_r[c * NSUB + k]] for k in range(NSUB)], axis=1)

    def blocks_of(c, wide):
        return [(lst_r[c * NSUB + k * (wide // SUB)], slice(k * wide, (k + 1) * wide)) for k in range(EC // wide)]

    def lookup(c):
        rt = nn(rte[...], one_hot_rows(row(c, TIME), 256))
        return (xg[:, place(c)].astype(f32) + rt).astype(bf16)

    def lookup_q(c):
        qe[:, place(c)] = nn(qt[...], one_hot_rows(row(c, TARGET), N)).astype(bf16)

    def project(c, xe):
        cu = row(c, TYPE)
        zero = jnp.zeros((), bf16)
        xm = jnp.concatenate([jnp.where(cu == s, xe, zero) for s in range(TYPES)], axis=0)
        kve[:, place(c)] = nn(wt[D:3 * D, :], xm).astype(bf16)

    def forward(wide, c, _):
        at = place(c)
        kv_e = kve[:, at]
        q_e = qe[:, at].astype(f32)
        ks, ms = [], []
        for r, sl in blocks_of(c, wide):
            ks.append(nn(bdat[r], kv_e[:D, sl]))
            ms.append(nn(bdmt[r], kv_e[D:, sl]))
        ka = jnp.concatenate(ks, axis=1)
        me_ = jnp.concatenate(ms, axis=1)
        xe = lookup(c + 1)
        xg[:, at] = ka.astype(bf16)
        msg[:, at] = me_.astype(bf16)
        raw = head_sum(ka * q_e)
        raws[:, at] = raw
        lanes = lax.broadcasted_iota(jnp.int32, (H, SUB), 1)
        w = jnp.exp(raw * mu_of(c))
        w = jnp.concatenate(
            [jnp.where(lanes < lst_c[c * NSUB + k], w[:, k * SUB:(k + 1) * SUB], 0.0) for k in range(NSUB)], axis=1
        )
        wexp[:, at] = w
        wm = (head_wide(w) * me_).astype(bf16)
        lookup_q(c + 1)
        num[...] += nt(jnp.concatenate([wm, hi_lo(w)], axis=0), one_hot_rows(row(c, TARGET), N))
        project(c + 1, xe)
        return 0

    xg_copy.wait()
    project(0, lookup(0))
    lookup_q(0)
    lax.fori_loop(0, whole, functools.partial(forward, 2 * SUB), 0)
    lax.fori_loop(whole, chunks, functools.partial(forward, SUB), 0)

    cot_copy.wait()
    nwt = nt(ident, lay.get_norm(wpk))

    def nodes(c):
        at = pl.ds(pl.multiple_of(c * NC, NC), NC)
        mk = (lax.broadcasted_iota(jnp.int32, (8, NC), 0) == kinds_ref[:, at]).astype(f32)
        live = (lax.broadcasted_iota(jnp.int32, (1, NC), 1) + c * NC < live_ref[0]).astype(f32)
        den = num[D:D + H, at] + num[D + H:, at] + (1.0 - live)
        denw = head_wide(den)
        agg = num[:D, at] / denw
        phi = 0.5 * (1.0 + lax.erf(agg * (0.5 ** 0.5)))
        act = (agg * phi).astype(bf16).astype(f32)
        acat = jnp.concatenate([(act * mk[s:s + 1]).astype(bf16) for s in range(TYPES)], axis=0)
        yield
        trans = nn(wt[3 * D:, :], acat)
        yield
        alpha = 1.0 / (1.0 + jnp.exp(-jnp.sum(mk * skip_col, axis=0, keepdims=True)))
        ft = nt(ident, feat_ref[at, :])
        res = alpha * trans + (1.0 - alpha) * ft
        mean = jnp.mean(res, axis=0, keepdims=True)
        cen = res - mean
        inv = lax.rsqrt(jnp.mean(cen * cen, axis=0, keepdims=True) + norm_eps)
        nrm = cen * inv
        gain = nwt[:, 0:1] * mk[0:1]
        bias = nwt[:, 4:5] * mk[0:1]
        for s in range(1, TYPES):
            gain = gain + nwt[:, s:s + 1] * mk[s:s + 1]
            bias = bias + nwt[:, 4 + s:5 + s] * mk[s:s + 1]
        outs[at, :] = (live * (nrm * gain + bias)).T.astype(bf16)
        dy = live * nt(ident, cot_ref[at, :])
        oh16 = jnp.concatenate([mk, jnp.zeros((8, NC), f32)], axis=0).astype(bf16)
        dyn = dy * nrm
        dyn_hi = dyn.astype(bf16)
        dyn_lo = (dyn - dyn_hi.astype(f32)).astype(bf16)
        gnorm[0:4, :] += (nt(oh16, dyn_hi) + nt(oh16, dyn_lo))[0:4]
        gnorm[4:8, :] += nt(oh16, dy.astype(bf16))[0:4]
        dn = dy * gain
        dres = inv * (dn - jnp.mean(dn, axis=0, keepdims=True) - nrm * jnp.mean(dn * nrm, axis=0, keepdims=True))
        dtr = (alpha * dres).astype(bf16)
        yield
        dact = pick(mk, [nn(lay.get_type(wpk, s, 3 * D, 4 * D), dtr) for s in range(TYPES)])
        yield
        skp[:, at] = (1.0 - alpha) * dres
        dal = jnp.sum(dres * (trans - ft), axis=0, keepdims=True) * alpha * (1.0 - alpha)
        gskip[...] += jnp.broadcast_to(jnp.sum(mk * dal, axis=1, keepdims=True), (8, 128))
        gout[...] += nt(acat, dtr)
        dagg = dact * (phi + agg * (jnp.exp(-0.5 * agg * agg) * (0.5 / np.pi) ** 0.5))
        dnum[0:D, at] = (dagg / denw).astype(bf16)
        dnum[D:, at] = hi_lo(-head_sum(dagg * agg) / den)
        yield

    def node_steps(c, _):
        for _ in zip(nodes(2 * c), nodes(2 * c + 1)):
            pass
        return 0

    lax.fori_loop(0, N // NC // 2, node_steps, 0)
    finish = [
        pltpu.make_async_copy(outs, out_ref, osem.at[0]),
        pltpu.make_async_copy(skp, skp_ref, osem.at[1]),
    ]
    for copy in finish:
        copy.start()

    def gather_back(c):
        dn_buf[...] = nn(dnum[...], one_hot_rows(row(c, TARGET), N))

    def scatter_back(c):
        dkve = dkve_buf[...]
        dqkv[:, D:] += nt(one_hot_rows(row(c, SOURCE), N), dkve)
        dtkv[...] += nt(one_hot_rows(row(c, BUCKET), 1024), dkve)

    def backward(wide, c, _):
        at = place(c)
        scatter_back(jnp.maximum(c - 1, 0))
        dn_e = dn_buf[:D]
        w = wexp[:, at]
        dw = head_sum(dn_e * msg[:, at].astype(f32)) + dn_buf[D:D + H] + dn_buf[D + H:]
        ds = dw * w
        dsr = ds * raws[:, at]
        ss = head_wide(ds * mu_of(c))
        dka = (ss * qe[:, at].astype(f32)).astype(bf16)
        dms = (head_wide(w) * dn_e).astype(bf16)
        dqe = (ss * xg[:, at].astype(f32)).astype(bf16)
        gather_back(c + 1)
        for r, sl in blocks_of(c, wide):
            dkve_buf[0:D, sl] = nn(bda[r], dka[:, sl]).astype(bf16)
            dkve_buf[D:, sl] = nn(bdm[r], dms[:, sl]).astype(bf16)
        for r, sl in blocks_of(c, wide):
            at_k = pl.ds(pl.multiple_of(c * EC + sl.start, SUB), wide)
            gak = nt(kve[0:D, at_k], dka[:, sl])
            gmk = nt(kve[D:, at_k], dms[:, sl])
            ga[r, 0:128] += gak[0:128, 0:128]
            ga[r, 128:] += gak[128:, 128:]
            gm[r, 0:128] += gmk[0:128, 0:128]
            gm[r, 128:] += gmk[128:, 128:]
            dmu[r] += sum(dsr[:, k:k + 128] for k in range(sl.start, sl.stop, 128))
        dqkv[:, :D] += nt(one_hot_rows(row(c, TARGET), N), dqe)
        return 0

    gather_back(0)
    lax.fori_loop(0, whole, functools.partial(backward, 2 * SUB), 0)
    lax.fori_loop(whole, chunks, functools.partial(backward, SUB), 0)
    scatter_back(chunks - 1)

    low[...] = dqkv[...].astype(bf16)
    last = pltpu.make_async_copy(low, dqkv_ref, osem.at[2])
    last.start()
    finish.append(last)
    dt = dtkv[...].astype(bf16)
    drte = jnp.zeros((D, 256), f32)
    for s in range(TYPES):
        drte = drte + nt(lay.get_type(wpk, s, D, 3 * D), dt[s * 256:(s + 1) * 256, :])

    def put_edge(c0, value):
        for f in range(lay.blocks):
            gpack[f * lay.part + lay.trows:(f + 1) * lay.part, c0:c0 + value.shape[1]] = value[
                f * lay.erows:(f + 1) * lay.erows
            ].astype(bf16)

    for p in range(4):
        acc = jnp.zeros((D, 128), f32)
        for g in range(4):
            r, m = 2 * p + g // 2, g % 2
            t = jnp.where(on_diag, (gm if m else ga)[r], 0.0)
            rolled = [t if k == 0 else pltpu.roll(t, 32 * k, 1) for k in range(4)]
            acc = acc + jnp.concatenate([rolled[(g - h % 4) % 4][h * 32:(h + 1) * 32] for h in range(H)], axis=0)
        put_edge(p * 128, acc)
    embt = nt(ident, emb_ref[...]).astype(bf16)
    put_edge(512, nt(embt, drte.astype(bf16)))

    lane8 = lax.broadcasted_iota(jnp.int32, (8, 256), 1)
    line8 = lax.broadcasted_iota(jnp.int32, (8, 256), 0)
    mixg = jnp.where(lane8 == REL * H + line8, gskip[:, 0:1], 0.0)
    for r in range(REL):
        col = jnp.sum(dmu[r], axis=1, keepdims=True) * score_scale
        mixg = mixg + jnp.where(lane8 == r * H + line8, col, 0.0)
    mixg = jnp.broadcast_to(jnp.sum(mixg, axis=0, keepdims=True), (8, 256))
    for f in range(lay.blocks):
        corner = jnp.concatenate(
            [gnorm[:, f * lay.wide:(f + 1) * lay.wide], jnp.zeros((8, 256 - lay.wide), f32)], axis=1
        )
        small = jnp.concatenate([corner, mixg, jnp.zeros((lay.erows - 16, 256), f32)], axis=0)
        gpack[f * lay.part + lay.trows:(f + 1) * lay.part, 768:] = small.astype(bf16)

    done = 0
    for s in range(TYPES):
        g = nn(xcat[s * D:(s + 1) * D, :], low[...])
        g_kv = g[:, D:] + nn(rte[...], dt[s * 256:(s + 1) * 256, :])
        value = jnp.concatenate([g[:, :D], g_kv, gout[s * D:(s + 1) * D, :]], axis=1).astype(bf16)
        for _, a, b, c, d in lay.type_rows(s):
            gpack[a:b, :] = value[c:d]
        while done < lay.blocks and (done + 1) * lay.trows <= (s + 1) * D:
            m = jnp.bitwise_xor(me, done)
            for i, (ref, side) in enumerate(((send_ref, 1 - core), (keep_ref, core))):
                at = pl.ds(pl.multiple_of(done * lay.part + side * lay.half, 16), lay.half)
                for j in range(GROUP):
                    copy = pltpu.make_async_copy(
                        gpack.at[at, pl.ds(j * WIDE, WIDE)], ref.at[m, jnp.bitwise_xor(zi, j)],
                        gsem.at[(2 * done + i) * GROUP + j],
                    )
                    copy.start()
                    finish.append(copy)
            done += 1
    for copy in finish:
        copy.wait()


def emb_table():
    steps = np.arange(TB, dtype=np.float32)[:, None]
    col = np.arange(D)
    freq = np.exp(-np.log(np.float32(10000.0)) * (2 * (col // 2)).astype(np.float32) / np.float32(D)).astype(np.float32)
    angle = steps * freq[None]
    tab = np.where(col[None] % 2 == 0, np.sin(angle), np.cos(angle)).astype(np.float32)
    return np.concatenate([tab, np.zeros((256 - TB, D), np.float32)], axis=0)


def layer(lay, live, cnt, kinds, mix, idx, cot, feat, own, near, far, xg):
    sums = S((lay.blocks, GROUP, lay.half, WIDE), bf16)
    edges = lambda rows, kind: V((rows, EDGES), kind)
    return pl.pallas_call(
        functools.partial(layer_kernel, lay),
        out_shape=[S((N, D), bf16), S((N, 3 * D), bf16), S((D, N), f32), sums, sums],
        in_specs=[SMEM, SMEM] + [VMEM] * 4 + [ANY] * (2 * lay.blocks + 2),
        out_specs=[ANY] * 5,
        scratch_shapes=LISTS + [
            V((lay.blocks * lay.part, 1024), bf16), V((lay.blocks * lay.part, 1024), bf16), V((TYPES * D, D), f32),
            V((8, D), f32), V((8, 128), f32), edges(D, bf16), V((N, D), bf16), V((N, 3 * D), bf16), V((N, D), bf16), V((N, D), bf16),
            V((4 * D, TYPES * D), bf16), V((TYPES * D, N), bf16), V((D, N), bf16), V((D, 256), bf16),
            V((D + 16, EC), f32), V((2 * D, EC), bf16), V((REL, H, 128), f32),
            V((8, D, D), bf16), V((8, D, D), bf16), V((8, D, D), bf16), V((8, D, D), bf16),
            V((8, D, 128), f32), V((8, D, 128), f32), V((8, 8, 128), f32),
            edges(2 * D, bf16), edges(D, bf16), V((D, REL * SLOTS), bf16),
            V((H, REL * SLOTS), f32), V((H, REL * SLOTS), f32),
            V((D + 16, N), f32), V((D + 16, N), bf16), V((N, 3 * D), f32), V((TYPES * 256, 2 * D), f32), V((D, N), f32),
            pltpu.SemaphoreType.DMA((2 * lay.blocks - 1,)), pltpu.SemaphoreType.DMA((3,)),
            pltpu.SemaphoreType.DMA((3,)), pltpu.SemaphoreType.DMA((2 * lay.blocks * GROUP,)),
        ],
        compiler_params=pltpu.CompilerParams(vmem_limit_bytes=LAYER_VMEM),
        cost_estimate=pl.CostEstimate(flops=60 * 10**9, bytes_accessed=16 * MIB, transcendentals=0),
        name="layer",
    )(live, cnt, kinds, mix, idx, jnp.asarray(emb_table(), bf16), cot, feat, own, *near, *far, xg)


def input_kernel(lay, *refs):
    nb = lay.blocks - 1
    kinds_ref, dqkv_ref, skp_ref, own_ref = refs[:4]
    near, far = refs[4:4 + nb], refs[4 + nb:4 + 2 * nb]
    out_ref, wpk, sems = refs[4 + 2 * nb:]
    me, core, _ = position()
    weights = lay.weight_copies(me, core, own_ref, near, far, wpk, sems)
    for copy in weights:
        copy.start()
    masks = (lax.broadcasted_iota(jnp.int32, (8, N), 0) == kinds_ref[...]).astype(f32)
    for copy in weights:
        copy.wait()
    for c in range(N // NC):
        at = slice(c * NC, (c + 1) * NC)
        proj = pick(masks[:, at], [nt(lay.get_type(wpk, s, 0, 3 * D), dqkv_ref[at, :]) for s in range(TYPES)])
        out_ref[at, :] = (proj + skp_ref[:, at]).T.astype(bf16)


def input_gradient(lay, kinds, dqkv, skp, own, near, far):
    return pl.pallas_call(
        functools.partial(input_kernel, lay),
        out_shape=S((N, D), bf16),
        in_specs=[VMEM] * 3 + [ANY] * (2 * lay.blocks - 1),
        scratch_shapes=[V((lay.blocks * lay.part, 1024), bf16), pltpu.SemaphoreType.DMA((2 * lay.blocks - 1,))],
        compiler_params=pltpu.CompilerParams(vmem_limit_bytes=63 * MIB),
        cost_estimate=pl.CostEstimate(flops=2 * N * D * D * 12, bytes_accessed=6 * MIB, transcendentals=0),
        name="input_gradient",
    )(kinds, dqkv, skp, own, *near, *far)


def tree(terms):
    while len(terms) > 1:
        terms = [terms[i] + terms[i + 1] for i in range(0, len(terms), 2)]
    return terms[0]


def add_core_kernel(blocks, keep_ref, got_ref, *refs):
    outs, keep, got, isem, osem = refs[:blocks - 1], *refs[blocks - 1:]
    loads = []
    for m in range(1, blocks):
        pair = [
            pltpu.make_async_copy(keep_ref.at[m], keep.at[m - 1], isem.at[2 * m - 2]),
            pltpu.make_async_copy(got_ref.at[m], got.at[m - 1], isem.at[2 * m - 1]),
        ]
        for copy in pair:
            copy.start()
        loads.append(pair)
    stores = []
    for m in range(1, blocks):
        for copy in loads[m - 1]:
            copy.wait()
        keep[m - 1] = (keep[m - 1].astype(f32) + got[m - 1].astype(f32)).astype(bf16)
        store = pltpu.make_async_copy(keep.at[m - 1], outs[m - 1], osem.at[m - 1])
        store.start()
        stores.append(store)
    for copy in stores:
        copy.wait()


def add_core(blocks, keep, got):
    buf = V((blocks - 1, *keep.shape[1:]), bf16)
    return pl.pallas_call(
        functools.partial(add_core_kernel, blocks),
        out_shape=[S(keep.shape[1:], bf16)] * (blocks - 1),
        in_specs=[ANY, ANY],
        out_specs=[ANY] * (blocks - 1),
        scratch_shapes=[
            buf, buf, pltpu.SemaphoreType.DMA((2 * blocks - 2,)), pltpu.SemaphoreType.DMA((blocks - 1,)),
        ],
        compiler_params=pltpu.CompilerParams(vmem_limit_bytes=63 * MIB),
        name="add_core",
    )(keep, got)


def summed(terms):
    return tree([x.astype(f32) for x in terms]).astype(bf16)


def adam(param, first, second, avg, grad, rate):
    first_new = beta_one * first + (1.0 - beta_one) * grad
    second_new = beta_two * second + (1.0 - beta_two) * grad * grad
    first_hat = first_new / (1.0 - beta_one**STEP)
    second_hat = second_new / (1.0 - beta_two**STEP)
    param_new = param - rate * (first_hat / (jnp.sqrt(second_hat) + adam_eps) + decay_rate * param)
    avg_new = ema_keep * avg + (1.0 - ema_keep) * param_new
    return (param_new, first_new, second_new, avg_new)


def update_kernel(jobs, count, *refs):
    pieces, refs = refs[:2 * GROUP], refs[2 * GROUP:]
    states, outs, refs = refs[:count], refs[count:2 * count], refs[2 * count:]
    gsum, bufs, news, isem, osem = refs[0], refs[1:1 + 4 * len(jobs)], refs[1 + 4 * len(jobs):-2], refs[-2], refs[-1]

    def view(ref, row, rows):
        return ref if rows == ref.shape[0] else ref.at[pl.ds(row, rows)]

    loads = [
        pltpu.make_async_copy(view(states[4 * job[0] + j], job[1], job[2]), bufs[4 * i + j], isem.at[4 * i + j])
        for i, job in enumerate(jobs) for j in range(4)
    ]
    for copy in loads:
        copy.start()
    _, core, zi = position()
    zi = lax.rem(zi, GROUP)
    high = gsum.shape[0] // 2
    for side in range(2):
        at = pl.ds(pl.multiple_of(jnp.bitwise_xor(core, side) * high, 16), high)
        for k in range(GROUP):
            want = jnp.bitwise_xor(zi, k)
            for j in range(GROUP):
                @pl.when(want == j)
                def _():
                    gsum[at, j * WIDE:(j + 1) * WIDE] = pieces[side * GROUP + k][...]
    stores = []
    for i, (group, row, rows, lanes, first, lane, rate) in enumerate(jobs):
        base = first // 16 * 16
        grad = gsum[base:base + max(16, rows), lane:lane + max(lanes, 128)].astype(f32)
        grad = grad[first - base:first - base + rows, :lanes]
        for j in range(4):
            loads[4 * i + j].wait()
        new = adam(*[bufs[4 * i + j][...] for j in range(4)], grad, rate)
        for j in range(4):
            news[4 * i + j][...] = new[j]
            copy = pltpu.make_async_copy(news[4 * i + j], view(outs[4 * group + j], row, rows), osem.at[4 * i + j])
            copy.start()
            stores.append(copy)
    for copy in stores:
        copy.wait()


def update(jobs, pieces, sets):
    states = [x for group in sets for x in group]
    bufs = [V((job[2], job[3]), f32) for job in jobs for _ in range(4)]
    return pl.pallas_call(
        functools.partial(update_kernel, jobs, len(states)),
        out_shape=[S(x.shape, f32) for x in states],
        in_specs=[VMEM] * len(pieces) + [ANY] * len(states),
        out_specs=[ANY] * len(states),
        scratch_shapes=[V((2 * pieces[0].shape[0], 1024), bf16)] + bufs + bufs
        + [pltpu.SemaphoreType.DMA((len(bufs),))] * 2,
        compiler_params=pltpu.CompilerParams(vmem_limit_bytes=63 * MIB),
        name="update",
    )(*pieces, *states)


def shards(dp, fsdp, *args):
    (
        node_feat, out_cot, node_type, node_count, edge_src, edge_dst, edge_time, edge_count,
        type_weight, type_first, type_second, type_avg,
        edge_weight, edge_first, edge_second, edge_avg,
        norm_params, norm_first, norm_second, norm_avg,
        mix_params, mix_first, mix_second, mix_avg,
    ) = args
    lines = dp // 2
    lay = Layout(fsdp)

    def swap(x, axis, mask):
        size = dp if axis == "dp" else fsdp
        return lax.ppermute(x, axis, [(i, i ^ mask) for i in range(size)])

    mine = pack_half(lay, type_weight, edge_weight, norm_params)
    near = [swap(mine, "fsdp", m) for m in range(1, fsdp)]
    kinds = node_type.reshape(1, N)
    own = pack(lay, type_weight, edge_weight, norm_params)
    idx, xg = before(edge_count, kinds, edge_src, edge_dst, edge_time, node_feat)
    own, idx, xg, near[0] = lax.optimization_barrier((own, idx, xg, near[0]))
    far = [swap(x, "dp", 1) for x in near]
    mixes = [x.reshape(1, 68) for x in (mix_params, mix_first, mix_second, mix_avg)]
    layer_out, dqkv, skp, keep, send = layer(
        lay, node_count, edge_count, kinds, mixes[0], idx, out_cot, node_feat,
        own, near, far, xg,
    )
    got = swap(send, "dp", 1)
    chip = add_core(fsdp, keep, got)
    parts = [summed([keep[0], got[0]])] + [swap(chip[m - 1], "fsdp", m) for m in range(1, fsdp)]
    input_grad = input_gradient(lay, kinds, dqkv, skp, own, near, far)
    input_grad, *parts = lax.optimization_barrier((input_grad, *parts))
    pieces = [summed([x[k] for x in parts]) for k in range(GROUP)]
    total = summed([pieces[0]] + [swap(pieces[k], "dp", 2 * k) for k in range(1, GROUP)])
    step = GROUP
    while step < lines:
        total = summed([total, swap(total, "dp", 2 * step)])
        step *= 2
    totals = [total] + [swap(total, "dp", 2 * k) for k in range(1, GROUP)]
    totals = totals + [swap(x, "dp", 1) for x in totals]
    trows, erows = lay.trows, lay.erows
    jobs = [(0, row, erows, 1024, row, 0, rates[0]) for row in range(0, trows, erows)] + [
        (1, 0, erows, 768, trows, 0, rates[1]), (2, 0, 8, lay.wide, trows, 768, rates[2]),
        (3, 0, 1, 68, trows + 8, 768, rates[3]),
    ]
    new = update(jobs, totals, [
        [type_weight, type_first, type_second, type_avg], [edge_weight, edge_first, edge_second, edge_avg],
        [norm_params, norm_first, norm_second, norm_avg], mixes,
    ])
    return (layer_out, input_grad, *new[:12], *[x.reshape(68) for x in new[12:]])


def solution(mesh):
    whole = P(("dp", "fsdp"), None)
    flat = P(("dp", "fsdp"))
    state = [P("fsdp", None)] * 8 + [P(None, "fsdp")] * 4 + [P()] * 4
    return jax.shard_map(
        functools.partial(shards, mesh.shape["dp"], mesh.shape["fsdp"]),
        mesh=mesh,
        in_specs=tuple([whole, whole, flat, flat, whole, whole, whole, flat] + state),
        out_specs=tuple([whole, whole] + state),
        check_vma=False,
    )
```

time: 186 us -> 152 us (0.82); the launches traced: 188 us -> 150 us
  starting transfers between devices: 53.6 us -> 28.7 us
  Pallas kernels: 66.3 us -> 88.7 us
  local copies, waits for them, and re-layouts: 20 us -> 1.36 us
  other arithmetic: 10.3 us -> 1.36 us
  waiting for transfers between devices: 36.2 us -> 28.3 us
    ppermute x20, starting transfers between devices: 53.6 us -> 28.7 us  [swap(): return lax.ppermute(x, axis, [(i, i ^ mask) for i in range(size)])]
    pallas_call x5 -> x7, Pallas kernels: 66.3 us -> 88.7 us  [the longest x1 60.8 us: layer(): pl.pallas_call(functools.partial(layer_kernel, lay), out_shape=[S((N, D),...]
    unnamed x48 -> x28, local copies, waits for them, and re-layouts: 9.9 us -> 1.36 us
    ppermute x20, waiting for transfers between devices: 36.2 us -> 28.3 us  [swap(): return lax.ppermute(x, axis, [(i, i ^ mask) for i in range(size)])]
    concatenate x13 -> x0, other arithmetic: 6.81 us -> none  [the longest x8 4.41 us: wide_mix(): return jnp.concatenate([mu, skip], axis=0)]
    reshape x8 -> x0, local copies, waits for them, and re-layouts: 5.03 us -> none  [the longest x4 4.72 us: wide_mix(): mu = jnp.pad(mix[:64].reshape(8, 8), ((0, 0), (0, 120)))]
    slice x11 -> x0, local copies, waits for them, and re-layouts: 4.29 us -> none  [the longest x4 3.41 us: wide_mix(): skip = jnp.pad(jnp.broadcast_to(mix[64:, None], (4, 128)), ((0, 4), (0, 0)))]
    another operation x4 -> x0, other arithmetic: 3.52 us -> none
  transfers between devices with their start and end apart: 20 -> 20, of which waited for: 11 -> 13; matrix products, arithmetic and copies ran while one was open for 7% -> 1% of each run, Pallas kernels for 0% -> 12%
where the time goes in v2:
time: 152 us; the launch traced here: 150 us
  Pallas kernels  88.7 us (58%)
  starting transfers between devices  28.7 us (19%)
  waiting for transfers between devices  28.3 us (19%)
  between operations  1.65 us (1%)
    pallas_call x1, Pallas kernels, layer(): pl.pallas_call(functools.partial(layer_kernel, lay), out_shape=[S((N, D),...  60.8 us
    ppermute x20, starting transfers between devices, swap(): return lax.ppermute(x, axis, [(i, i ^ mask) for i in range(size)])  28.7 us
    ppermute x20, waiting for transfers between devices, swap(): return lax.ppermute(x, axis, [(i, i ^ mask) for i in range(size)])  28.3 us
    pallas_call x1, Pallas kernels, before(): pl.pallas_call(before_kernel, out_shape=(S((EDGES // EC * 8, EC), jnp.int...  9.3 us
    pallas_call x1, Pallas kernels, input_gradient(): pl.pallas_call(functools.partial(input_kernel, lay), out_shape=S((N, D),...  6.13 us
    pallas_call x1, Pallas kernels, update(): pl.pallas_call(functools.partial(update_kernel, jobs, len(states)), out_s...  5.32 us
  transfers between devices with their start and end apart: 20, of which 13 were waited for; matrix products, arithmetic and copies ran while one was open for 1% of the time, Pallas kernels for 12%

profile of v2, /device:TPU:0, one launch (start us, length us, event | category | flops | bytes accessed | tf_op | source)
XLA Modules:
  0.0 150.1 jit_solution(3527994032678337083)
XLA Ops:
  0.7 2.5 %pack_half.1 = bf16[160,1024]{1,0:T(8,128)(2,1)} custom-call(f32[256,1024]{1,0:T(8,128)} %refs_8_.1, f32[64,768]{1,0:T(8,128)} %refs_12_.1, f32[8,64]{1,0:T(8,128)} %refs_16_.1), custom_call_target="tpu_custom_call" | custom-call | tf_op jit(solution)/shard_map/pack_half/pallas_call | solution.py:193
  3.2 4.0 %collective-permute-start.2 = (bf16[160,1024]{1,0:T(8,128)(2,1)}, bf16[160,1024]{1,0:T(8,128)(2,1)S(1)}, u32[]{:S(2)}, u32[]{:S(2)}) collective-permute-start(bf16[160,1024]{1,0:T(8,128)(2,1)} %pack_half.1), channel_id=1, source_target_pairs={{0,3},{1,2},{2,1},{3,0},{4,7},{5,6},{6,5},{7,4},{8,11},{9,10},{10,... | collective-permute-start | bytes 983048 | tf_op jit(solution)/shard_map/ppermute | solution.py:755
  7.2 0.5 collective-permute-start.1
  7.7 0.1 collective-permute-start
  7.8 2.2 %pack.1.refs_8_.refs_3_ = bf16[320,1024]{1,0:T(8,128)(2,1)} custom-call(f32[256,1024]{1,0:T(8,128)} %refs_8_.1, f32[64,768]{1,0:T(8,128)} %refs_12_.1, f32[8,64]{1,0:T(8,128)} %refs_16_.1), custom_call_target="tpu_custom_call" | custom-call | tf_op jit(solution)/shard_map/pack/pallas_call | solution.py:211
  10.1 9.3 %before.1 = (s32[136,512]{1,0:T(8,128)}, bf16[256,8704]{1,0:T(8,128)(2,1)}) custom-call(s32[8]{0:T(128)} %refs_1_.1, s32[1,1024]{1,0:T(1,128)} %bitcast.27, s32[8,1024]{1,0:T(8,128)} %src_ref.1, s32[8,1024]{1,0:T(8,128)} %dst_ref.1, s32[8,1024]{1,0:T(8,128)} %tim_ref.1, bf16[1024,256]{1,0:T(8,128)(2,1)} %refs_7_.1), custom_call_target="tpu_custom_call" | custom-call | flops 4563402752 | bytes 6291456 | tf_op jit(solution)/shard_map/before/pallas_call | solution.py:245
  19.4 3.0 %collective-permute-done.refs_9_.refs_4_ = bf16[160,1024]{1,0:T(8,128)(2,1)S(1)} collective-permute-done((bf16[160,1024]{1,0:T(8,128)(2,1)}, bf16[160,1024]{1,0:T(8,128)(2,1)S(1)}, u32[]{:S(2)}, u32[]{:S(2)}) %collective-permute-start) | collective-permute-done | bytes 327712 | tf_op jit(solution)/shard_map/ppermute | solution.py:755
  22.4 0.1 collective-permute-start.5
  22.5 0.0 copy-start.9
  22.5 0.5 collective-permute-start.4
  23.0 0.1 collective-permute-start.3
  23.7 0.4 collective-permute-done.5.refs_14_.refs_9_
  24.1 0.5 collective-permute-done.4.refs_13_.refs_8_
  24.5 0.5 collective-permute-done.3.refs_12_.refs_7_
  25.0 0.2 copy-done.12
  25.3 0.4 copy-done.13
  25.7 60.8 %layer.1 = (bf16[1024,256]{1,0:T(8,128)(2,1)}, bf16[1024,768]{1,0:T(8,128)(2,1)}, f32[256,1024]{1,0:T(8,128)}, bf16[4,4,160,256]{3,2,1,0:T(8,128)(2,1)}, bf16[4,4,160,256]{3,2,1,0:T(8,128)(2,1)}) custom-call(s32[1]{0:T(128)S(6)} %copy.43.refs_0_, s32[8]{0:T(128)} %refs_1_.1, s32[1,1024]{1,0:T(1,128)} %bitcast.28, f32[1,68]{1,0:T(1,128)} %bitcast.22, ...), custom_call_target="tpu_custom_call" | custom-call | flops 60000002048 | bytes 16777216 | tf_op jit(solution)/shard_map/layer/pallas_call | solution.py:573
  86.6 0.1 collective-permute-start.6
  86.6 3.4 %collective-permute-done.6.got_ref = bf16[4,4,160,256]{3,2,1,0:T(8,128)(2,1)} collective-permute-done((bf16[4,4,160,256]{3,2,1,0:T(8,128)(2,1)}, bf16[4,4,160,256]{3,2,1,0:T(8,128)(2,1)}, u32[]{:S(2)}, u32[]{:S(2)}) %collective-permute-start.6) | collective-permute-done | bytes 1310752 | tf_op jit(solution)/shard_map/ppermute | solution.py:755
  90.0 2.4 %add_core.1 = (bf16[4,160,256]{2,1,0:T(8,128)(2,1)}, bf16[4,160,256]{2,1,0:T(8,128)(2,1)}, bf16[4,160,256]{2,1,0:T(8,128)(2,1)}) custom-call(bf16[4,4,160,256]{3,2,1,0:T(8,128)(2,1)} %get-tuple-element.62.keep_ref, bf16[4,4,160,256]{3,2,1,0:T(8,128)(2,1)} %collective-permute-done.6.got_ref), custom_call_target="tpu_custom_call" | custom-call | tf_op jit(solution)/shard_map/add_core/pallas_call | solution.py:658
  92.4 0.1 collective-permute-start.7
  92.5 9.0 %collective-permute-start.8 = (bf16[4,160,256]{2,1,0:T(8,128)(2,1)}, bf16[4,160,256]{2,1,0:T(8,128)(2,1)S(1)}, u32[]{:S(2)}, u32[]{:S(2)}) collective-permute-start(bf16[4,160,256]{2,1,0:T(8,128)(2,1)} %get-tuple-element.65), channel_id=1, source_target_pairs={{0,2},{1,3},{2,0},{3,1},{4,6},{5,7},{6,4},{7,5},{8,10},{9,11},{10,... | collective-permute-start | bytes 983048 | tf_op jit(solution)/shard_map/ppermute | solution.py:755
  101.4 1.4 collective-permute-start.9
  102.8 6.1 %input_gradient.1 = bf16[1024,256]{1,0:T(8,128)(2,1)} custom-call(s32[1,1024]{1,0:T(1,128)} %bitcast.29, bf16[1024,768]{1,0:T(8,128)(2,1)} %get-tuple-element.60.refs_1_, f32[256,1024]{1,0:T(8,128)} %get-tuple-element.61.refs_2_, bf16[320,1024]{1,0:T(8,128)(2,1)} %pack.1.refs_8_.refs_3_, bf16[160,1024]{1,0:T(8,128)(2,1)} %copy-done.10, ...), custom_call_target="tpu_custom_call" | custom-call | flops 1610612736 | bytes 6291456 | tf_op jit(solution)/shard_map/input_gradient/pallas_call | solution.py:616
  108.9 1.2 fusion
  110.1 5.9 %collective-permute-done.8 = bf16[4,160,256]{2,1,0:T(8,128)(2,1)S(1)} collective-permute-done((bf16[4,160,256]{2,1,0:T(8,128)(2,1)}, bf16[4,160,256]{2,1,0:T(8,128)(2,1)S(1)}, u32[]{:S(2)}, u32[]{:S(2)}) %collective-permute-start.8) | collective-permute-done | bytes 327712 | tf_op jit(solution)/shard_map/ppermute | solution.py:755
  116.0 1.7 %collective-permute-done.9 = bf16[4,160,256]{2,1,0:T(8,128)(2,1)S(1)} collective-permute-done((bf16[4,160,256]{2,1,0:T(8,128)(2,1)}, bf16[4,160,256]{2,1,0:T(8,128)(2,1)S(1)}, u32[]{:S(2)}, u32[]{:S(2)}) %collective-permute-start.9) | collective-permute-done | bytes 327712 | tf_op jit(solution)/shard_map/ppermute | solution.py:755
  117.8 0.1 fusion.4
  117.9 0.1 collective-permute-start.10
  118.0 7.8 %collective-permute-start.12 = (bf16[160,256]{1,0:T(8,128)(2,1)S(1)}, bf16[160,256]{1,0:T(8,128)(2,1)S(1)}, u32[]{:S(2)}, u32[]{:S(2)}) collective-permute-start(bf16[160,256]{1,0:T(8,128)(2,1)S(1)} %get-tuple-element.89), channel_id=1, source_target_pairs={{0,24},{4,28},{8,16},{12,20},{16,8},{20,12},{24,0},{28,4},{1,25},{... | collective-permute-start | bytes 245768 | tf_op jit(solution)/shard_map/ppermute | solution.py:755
  125.8 0.1 collective-permute-start.11
  125.9 0.0 collective-permute-done.10
  125.9 4.4 %collective-permute-done.12 = bf16[160,256]{1,0:T(8,128)(2,1)S(1)} collective-permute-done((bf16[160,256]{1,0:T(8,128)(2,1)S(1)}, bf16[160,256]{1,0:T(8,128)(2,1)S(1)}, u32[]{:S(2)}, u32[]{:S(2)}) %collective-permute-start.12) | collective-permute-done | bytes 81952 | tf_op jit(solution)/shard_map/ppermute | solution.py:755
  130.3 2.7 %collective-permute-done.11 = bf16[160,256]{1,0:T(8,128)(2,1)S(1)} collective-permute-done((bf16[160,256]{1,0:T(8,128)(2,1)S(1)}, bf16[160,256]{1,0:T(8,128)(2,1)S(1)}, u32[]{:S(2)}, u32[]{:S(2)}) %collective-permute-start.11) | collective-permute-done | bytes 81952 | tf_op jit(solution)/shard_map/ppermute | solution.py:755
  132.9 0.1 fusion.2.refs_0_
  133.0 2.6 %collective-permute-start.15 = (bf16[160,256]{1,0:T(8,128)(2,1)S(1)}, bf16[160,256]{1,0:T(8,128)(2,1)S(1)}, u32[]{:S(2)}, u32[]{:S(2)}) collective-permute-start(bf16[160,256]{1,0:T(8,128)(2,1)S(1)} %fusion.2.refs_0_), channel_id=1, source_target_pairs={{0,24},{4,28},{8,16},{12,20},{16,8},{20,12},{24,0},{28,4},{1,25},{... | collective-permute-start | bytes 245768 | tf_op jit(solution)/shard_map/ppermute | solution.py:755
  135.6 0.0 collective-permute-start.14
  135.6 1.8 %collective-permute-start.13 = (bf16[160,256]{1,0:T(8,128)(2,1)S(1)}, bf16[160,256]{1,0:T(8,128)(2,1)S(1)}, u32[]{:S(2)}, u32[]{:S(2)}) collective-permute-start(bf16[160,256]{1,0:T(8,128)(2,1)S(1)} %fusion.2.refs_0_), channel_id=1, source_target_pairs={{0,8},{4,12},{8,0},{12,4},{16,24},{20,28},{24,16},{28,20},{1,9},{5... | collective-permute-start | bytes 245768 | tf_op jit(solution)/shard_map/ppermute | solution.py:755
  137.5 0.0 collective-permute-start.16
  137.5 2.8 %collective-permute-done.15.refs_3_ = bf16[160,256]{1,0:T(8,128)(2,1)S(1)} collective-permute-done((bf16[160,256]{1,0:T(8,128)(2,1)S(1)}, bf16[160,256]{1,0:T(8,128)(2,1)S(1)}, u32[]{:S(2)}, u32[]{:S(2)}) %collective-permute-start.15) | collective-permute-done | bytes 81952 | tf_op jit(solution)/shard_map/ppermute | solution.py:755
  140.3 0.0 collective-permute-start.19
  140.3 2.2 %collective-permute-done.14.refs_2_ = bf16[160,256]{1,0:T(8,128)(2,1)S(1)} collective-permute-done((bf16[160,256]{1,0:T(8,128)(2,1)S(1)}, bf16[160,256]{1,0:T(8,128)(2,1)S(1)}, u32[]{:S(2)}, u32[]{:S(2)}) %collective-permute-start.14) | collective-permute-done | bytes 81952 | tf_op jit(solution)/shard_map/ppermute | solution.py:755
  142.5 0.5 collective-permute-start.17
  143.1 0.7 collective-permute-done.18.refs_6_
  143.8 0.2 collective-permute-done.17.refs_5_
  144.0 0.4 copy-done.6
  144.4 0.2 copy-done.7
  144.6 5.3 %update.1 = (f32[256,1024]{1,0:T(8,128)}, f32[256,1024]{1,0:T(8,128)}, f32[256,1024]{1,0:T(8,128)}, f32[256,1024]{1,0:T(8,128)}, f32[64,768]{1,0:T(8,128)}, /*in...) custom-call(bf16[160,256]{1,0:T(8,128)(2,1)} %copy-done, ...), custom_call_target="tpu_custom_call" | custom-call | tf_op jit(solution)/shard_map/update/pallas_call | solution.py:730
  (30 shorter events, 0.1 us)
Async XLA Ops:
  3.2 19.2 %collective-permute-start.2 = (bf16[160,1024]{1,0:T(8,128)(2,1)}, bf16[160,1024]{1,0:T(8,128)(2,1)S(1)}, u32[]{:S(2)}, u32[]{:S(2)}) collective-permute-start(bf16[160,1024]{1,0:T(8,128)(2,1)} %pack_half.1), channel_id=1, source_target_pairs={{0,3},{1,2},{2,1},{3,0},{4,7},{5,6},{6,5},{7,4},{8,11},{9,10},{10,... | collective-permute-start | bytes 983048 | tf_op jit(solution)/shard_map/ppermute | solution.py:755
  7.2 15.3 %collective-permute-start.1 = (bf16[160,1024]{1,0:T(8,128)(2,1)}, bf16[160,1024]{1,0:T(8,128)(2,1)S(1)}, u32[]{:S(2)}, u32[]{:S(2)}) collective-permute-start(bf16[160,1024]{1,0:T(8,128)(2,1)} %pack_half.1), channel_id=1, source_target_pairs={{0,2},{1,3},{2,0},{3,1},{4,6},{5,7},{6,4},{7,5},{8,10},{9,11},{10,... | collective-permute-start | bytes 983048 | tf_op jit(solution)/shard_map/ppermute | solution.py:755
  7.7 14.7 %collective-permute-start = (bf16[160,1024]{1,0:T(8,128)(2,1)}, bf16[160,1024]{1,0:T(8,128)(2,1)S(1)}, u32[]{:S(2)}, u32[]{:S(2)}) collective-permute-start(bf16[160,1024]{1,0:T(8,128)(2,1)} %pack_half.1), channel_id=1, source_target_pairs={{0,1},{1,0},{2,3},{3,2},{4,5},{5,4},{6,7},{7,6},{8,9},{9,8},{10,11... | collective-permute-start | bytes 983048 | tf_op jit(solution)/shard_map/ppermute | solution.py:755
  22.4 2.6 %copy-start.10 = (bf16[160,1024]{1,0:T(8,128)(2,1)}, bf16[160,1024]{1,0:T(8,128)(2,1)S(1)}, u32[]{:S(2)}) copy-start(bf16[160,1024]{1,0:T(8,128)(2,1)S(1)} %collective-permute-done.refs_9_.refs_4_) | copy-start | bytes 983044
  22.4 2.6 %copy-start.8 = (bf16[160,1024]{1,0:T(8,128)(2,1)}, bf16[160,1024]{1,0:T(8,128)(2,1)S(1)}, u32[]{:S(2)}) copy-start(bf16[160,1024]{1,0:T(8,128)(2,1)S(1)} %collective-permute-done.2.refs_11_.refs_6_) | copy-start | bytes 983044
  22.4 1.7 %collective-permute-start.5 = (bf16[160,1024]{1,0:T(8,128)(2,1)S(1)}, bf16[160,1024]{1,0:T(8,128)(2,1)S(1)}, u32[]{:S(2)}, u32[]{:S(2)}) collective-permute-start(bf16[160,1024]{1,0:T(8,128)(2,1)S(1)} %collective-permute-done.2.refs_11_.refs_6_), channel_id=1, source_target_pairs={{0,4},{4,0},{8,12},{12,8},{16,20},{20,16},{24,28},{28,24},{1,5},{5... | collective-permute-start | bytes 983048 | tf_op jit(solution)/shard_map/ppermute | solution.py:755
  22.5 2.6 %copy-start.9 = (bf16[160,1024]{1,0:T(8,128)(2,1)}, bf16[160,1024]{1,0:T(8,128)(2,1)S(1)}, u32[]{:S(2)}) copy-start(bf16[160,1024]{1,0:T(8,128)(2,1)S(1)} %collective-permute-done.1.refs_10_.refs_5_) | copy-start | bytes 983044
  22.5 2.1 %collective-permute-start.4 = (bf16[160,1024]{1,0:T(8,128)(2,1)S(1)}, bf16[160,1024]{1,0:T(8,128)(2,1)S(1)}, u32[]{:S(2)}, u32[]{:S(2)}) collective-permute-start(bf16[160,1024]{1,0:T(8,128)(2,1)S(1)} %collective-permute-done.1.refs_10_.refs_5_), channel_id=1, source_target_pairs={{0,4},{4,0},{8,12},{12,8},{16,20},{20,16},{24,28},{28,24},{1,5},{5... | collective-permute-start | bytes 983048 | tf_op jit(solution)/shard_map/ppermute | solution.py:755
  23.0 2.0 %collective-permute-start.3 = (bf16[160,1024]{1,0:T(8,128)(2,1)S(1)}, bf16[160,1024]{1,0:T(8,128)(2,1)S(1)}, u32[]{:S(2)}, u32[]{:S(2)}) collective-permute-start(bf16[160,1024]{1,0:T(8,128)(2,1)S(1)} %collective-permute-done.refs_9_.refs_4_), channel_id=1, source_target_pairs={{0,4},{4,0},{8,12},{12,8},{16,20},{20,16},{24,28},{28,24},{1,5},{5... | collective-permute-start | bytes 983048 | tf_op jit(solution)/shard_map/ppermute | solution.py:755
  24.1 1.0 copy-start.11
  24.5 0.7 copy-start.12
  25.0 0.7 copy-start.13
  86.6 3.4 %collective-permute-start.6 = (bf16[4,4,160,256]{3,2,1,0:T(8,128)(2,1)}, bf16[4,4,160,256]{3,2,1,0:T(8,128)(2,1)}, u32[]{:S(2)}, u32[]{:S(2)}) collective-permute-start(bf16[4,4,160,256]{3,2,1,0:T(8,128)(2,1)} %get-tuple-element.63), channel_id=1, source_target_pairs={{0,4},{4,0},{8,12},{12,8},{16,20},{20,16},{24,28},{28,24},{1,5},{5... | collective-permute-start | bytes 3932168 | tf_op jit(solution)/shard_map/ppermute | solution.py:755
  92.4 17.7 %collective-permute-start.7 = (bf16[4,160,256]{2,1,0:T(8,128)(2,1)}, bf16[4,160,256]{2,1,0:T(8,128)(2,1)S(1)}, u32[]{:S(2)}, u32[]{:S(2)}) collective-permute-start(bf16[4,160,256]{2,1,0:T(8,128)(2,1)} %get-tuple-element.64), channel_id=1, source_target_pairs={{0,1},{1,0},{2,3},{3,2},{4,5},{5,4},{6,7},{7,6},{8,9},{9,8},{10,11... | collective-permute-start | bytes 983048 | tf_op jit(solution)/shard_map/ppermute | solution.py:755
  92.5 23.6 %collective-permute-start.8 = (bf16[4,160,256]{2,1,0:T(8,128)(2,1)}, bf16[4,160,256]{2,1,0:T(8,128)(2,1)S(1)}, u32[]{:S(2)}, u32[]{:S(2)}) collective-permute-start(bf16[4,160,256]{2,1,0:T(8,128)(2,1)} %get-tuple-element.65), channel_id=1, source_target_pairs={{0,2},{1,3},{2,0},{3,1},{4,6},{5,7},{6,4},{7,5},{8,10},{9,11},{10,... | collective-permute-start | bytes 983048 | tf_op jit(solution)/shard_map/ppermute | solution.py:755
  101.4 16.3 %collective-permute-start.9 = (bf16[4,160,256]{2,1,0:T(8,128)(2,1)}, bf16[4,160,256]{2,1,0:T(8,128)(2,1)S(1)}, u32[]{:S(2)}, u32[]{:S(2)}) collective-permute-start(bf16[4,160,256]{2,1,0:T(8,128)(2,1)} %get-tuple-element.66), channel_id=1, source_target_pairs={{0,3},{1,2},{2,1},{3,0},{4,7},{5,6},{6,5},{7,4},{8,11},{9,10},{10,... | collective-permute-start | bytes 983048 | tf_op jit(solution)/shard_map/ppermute | solution.py:755
  117.9 8.0 %collective-permute-start.10 = (bf16[160,256]{1,0:T(8,128)(2,1)S(1)}, bf16[160,256]{1,0:T(8,128)(2,1)S(1)}, u32[]{:S(2)}, u32[]{:S(2)}) collective-permute-start(bf16[160,256]{1,0:T(8,128)(2,1)S(1)} %get-tuple-element.88), channel_id=1, source_target_pairs={{0,8},{4,12},{8,0},{12,4},{16,24},{20,28},{24,16},{28,20},{1,9},{5... | collective-permute-start | bytes 245768 | tf_op jit(solution)/shard_map/ppermute | solution.py:755
  118.0 12.3 %collective-permute-start.12 = (bf16[160,256]{1,0:T(8,128)(2,1)S(1)}, bf16[160,256]{1,0:T(8,128)(2,1)S(1)}, u32[]{:S(2)}, u32[]{:S(2)}) collective-permute-start(bf16[160,256]{1,0:T(8,128)(2,1)S(1)} %get-tuple-element.89), channel_id=1, source_target_pairs={{0,24},{4,28},{8,16},{12,20},{16,8},{20,12},{24,0},{28,4},{1,25},{... | collective-permute-start | bytes 245768 | tf_op jit(solution)/shard_map/ppermute | solution.py:755
  125.8 7.2 %collective-permute-start.11 = (bf16[160,256]{1,0:T(8,128)(2,1)S(1)}, bf16[160,256]{1,0:T(8,128)(2,1)S(1)}, u32[]{:S(2)}, u32[]{:S(2)}) collective-permute-start(bf16[160,256]{1,0:T(8,128)(2,1)S(1)} %get-tuple-element.90), channel_id=1, source_target_pairs={{0,16},{4,20},{8,24},{12,28},{16,0},{20,4},{24,8},{28,12},{1,17},{... | collective-permute-start | bytes 245768 | tf_op jit(solution)/shard_map/ppermute | solution.py:755
  133.0 4.5 %copy-start = (bf16[160,256]{1,0:T(8,128)(2,1)}, bf16[160,256]{1,0:T(8,128)(2,1)S(1)}, u32[]{:S(2)}) copy-start(bf16[160,256]{1,0:T(8,128)(2,1)S(1)} %fusion.2.refs_0_) | copy-start | bytes 245764
  133.0 7.3 %collective-permute-start.15 = (bf16[160,256]{1,0:T(8,128)(2,1)S(1)}, bf16[160,256]{1,0:T(8,128)(2,1)S(1)}, u32[]{:S(2)}, u32[]{:S(2)}) collective-permute-start(bf16[160,256]{1,0:T(8,128)(2,1)S(1)} %fusion.2.refs_0_), channel_id=1, source_target_pairs={{0,24},{4,28},{8,16},{12,20},{16,8},{20,12},{24,0},{28,4},{1,25},{... | collective-permute-start | bytes 245768 | tf_op jit(solution)/shard_map/ppermute | solution.py:755
  135.6 6.9 %collective-permute-start.14 = (bf16[160,256]{1,0:T(8,128)(2,1)S(1)}, bf16[160,256]{1,0:T(8,128)(2,1)S(1)}, u32[]{:S(2)}, u32[]{:S(2)}) collective-permute-start(bf16[160,256]{1,0:T(8,128)(2,1)S(1)} %fusion.2.refs_0_), channel_id=1, source_target_pairs={{0,16},{4,20},{8,24},{12,28},{16,0},{20,4},{24,8},{28,12},{1,17},{... | collective-permute-start | bytes 245768 | tf_op jit(solution)/shard_map/ppermute | solution.py:755
  135.6 6.9 %collective-permute-start.13 = (bf16[160,256]{1,0:T(8,128)(2,1)S(1)}, bf16[160,256]{1,0:T(8,128)(2,1)S(1)}, u32[]{:S(2)}, u32[]{:S(2)}) collective-permute-start(bf16[160,256]{1,0:T(8,128)(2,1)S(1)} %fusion.2.refs_0_), channel_id=1, source_target_pairs={{0,8},{4,12},{8,0},{12,4},{16,24},{20,28},{24,16},{28,20},{1,9},{5... | collective-permute-start | bytes 245768 | tf_op jit(solution)/shard_map/ppermute | solution.py:755
  137.5 5.6 %collective-permute-start.16 = (bf16[160,256]{1,0:T(8,128)(2,1)S(1)}, bf16[160,256]{1,0:T(8,128)(2,1)S(1)}, u32[]{:S(2)}, u32[]{:S(2)}) collective-permute-start(bf16[160,256]{1,0:T(8,128)(2,1)S(1)} %fusion.2.refs_0_), channel_id=1, source_target_pairs={{0,4},{4,0},{8,12},{12,8},{16,20},{20,16},{24,28},{28,24},{1,5},{5... | collective-permute-start | bytes 245768 | tf_op jit(solution)/shard_map/ppermute | solution.py:755
  140.3 3.6 %copy-start.1 = (bf16[160,256]{1,0:T(8,128)(2,1)}, bf16[160,256]{1,0:T(8,128)(2,1)S(1)}, u32[]{:S(2)}) copy-start(bf16[160,256]{1,0:T(8,128)(2,1)S(1)} %collective-permute-done.15.refs_3_) | copy-start | bytes 245764
  140.3 2.7 %collective-permute-start.19 = (bf16[160,256]{1,0:T(8,128)(2,1)S(1)}, bf16[160,256]{1,0:T(8,128)(2,1)S(1)}, u32[]{:S(2)}, u32[]{:S(2)}) collective-permute-start(bf16[160,256]{1,0:T(8,128)(2,1)S(1)} %collective-permute-done.15.refs_3_), channel_id=1, source_target_pairs={{0,4},{4,0},{8,12},{12,8},{16,20},{20,16},{24,28},{28,24},{1,5},{5... | collective-permute-start | bytes 245768 | tf_op jit(solution)/shard_map/ppermute | solution.py:755
  142.5 1.4 copy-start.2
  142.5 1.3 collective-permute-start.18
  142.5 1.4 copy-start.3
  142.5 1.4 collective-permute-start.17
  143.0 0.9 copy-start.4
  143.1 0.9 copy-start.5
  143.8 0.6 copy-start.6
  144.0 0.6 copy-start.7

commit v3 on v2

--- a/solution.py
+++ b/solution.py
@@ -15,6 +15,7 @@
 SUB = 128
 NSUB = EC // SUB
 NC = 256
+NODE_STEPS = 4
 EDGES = REL * SLOTS + EC
 bf16 = jnp.bfloat16
 f32 = jnp.float32
@@ -35,7 +36,7 @@
 V = pltpu.VMEM
 MIB = 1 << 20
 SOURCE, TARGET, TIME, TYPE, BUCKET = range(5)
-LAYER_VMEM = 60 * MIB
+LAYER_VMEM = 63 * MIB
 GROUP = 4
 WIDE = 1024 // GROUP
 
@@ -50,10 +51,10 @@
 
 def one_hot_rows(row, count):
     wide = row.shape[1]
-    base = lax.broadcasted_iota(jnp.int32, (256, wide), 0).astype(bf16)
+    base = lax.broadcasted_iota(jnp.int16, (256, wide), 0)
     one, zero = jnp.ones((), bf16), jnp.zeros((), bf16)
     return jnp.concatenate(
-        [jnp.where(base == (row - 256 * g).astype(bf16), one, zero) for g in range(count // 256)], axis=0
+        [jnp.where(base == (row - 256 * g).astype(jnp.int16), one, zero) for g in range(count // 256)], axis=0
     )
 
 
@@ -168,33 +169,47 @@
 LISTS = [pltpu.SMEM((REL * SLOTS // SUB + 2 * NSUB,), jnp.int32)] * 3
 
 
-def pack_half_kernel(lay, type_ref, edge_ref, norm_ref, mine_ref, buf, sems):
+def pack_half_kernel(lay, type_ref, edge_ref, norm_hbm, mine_ref, buf, low, norm_ref, isem, osem):
     _, core, _ = position()
-    rest = lay.half - lay.erows
+    norm = pltpu.make_async_copy(norm_hbm, norm_ref, isem.at[5])
+    norm.start()
+    rows = lay.half // 5
     for side in range(2):
         @pl.when(core == side)
         def _():
-            rows = lay.half if side == 0 else rest
-            first = pltpu.make_async_copy(
-                type_ref.at[pl.ds(side * lay.half, rows)], buf.at[pl.ds(0, rows)], sems.at[0]
-            )
-            first.start()
+            loads = []
+            for i in range(5):
+                if side == 1 and i >= 3:
+                    source, to = edge_ref.at[pl.ds((i - 3) * rows, rows)], buf.at[pl.ds(i * rows, rows), pl.ds(0, 768)]
+                else:
+                    source, to = type_ref.at[pl.ds(side * lay.half + i * rows, rows)], buf.at[pl.ds(i * rows, rows)]
+                loads.append(pltpu.make_async_copy(source, to, isem.at[i]))
+                loads[-1].start()
+            norm.wait()
             if side == 1:
-                second = pltpu.make_async_copy(edge_ref, buf.at[pl.ds(rest, lay.erows), pl.ds(0, 768)], sems.at[1])
-                second.start()
                 corner = jnp.concatenate([norm_ref[...], jnp.zeros((8, 256 - lay.wide), f32)], axis=1)
-                buf[rest:, 768:] = jnp.concatenate([corner, jnp.zeros((lay.erows - 8, 256), f32)], axis=0)
-                second.wait()
-            first.wait()
-    mine_ref[...] = buf[...].astype(bf16)
+                buf[3 * rows:, 768:] = jnp.concatenate([corner, jnp.zeros((lay.erows - 8, 256), f32)], axis=0)
+            stores = []
+            for i in range(5):
+                loads[i].wait()
+                at = slice(i * rows, (i + 1) * rows)
+                low[at] = buf[at].astype(bf16)
+                stores.append(pltpu.make_async_copy(low.at[pl.ds(i * rows, rows)], mine_ref.at[pl.ds(i * rows, rows)], osem.at[i]))
+                stores[-1].start()
+            for copy in stores:
+                copy.wait()
 
 
 def pack_half(lay, type_weight, edge_weight, norm_params):
     return pl.pallas_call(
         functools.partial(pack_half_kernel, lay),
         out_shape=S((lay.half, 1024), bf16),
-        in_specs=[ANY, ANY, VMEM],
-        scratch_shapes=[V((lay.half, 1024), f32), pltpu.SemaphoreType.DMA((2,))],
+        in_specs=[ANY] * 3,
+        out_specs=ANY,
+        scratch_shapes=[
+            V((lay.half, 1024), f32), V((lay.half, 1024), bf16), V((8, lay.wide), f32),
+            pltpu.SemaphoreType.DMA((6,)), pltpu.SemaphoreType.DMA((5,)),
+        ],
         compiler_params=pltpu.CompilerParams(vmem_limit_bytes=63 * MIB),
         name="pack_half",
     )(type_weight, edge_weight, norm_params)
@@ -256,13 +271,13 @@
 def layer_kernel(lay, *refs):
     nb = lay.blocks - 1
     (
-        live_ref, cnt_ref, kinds_ref, mix_ref, idx_ref, emb_ref, cot_hbm, feat_hbm, own_ref,
+        live_ref, cnt_ref, kinds_hbm, mix_hbm, idx_hbm, emb_hbm, cot_hbm, feat_hbm, own_ref,
     ) = refs[:9]
     near, far, xg_hbm = refs[9:9 + nb], refs[9 + nb:9 + 2 * nb], refs[9 + 2 * nb]
     (
         out_ref, dqkv_ref, skp_ref, keep_ref, send_ref,
         lst_r, lst_o, lst_c,
-        wpk, gpack, gout, gnorm, gskip, xg, outs, low, cot_ref, feat_ref,
+        wpk, gpack, gout, gnorm, gskip, xg, low, cot_ref, feat_ref, kinds_ref, mix_ref, idx_ref, emb_ref,
         wt, xcat, qt, rte, dn_buf, dkve_buf, mu,
         bda, bdat, bdm, bdmt, ga, gm, dmu,
         kve, qe, msg, wexp, raws,
@@ -271,10 +286,14 @@
     ) = refs[10 + 2 * nb:]
     me, core, zi = position()
     zi = lax.rem(zi, GROUP)
-    feat_copy = pltpu.make_async_copy(feat_hbm, feat_ref, xsem.at[1])
-    feat_copy.start()
+    small = [
+        pltpu.make_async_copy(source, to, xsem.at[3 + i])
+        for i, (source, to) in enumerate(
+            ((kinds_hbm, kinds_ref), (mix_hbm, mix_ref), (feat_hbm, feat_ref), (idx_hbm, idx_ref), (emb_hbm, emb_ref))
+        )
+    ]
     weights = lay.weight_copies(me, core, own_ref, near, far, wpk, wsem)
-    for copy in weights:
+    for copy in small + weights:
         copy.start()
     xg_copy = pltpu.make_async_copy(xg_hbm, xg, xsem.at[0])
     xg_copy.start()
@@ -290,6 +309,8 @@
         ref[...] = jnp.zeros_like(ref)
     dkve_buf[...] = jnp.zeros_like(dkve_buf)
 
+    small[0].wait()
+    small[1].wait()
     mix = jnp.broadcast_to(mix_ref[...].astype(bf16).astype(f32), (8, 68))
     lanes68 = lax.broadcasted_iota(jnp.int32, (8, 68), 1)
     line68 = lax.broadcasted_iota(jnp.int32, (8, 68), 0)
@@ -303,11 +324,11 @@
 
     kinds = kinds_ref[...]
     masks = (lax.broadcasted_iota(jnp.int32, (8, N), 0) == kinds).astype(f32)
-    feat_copy.wait()
+    small[2].wait()
     featt = nt(ident, feat_ref[...])
     for s in range(TYPES):
         xcat[s * D:(s + 1) * D, :] = (featt * masks[s:s + 1]).astype(bf16)
-    for copy in weights:
+    for copy in weights + small[3:]:
         copy.wait()
     cot_copy.start()
 
@@ -391,36 +412,36 @@
     lax.fori_loop(whole, chunks, functools.partial(forward, SUB), 0)
 
     cot_copy.wait()
-    nwt = nt(ident, lay.get_norm(wpk))
+    nwt = nt(ident, lay.get_norm(wpk)).astype(bf16)
+    out_rows = jnp.concatenate([lay.get_type(wpk, s, 3 * D, 4 * D) for s in range(TYPES)], axis=1)
 
     def nodes(c):
         at = pl.ds(pl.multiple_of(c * NC, NC), NC)
         mk = (lax.broadcasted_iota(jnp.int32, (8, NC), 0) == kinds_ref[:, at]).astype(f32)
         live = (lax.broadcasted_iota(jnp.int32, (1, NC), 1) + c * NC < live_ref[0]).astype(f32)
         den = num[D:D + H, at] + num[D + H:, at] + (1.0 - live)
-        denw = head_wide(den)
-        agg = num[:D, at] / denw
+        inv_den = head_wide(1.0 / den)
+        agg = num[:D, at] * inv_den
         phi = 0.5 * (1.0 + lax.erf(agg * (0.5 ** 0.5)))
-        act = (agg * phi).astype(bf16).astype(f32)
-        acat = jnp.concatenate([(act * mk[s:s + 1]).astype(bf16) for s in range(TYPES)], axis=0)
+        act = (agg * phi).astype(bf16)
+        mkl = mk.astype(bf16)
+        acat = jnp.concatenate([act * mkl[s:s + 1] for s in range(TYPES)], axis=0)
         yield
         trans = nn(wt[3 * D:, :], acat)
         yield
         alpha = 1.0 / (1.0 + jnp.exp(-jnp.sum(mk * skip_col, axis=0, keepdims=True)))
         ft = nt(ident, feat_ref[at, :])
+        none = jnp.zeros((4, NC), f32)
+        oh16 = jnp.concatenate([mk[0:4], none, none, none], axis=0).astype(bf16)
+        gain = nn(nwt, oh16)
+        bias = nn(nwt, jnp.concatenate([none, mk[0:4], none, none], axis=0).astype(bf16))
+        dy = live * nt(ident, cot_ref[at, :])
         res = alpha * trans + (1.0 - alpha) * ft
         mean = jnp.mean(res, axis=0, keepdims=True)
         cen = res - mean
         inv = lax.rsqrt(jnp.mean(cen * cen, axis=0, keepdims=True) + norm_eps)
         nrm = cen * inv
-        gain = nwt[:, 0:1] * mk[0:1]
-        bias = nwt[:, 4:5] * mk[0:1]
-        for s in range(1, TYPES):
-            gain = gain + nwt[:, s:s + 1] * mk[s:s + 1]
-            bias = bias + nwt[:, 4 + s:5 + s] * mk[s:s + 1]
-        outs[at, :] = (live * (nrm * gain + bias)).T.astype(bf16)
-        dy = live * nt(ident, cot_ref[at, :])
-        oh16 = jnp.concatenate([mk, jnp.zeros((8, NC), f32)], axis=0).astype(bf16)
+        cot_ref[at, :] = (live * (nrm * gain + bias)).T.astype(bf16)
         dyn = dy * nrm
         dyn_hi = dyn.astype(bf16)
         dyn_lo = (dyn - dyn_hi.astype(f32)).astype(bf16)
@@ -430,25 +451,25 @@
         dres = inv * (dn - jnp.mean(dn, axis=0, keepdims=True) - nrm * jnp.mean(dn * nrm, axis=0, keepdims=True))
         dtr = (alpha * dres).astype(bf16)
         yield
-        dact = pick(mk, [nn(lay.get_type(wpk, s, 3 * D, 4 * D), dtr) for s in range(TYPES)])
+        dact = nn(out_rows, jnp.concatenate([dtr * mkl[s:s + 1] for s in range(TYPES)], axis=0))
         yield
         skp[:, at] = (1.0 - alpha) * dres
         dal = jnp.sum(dres * (trans - ft), axis=0, keepdims=True) * alpha * (1.0 - alpha)
         gskip[...] += jnp.broadcast_to(jnp.sum(mk * dal, axis=1, keepdims=True), (8, 128))
         gout[...] += nt(acat, dtr)
         dagg = dact * (phi + agg * (jnp.exp(-0.5 * agg * agg) * (0.5 / np.pi) ** 0.5))
-        dnum[0:D, at] = (dagg / denw).astype(bf16)
+        dnum[0:D, at] = (dagg * inv_den).astype(bf16)
         dnum[D:, at] = hi_lo(-head_sum(dagg * agg) / den)
         yield
 
     def node_steps(c, _):
-        for _ in zip(nodes(2 * c), nodes(2 * c + 1)):
+        for _ in zip(*[nodes(NODE_STEPS * c + i) for i in range(NODE_STEPS)]):
             pass
         return 0
 
-    lax.fori_loop(0, N // NC // 2, node_steps, 0)
+    lax.fori_loop(0, N // NC // NODE_STEPS, node_steps, 0)
     finish = [
-        pltpu.make_async_copy(outs, out_ref, osem.at[0]),
+        pltpu.make_async_copy(cot_ref, out_ref, osem.at[0]),
         pltpu.make_async_copy(skp, skp_ref, osem.at[1]),
     ]
     for copy in finish:
@@ -491,7 +512,13 @@
         return 0
 
     gather_back(0)
-    lax.fori_loop(0, whole, functools.partial(backward, 2 * SUB), 0)
+    def backward_pair(c, _):
+        backward(2 * SUB, 2 * c, 0)
+        backward(2 * SUB, 2 * c + 1, 0)
+        return 0
+
+    lax.fori_loop(0, whole // 2, backward_pair, 0)
+    lax.fori_loop(whole // 2 * 2, whole, functools.partial(backward, 2 * SUB), 0)
     lax.fori_loop(whole, chunks, functools.partial(backward, SUB), 0)
     scatter_back(chunks - 1)
 
@@ -573,11 +600,12 @@
     return pl.pallas_call(
         functools.partial(layer_kernel, lay),
         out_shape=[S((N, D), bf16), S((N, 3 * D), bf16), S((D, N), f32), sums, sums],
-        in_specs=[SMEM, SMEM] + [VMEM] * 4 + [ANY] * (2 * lay.blocks + 2),
+        in_specs=[SMEM, SMEM] + [ANY] * (2 * lay.blocks + 6),
         out_specs=[ANY] * 5,
         scratch_shapes=LISTS + [
             V((lay.blocks * lay.part, 1024), bf16), V((lay.blocks * lay.part, 1024), bf16), V((TYPES * D, D), f32),
-            V((8, D), f32), V((8, 128), f32), edges(D, bf16), V((N, D), bf16), V((N, 3 * D), bf16), V((N, D), bf16), V((N, D), bf16),
+            V((8, D), f32), V((8, 128), f32), edges(D, bf16), V((N, 3 * D), bf16), V((N, D), bf16), V((N, D), bf16),
+            V(kinds.shape, jnp.int32), V(mix.shape, f32), V(idx.shape, jnp.int32), V((256, D), bf16),
             V((4 * D, TYPES * D), bf16), V((TYPES * D, N), bf16), V((D, N), bf16), V((D, 256), bf16),
             V((D + 16, EC), f32), V((2 * D, EC), bf16), V((REL, H, 128), f32),
             V((8, D, D), bf16), V((8, D, D), bf16), V((8, D, D), bf16), V((8, D, D), bf16),
@@ -585,7 +613,7 @@
             edges(2 * D, bf16), edges(D, bf16), V((D, REL * SLOTS), bf16),
             V((H, REL * SLOTS), f32), V((H, REL * SLOTS), f32),
             V((D + 16, N), f32), V((D + 16, N), bf16), V((N, 3 * D), f32), V((TYPES * 256, 2 * D), f32), V((D, N), f32),
-            pltpu.SemaphoreType.DMA((2 * lay.blocks - 1,)), pltpu.SemaphoreType.DMA((3,)),
+            pltpu.SemaphoreType.DMA((2 * lay.blocks - 1,)), pltpu.SemaphoreType.DMA((8,)),
             pltpu.SemaphoreType.DMA((3,)), pltpu.SemaphoreType.DMA((2 * lay.blocks * GROUP,)),
         ],
         compiler_params=pltpu.CompilerParams(vmem_limit_bytes=LAYER_VMEM),
@@ -673,11 +701,13 @@
 
 
 def adam(param, first, second, avg, grad, rate):
+    root = (1.0 - beta_two**STEP) ** 0.5
     first_new = beta_one * first + (1.0 - beta_one) * grad
-    second_new = beta_two * second + (1.0 - beta_two) * grad * grad
-    first_hat = first_new / (1.0 - beta_one**STEP)
-    second_hat = second_new / (1.0 - beta_two**STEP)
-    param_new = param - rate * (first_hat / (jnp.sqrt(second_hat) + adam_eps) + decay_rate * param)
+    second_new = beta_two * second + (1.0 - beta_two) * (grad * grad)
+    below = jnp.sqrt(second_new) + adam_eps * root
+    guess = pl.reciprocal(below, approx=True)
+    guess = guess * (2.0 - below * guess)
+    param_new = (1.0 - rate * decay_rate) * param - (rate * root / (1.0 - beta_one**STEP)) * (first_new * guess)
     avg_new = ema_keep * avg + (1.0 - ema_keep) * param_new
     return (param_new, first_new, second_new, avg_new)
 

time: 152 us -> 147 us (0.967); the launches traced: 150 us -> 148 us
  Pallas kernels: 88.7 us -> 59.3 us
  starting transfers between devices: 28.7 us -> 53.6 us
  waiting for transfers between devices: 28.3 us -> 30.7 us
    pallas_call x1, Pallas kernels: 60.8 us -> 35 us  [layer(): pl.pallas_call(functools.partial(layer_kernel, lay), out_shape=[S((N, D),...]
    ppermute x20, starting transfers between devices: 28.7 us -> 53.6 us  [swap(): return lax.ppermute(x, axis, [(i, i ^ mask) for i in range(size)])]
    pallas_call x1, Pallas kernels: 9.3 us -> 6.33 us  [before(): pl.pallas_call(before_kernel, out_shape=(S((EDGES // EC * 8, EC), jnp.int...]
    ppermute x20, waiting for transfers between devices: 28.3 us -> 30.7 us  [swap(): return lax.ppermute(x, axis, [(i, i ^ mask) for i in range(size)])]
  transfers between devices with their start and end apart: 20 -> 20, of which waited for: 13 -> 13; matrix products, arithmetic and copies ran while one was open for 1% -> 1% of each run, Pallas kernels for 12% -> 10%
where the time goes in v3:
time: 147 us; the launch traced here: 148 us
  Pallas kernels  59.3 us (40%)
  starting transfers between devices  53.6 us (36%)
  waiting for transfers between devices  30.7 us (21%)
  local copies, waits for them, and re-layouts  1.65 us (1%)
  between operations  1.64 us (1%)
    ppermute x20, starting transfers between devices, swap(): return lax.ppermute(x, axis, [(i, i ^ mask) for i in range(size)])  53.6 us
    pallas_call x1, Pallas kernels, layer(): pl.pallas_call(functools.partial(layer_kernel, lay), out_shape=[S((N, D),...  35 us
    ppermute x20, waiting for transfers between devices, swap(): return lax.ppermute(x, axis, [(i, i ^ mask) for i in range(size)])  30.7 us
    pallas_call x1, Pallas kernels, before(): pl.pallas_call(before_kernel, out_shape=(S((EDGES // EC * 8, EC), jnp.int...  6.33 us
    pallas_call x1, Pallas kernels, input_gradient(): pl.pallas_call(functools.partial(input_kernel, lay), out_shape=S((N, D),...  6.14 us
    pallas_call x1, Pallas kernels, update(): pl.pallas_call(functools.partial(update_kernel, jobs, len(states)), out_s...  5.32 us
  transfers between devices with their start and end apart: 20, of which 13 were waited for; matrix products, arithmetic and copies ran while one was open for 1% of the time, Pallas kernels for 10%

profile of v3, /device:TPU:0, one launch (start us, length us, event | category | flops | bytes accessed | tf_op | source)
XLA Modules:
  0.0 148.2 jit_solution(17848936823988335500)
XLA Ops:
  0.7 1.9 %pack_half.1 = bf16[160,1024]{1,0:T(8,128)(2,1)} custom-call(f32[256,1024]{1,0:T(8,128)} %refs_8_.1, f32[64,768]{1,0:T(8,128)} %refs_12_.1, f32[8,64]{1,0:T(8,128)} %refs_16_.1), custom_call_target="tpu_custom_call" | custom-call | tf_op jit(solution)/shard_map/pack_half/pallas_call | solution.py:204
  2.6 4.0 %collective-permute-start.2 = (bf16[160,1024]{1,0:T(8,128)(2,1)}, bf16[160,1024]{1,0:T(8,128)(2,1)S(1)}, u32[]{:S(2)}, u32[]{:S(2)}) collective-permute-start(bf16[160,1024]{1,0:T(8,128)(2,1)} %pack_half.1), channel_id=1, source_target_pairs={{0,3},{1,2},{2,1},{3,0},{4,7},{5,6},{6,5},{7,4},{8,11},{9,10},{10,... | collective-permute-start | bytes 983048 | tf_op jit(solution)/shard_map/ppermute | solution.py:785
  6.5 0.5 collective-permute-start.1
  7.0 0.1 collective-permute-start
  7.2 2.2 %pack.1.refs_8_.refs_3_ = bf16[320,1024]{1,0:T(8,128)(2,1)} custom-call(f32[256,1024]{1,0:T(8,128)} %refs_8_.1, f32[64,768]{1,0:T(8,128)} %refs_12_.1, f32[8,64]{1,0:T(8,128)} %refs_16_.1), custom_call_target="tpu_custom_call" | custom-call | tf_op jit(solution)/shard_map/pack/pallas_call | solution.py:226
  9.4 6.3 %before.1 = (s32[136,512]{1,0:T(8,128)}, bf16[256,8704]{1,0:T(8,128)(2,1)}) custom-call(s32[8]{0:T(128)} %refs_1_.1, s32[1,1024]{1,0:T(1,128)} %bitcast.27, s32[8,1024]{1,0:T(8,128)} %src_ref.1, s32[8,1024]{1,0:T(8,128)} %dst_ref.1, s32[8,1024]{1,0:T(8,128)} %tim_ref.1, bf16[1024,256]{1,0:T(8,128)(2,1)} %refs_7_.1), custom_call_target="tpu_custom_call" | custom-call | flops 4563402752 | bytes 6291456 | tf_op jit(solution)/shard_map/before/pallas_call | solution.py:260
  15.8 6.0 %collective-permute-done.refs_9_.refs_4_ = bf16[160,1024]{1,0:T(8,128)(2,1)S(1)} collective-permute-done((bf16[160,1024]{1,0:T(8,128)(2,1)}, bf16[160,1024]{1,0:T(8,128)(2,1)S(1)}, u32[]{:S(2)}, u32[]{:S(2)}) %collective-permute-start) | collective-permute-done | bytes 327712 | tf_op jit(solution)/shard_map/ppermute | solution.py:785
  21.7 0.0 collective-permute-done.2.refs_11_.refs_6_
  21.7 0.1 collective-permute-start.5
  21.8 0.0 collective-permute-done.1.refs_10_.refs_5_
  21.8 0.0 copy-start.9
  21.8 0.5 collective-permute-start.4
  22.3 0.1 collective-permute-start.3
  23.1 0.4 collective-permute-done.5.refs_14_.refs_9_
  23.4 0.5 collective-permute-done.4.refs_13_.refs_8_
  23.9 0.5 collective-permute-done.3.refs_12_.refs_7_
  24.4 0.3 copy-done.12
  24.7 0.7 copy-done.13
  25.4 35.0 %layer.1 = (bf16[1024,256]{1,0:T(8,128)(2,1)}, bf16[1024,768]{1,0:T(8,128)(2,1)}, f32[256,1024]{1,0:T(8,128)}, bf16[4,4,160,256]{3,2,1,0:T(8,128)(2,1)}, bf16[4,4,160,256]{3,2,1,0:T(8,128)(2,1)}) custom-call(s32[1]{0:T(128)S(6)} %copy.43.refs_0_, s32[8]{0:T(128)} %refs_1_.1, s32[1,1024]{1,0:T(1,128)} %bitcast.28, f32[1,68]{1,0:T(1,128)} %bitcast.22, ...), custom_call_target="tpu_custom_call" | custom-call | flops 60000002048 | bytes 16777216 | tf_op jit(solution)/shard_map/layer/pallas_call | solution.py:600
  60.3 22.4 %collective-permute-start.6 = (bf16[4,4,160,256]{3,2,1,0:T(8,128)(2,1)}, bf16[4,4,160,256]{3,2,1,0:T(8,128)(2,1)}, u32[]{:S(2)}, u32[]{:S(2)}) collective-permute-start(bf16[4,4,160,256]{3,2,1,0:T(8,128)(2,1)} %get-tuple-element.63), channel_id=1, source_target_pairs={{0,4},{4,0},{8,12},{12,8},{16,20},{20,16},{24,28},{28,24},{1,5},{5... | collective-permute-start | bytes 3932168 | tf_op jit(solution)/shard_map/ppermute | solution.py:785
  82.7 3.0 %collective-permute-done.6.got_ref = bf16[4,4,160,256]{3,2,1,0:T(8,128)(2,1)} collective-permute-done((bf16[4,4,160,256]{3,2,1,0:T(8,128)(2,1)}, bf16[4,4,160,256]{3,2,1,0:T(8,128)(2,1)}, u32[]{:S(2)}, u32[]{:S(2)}) %collective-permute-start.6) | collective-permute-done | bytes 1310752 | tf_op jit(solution)/shard_map/ppermute | solution.py:785
  85.8 2.4 %add_core.1 = (bf16[4,160,256]{2,1,0:T(8,128)(2,1)}, bf16[4,160,256]{2,1,0:T(8,128)(2,1)}, bf16[4,160,256]{2,1,0:T(8,128)(2,1)}) custom-call(bf16[4,4,160,256]{3,2,1,0:T(8,128)(2,1)} %get-tuple-element.62.keep_ref, bf16[4,4,160,256]{3,2,1,0:T(8,128)(2,1)} %collective-permute-done.6.got_ref), custom_call_target="tpu_custom_call" | custom-call | tf_op jit(solution)/shard_map/add_core/pallas_call | solution.py:686
  88.1 4.9 %collective-permute-start.7 = (bf16[4,160,256]{2,1,0:T(8,128)(2,1)}, bf16[4,160,256]{2,1,0:T(8,128)(2,1)S(1)}, u32[]{:S(2)}, u32[]{:S(2)}) collective-permute-start(bf16[4,160,256]{2,1,0:T(8,128)(2,1)} %get-tuple-element.64), channel_id=1, source_target_pairs={{0,1},{1,0},{2,3},{3,2},{4,5},{5,4},{6,7},{7,6},{8,9},{9,8},{10,11... | collective-permute-start | bytes 983048 | tf_op jit(solution)/shard_map/ppermute | solution.py:785
  93.0 2.7 %collective-permute-start.8 = (bf16[4,160,256]{2,1,0:T(8,128)(2,1)}, bf16[4,160,256]{2,1,0:T(8,128)(2,1)S(1)}, u32[]{:S(2)}, u32[]{:S(2)}) collective-permute-start(bf16[4,160,256]{2,1,0:T(8,128)(2,1)} %get-tuple-element.65), channel_id=1, source_target_pairs={{0,2},{1,3},{2,0},{3,1},{4,6},{5,7},{6,4},{7,5},{8,10},{9,11},{10,... | collective-permute-start | bytes 983048 | tf_op jit(solution)/shard_map/ppermute | solution.py:785
  95.7 1.4 collective-permute-start.9
  97.1 6.1 %input_gradient.1 = bf16[1024,256]{1,0:T(8,128)(2,1)} custom-call(s32[1,1024]{1,0:T(1,128)} %bitcast.29, bf16[1024,768]{1,0:T(8,128)(2,1)} %get-tuple-element.60.refs_1_, f32[256,1024]{1,0:T(8,128)} %get-tuple-element.61.refs_2_, bf16[320,1024]{1,0:T(8,128)(2,1)} %pack.1.refs_8_.refs_3_, bf16[160,1024]{1,0:T(8,128)(2,1)} %copy-done.10, ...), custom_call_target="tpu_custom_call" | custom-call | flops 1610612736 | bytes 6291456 | tf_op jit(solution)/shard_map/input_gradient/pallas_call | solution.py:644
  103.3 1.2 fusion
  104.4 6.1 %collective-permute-done.8 = bf16[4,160,256]{2,1,0:T(8,128)(2,1)S(1)} collective-permute-done((bf16[4,160,256]{2,1,0:T(8,128)(2,1)}, bf16[4,160,256]{2,1,0:T(8,128)(2,1)S(1)}, u32[]{:S(2)}, u32[]{:S(2)}) %collective-permute-start.8) | collective-permute-done | bytes 327712 | tf_op jit(solution)/shard_map/ppermute | solution.py:785
  110.6 1.7 %collective-permute-done.9 = bf16[4,160,256]{2,1,0:T(8,128)(2,1)S(1)} collective-permute-done((bf16[4,160,256]{2,1,0:T(8,128)(2,1)}, bf16[4,160,256]{2,1,0:T(8,128)(2,1)S(1)}, u32[]{:S(2)}, u32[]{:S(2)}) %collective-permute-start.9) | collective-permute-done | bytes 327712 | tf_op jit(solution)/shard_map/ppermute | solution.py:785
  112.3 0.1 fusion.4
  112.4 2.0 %collective-permute-start.10 = (bf16[160,256]{1,0:T(8,128)(2,1)S(1)}, bf16[160,256]{1,0:T(8,128)(2,1)S(1)}, u32[]{:S(2)}, u32[]{:S(2)}) collective-permute-start(bf16[160,256]{1,0:T(8,128)(2,1)S(1)} %get-tuple-element.88), channel_id=1, source_target_pairs={{0,8},{4,12},{8,0},{12,4},{16,24},{20,28},{24,16},{28,20},{1,9},{5... | collective-permute-start | bytes 245768 | tf_op jit(solution)/shard_map/ppermute | solution.py:785
  114.4 10.0 %collective-permute-start.12 = (bf16[160,256]{1,0:T(8,128)(2,1)S(1)}, bf16[160,256]{1,0:T(8,128)(2,1)S(1)}, u32[]{:S(2)}, u32[]{:S(2)}) collective-permute-start(bf16[160,256]{1,0:T(8,128)(2,1)S(1)} %get-tuple-element.89), channel_id=1, source_target_pairs={{0,24},{4,28},{8,16},{12,20},{16,8},{20,12},{24,0},{28,4},{1,25},{... | collective-permute-start | bytes 245768 | tf_op jit(solution)/shard_map/ppermute | solution.py:785
  124.4 0.0 collective-permute-done.10
  124.4 4.5 %collective-permute-done.12 = bf16[160,256]{1,0:T(8,128)(2,1)S(1)} collective-permute-done((bf16[160,256]{1,0:T(8,128)(2,1)S(1)}, bf16[160,256]{1,0:T(8,128)(2,1)S(1)}, u32[]{:S(2)}, u32[]{:S(2)}) %collective-permute-start.12) | collective-permute-done | bytes 81952 | tf_op jit(solution)/shard_map/ppermute | solution.py:785
  128.9 2.2 %collective-permute-done.11 = bf16[160,256]{1,0:T(8,128)(2,1)S(1)} collective-permute-done((bf16[160,256]{1,0:T(8,128)(2,1)S(1)}, bf16[160,256]{1,0:T(8,128)(2,1)S(1)}, u32[]{:S(2)}, u32[]{:S(2)}) %collective-permute-start.11) | collective-permute-done | bytes 81952 | tf_op jit(solution)/shard_map/ppermute | solution.py:785
  131.1 0.1 fusion.2.refs_0_
  131.2 2.3 %collective-permute-start.15 = (bf16[160,256]{1,0:T(8,128)(2,1)S(1)}, bf16[160,256]{1,0:T(8,128)(2,1)S(1)}, u32[]{:S(2)}, u32[]{:S(2)}) collective-permute-start(bf16[160,256]{1,0:T(8,128)(2,1)S(1)} %fusion.2.refs_0_), channel_id=1, source_target_pairs={{0,24},{4,28},{8,16},{12,20},{16,8},{20,12},{24,0},{28,4},{1,25},{... | collective-permute-start | bytes 245768 | tf_op jit(solution)/shard_map/ppermute | solution.py:785
  133.5 0.0 collective-permute-start.14
  133.5 2.2 %collective-permute-start.13 = (bf16[160,256]{1,0:T(8,128)(2,1)S(1)}, bf16[160,256]{1,0:T(8,128)(2,1)S(1)}, u32[]{:S(2)}, u32[]{:S(2)}) collective-permute-start(bf16[160,256]{1,0:T(8,128)(2,1)S(1)} %fusion.2.refs_0_), channel_id=1, source_target_pairs={{0,8},{4,12},{8,0},{12,4},{16,24},{20,28},{24,16},{28,20},{1,9},{5... | collective-permute-start | bytes 245768 | tf_op jit(solution)/shard_map/ppermute | solution.py:785
  135.7 0.0 collective-permute-start.16
  135.7 2.9 %collective-permute-done.15.refs_3_ = bf16[160,256]{1,0:T(8,128)(2,1)S(1)} collective-permute-done((bf16[160,256]{1,0:T(8,128)(2,1)S(1)}, bf16[160,256]{1,0:T(8,128)(2,1)S(1)}, u32[]{:S(2)}, u32[]{:S(2)}) %collective-permute-start.15) | collective-permute-done | bytes 81952 | tf_op jit(solution)/shard_map/ppermute | solution.py:785
  138.6 2.0 %collective-permute-done.14.refs_2_ = bf16[160,256]{1,0:T(8,128)(2,1)S(1)} collective-permute-done((bf16[160,256]{1,0:T(8,128)(2,1)S(1)}, bf16[160,256]{1,0:T(8,128)(2,1)S(1)}, u32[]{:S(2)}, u32[]{:S(2)}) %collective-permute-start.14) | collective-permute-done | bytes 81952 | tf_op jit(solution)/shard_map/ppermute | solution.py:785
  140.6 0.5 collective-permute-start.17
  141.1 0.7 collective-permute-done.18.refs_6_
  141.9 0.2 collective-permute-done.17.refs_5_
  142.1 0.4 copy-done.6
  142.5 0.2 copy-done.7
  142.7 5.3 %update.1 = (f32[256,1024]{1,0:T(8,128)}, f32[256,1024]{1,0:T(8,128)}, f32[256,1024]{1,0:T(8,128)}, f32[256,1024]{1,0:T(8,128)}, f32[64,768]{1,0:T(8,128)}, /*in...) custom-call(bf16[160,256]{1,0:T(8,128)(2,1)} %copy-done, ...), custom_call_target="tpu_custom_call" | custom-call | tf_op jit(solution)/shard_map/update/pallas_call | solution.py:760
  (30 shorter events, 0.1 us)
Async XLA Ops:
  2.6 19.2 %collective-permute-start.2 = (bf16[160,1024]{1,0:T(8,128)(2,1)}, bf16[160,1024]{1,0:T(8,128)(2,1)S(1)}, u32[]{:S(2)}, u32[]{:S(2)}) collective-permute-start(bf16[160,1024]{1,0:T(8,128)(2,1)} %pack_half.1), channel_id=1, source_target_pairs={{0,3},{1,2},{2,1},{3,0},{4,7},{5,6},{6,5},{7,4},{8,11},{9,10},{10,... | collective-permute-start | bytes 983048 | tf_op jit(solution)/shard_map/ppermute | solution.py:785
  6.5 15.3 %collective-permute-start.1 = (bf16[160,1024]{1,0:T(8,128)(2,1)}, bf16[160,1024]{1,0:T(8,128)(2,1)S(1)}, u32[]{:S(2)}, u32[]{:S(2)}) collective-permute-start(bf16[160,1024]{1,0:T(8,128)(2,1)} %pack_half.1), channel_id=1, source_target_pairs={{0,2},{1,3},{2,0},{3,1},{4,6},{5,7},{6,4},{7,5},{8,10},{9,11},{10,... | collective-permute-start | bytes 983048 | tf_op jit(solution)/shard_map/ppermute | solution.py:785
  7.0 14.7 %collective-permute-start = (bf16[160,1024]{1,0:T(8,128)(2,1)}, bf16[160,1024]{1,0:T(8,128)(2,1)S(1)}, u32[]{:S(2)}, u32[]{:S(2)}) collective-permute-start(bf16[160,1024]{1,0:T(8,128)(2,1)} %pack_half.1), channel_id=1, source_target_pairs={{0,1},{1,0},{2,3},{3,2},{4,5},{5,4},{6,7},{7,6},{8,9},{9,8},{10,11... | collective-permute-start | bytes 983048 | tf_op jit(solution)/shard_map/ppermute | solution.py:785
  21.7 3.6 %copy-start.10 = (bf16[160,1024]{1,0:T(8,128)(2,1)}, bf16[160,1024]{1,0:T(8,128)(2,1)S(1)}, u32[]{:S(2)}) copy-start(bf16[160,1024]{1,0:T(8,128)(2,1)S(1)} %collective-permute-done.refs_9_.refs_4_) | copy-start | bytes 983044
  21.7 3.6 %copy-start.8 = (bf16[160,1024]{1,0:T(8,128)(2,1)}, bf16[160,1024]{1,0:T(8,128)(2,1)S(1)}, u32[]{:S(2)}) copy-start(bf16[160,1024]{1,0:T(8,128)(2,1)S(1)} %collective-permute-done.2.refs_11_.refs_6_) | copy-start | bytes 983044
  21.7 1.7 %collective-permute-start.5 = (bf16[160,1024]{1,0:T(8,128)(2,1)S(1)}, bf16[160,1024]{1,0:T(8,128)(2,1)S(1)}, u32[]{:S(2)}, u32[]{:S(2)}) collective-permute-start(bf16[160,1024]{1,0:T(8,128)(2,1)S(1)} %collective-permute-done.2.refs_11_.refs_6_), channel_id=1, source_target_pairs={{0,4},{4,0},{8,12},{12,8},{16,20},{20,16},{24,28},{28,24},{1,5},{5... | collective-permute-start | bytes 983048 | tf_op jit(solution)/shard_map/ppermute | solution.py:785
  21.8 3.5 %copy-start.9 = (bf16[160,1024]{1,0:T(8,128)(2,1)}, bf16[160,1024]{1,0:T(8,128)(2,1)S(1)}, u32[]{:S(2)}) copy-start(bf16[160,1024]{1,0:T(8,128)(2,1)S(1)} %collective-permute-done.1.refs_10_.refs_5_) | copy-start | bytes 983044
  21.8 2.1 %collective-permute-start.4 = (bf16[160,1024]{1,0:T(8,128)(2,1)S(1)}, bf16[160,1024]{1,0:T(8,128)(2,1)S(1)}, u32[]{:S(2)}, u32[]{:S(2)}) collective-permute-start(bf16[160,1024]{1,0:T(8,128)(2,1)S(1)} %collective-permute-done.1.refs_10_.refs_5_), channel_id=1, source_target_pairs={{0,4},{4,0},{8,12},{12,8},{16,20},{20,16},{24,28},{28,24},{1,5},{5... | collective-permute-start | bytes 983048 | tf_op jit(solution)/shard_map/ppermute | solution.py:785
  22.3 2.0 %collective-permute-start.3 = (bf16[160,1024]{1,0:T(8,128)(2,1)S(1)}, bf16[160,1024]{1,0:T(8,128)(2,1)S(1)}, u32[]{:S(2)}, u32[]{:S(2)}) collective-permute-start(bf16[160,1024]{1,0:T(8,128)(2,1)S(1)} %collective-permute-done.refs_9_.refs_4_), channel_id=1, source_target_pairs={{0,4},{4,0},{8,12},{12,8},{16,20},{20,16},{24,28},{28,24},{1,5},{5... | collective-permute-start | bytes 983048 | tf_op jit(solution)/shard_map/ppermute | solution.py:785
  23.4 0.9 copy-start.11
  23.9 0.7 copy-start.12
  24.6 0.7 copy-start.13
  60.3 25.4 %collective-permute-start.6 = (bf16[4,4,160,256]{3,2,1,0:T(8,128)(2,1)}, bf16[4,4,160,256]{3,2,1,0:T(8,128)(2,1)}, u32[]{:S(2)}, u32[]{:S(2)}) collective-permute-start(bf16[4,4,160,256]{3,2,1,0:T(8,128)(2,1)} %get-tuple-element.63), channel_id=1, source_target_pairs={{0,4},{4,0},{8,12},{12,8},{16,20},{20,16},{24,28},{28,24},{1,5},{5... | collective-permute-start | bytes 3932168 | tf_op jit(solution)/shard_map/ppermute | solution.py:785
  88.1 16.3 %collective-permute-start.7 = (bf16[4,160,256]{2,1,0:T(8,128)(2,1)}, bf16[4,160,256]{2,1,0:T(8,128)(2,1)S(1)}, u32[]{:S(2)}, u32[]{:S(2)}) collective-permute-start(bf16[4,160,256]{2,1,0:T(8,128)(2,1)} %get-tuple-element.64), channel_id=1, source_target_pairs={{0,1},{1,0},{2,3},{3,2},{4,5},{5,4},{6,7},{7,6},{8,9},{9,8},{10,11... | collective-permute-start | bytes 983048 | tf_op jit(solution)/shard_map/ppermute | solution.py:785
  93.0 17.5 %collective-permute-start.8 = (bf16[4,160,256]{2,1,0:T(8,128)(2,1)}, bf16[4,160,256]{2,1,0:T(8,128)(2,1)S(1)}, u32[]{:S(2)}, u32[]{:S(2)}) collective-permute-start(bf16[4,160,256]{2,1,0:T(8,128)(2,1)} %get-tuple-element.65), channel_id=1, source_target_pairs={{0,2},{1,3},{2,0},{3,1},{4,6},{5,7},{6,4},{7,5},{8,10},{9,11},{10,... | collective-permute-start | bytes 983048 | tf_op jit(solution)/shard_map/ppermute | solution.py:785
  95.7 16.6 %collective-permute-start.9 = (bf16[4,160,256]{2,1,0:T(8,128)(2,1)}, bf16[4,160,256]{2,1,0:T(8,128)(2,1)S(1)}, u32[]{:S(2)}, u32[]{:S(2)}) collective-permute-start(bf16[4,160,256]{2,1,0:T(8,128)(2,1)} %get-tuple-element.66), channel_id=1, source_target_pairs={{0,3},{1,2},{2,1},{3,0},{4,7},{5,6},{6,5},{7,4},{8,11},{9,10},{10,... | collective-permute-start | bytes 983048 | tf_op jit(solution)/shard_map/ppermute | solution.py:785
  112.4 12.0 %collective-permute-start.10 = (bf16[160,256]{1,0:T(8,128)(2,1)S(1)}, bf16[160,256]{1,0:T(8,128)(2,1)S(1)}, u32[]{:S(2)}, u32[]{:S(2)}) collective-permute-start(bf16[160,256]{1,0:T(8,128)(2,1)S(1)} %get-tuple-element.88), channel_id=1, source_target_pairs={{0,8},{4,12},{8,0},{12,4},{16,24},{20,28},{24,16},{28,20},{1,9},{5... | collective-permute-start | bytes 245768 | tf_op jit(solution)/shard_map/ppermute | solution.py:785
  114.4 14.5 %collective-permute-start.12 = (bf16[160,256]{1,0:T(8,128)(2,1)S(1)}, bf16[160,256]{1,0:T(8,128)(2,1)S(1)}, u32[]{:S(2)}, u32[]{:S(2)}) collective-permute-start(bf16[160,256]{1,0:T(8,128)(2,1)S(1)} %get-tuple-element.89), channel_id=1, source_target_pairs={{0,24},{4,28},{8,16},{12,20},{16,8},{20,12},{24,0},{28,4},{1,25},{... | collective-permute-start | bytes 245768 | tf_op jit(solution)/shard_map/ppermute | solution.py:785
  124.4 6.7 %collective-permute-start.11 = (bf16[160,256]{1,0:T(8,128)(2,1)S(1)}, bf16[160,256]{1,0:T(8,128)(2,1)S(1)}, u32[]{:S(2)}, u32[]{:S(2)}) collective-permute-start(bf16[160,256]{1,0:T(8,128)(2,1)S(1)} %get-tuple-element.90), channel_id=1, source_target_pairs={{0,16},{4,20},{8,24},{12,28},{16,0},{20,4},{24,8},{28,12},{1,17},{... | collective-permute-start | bytes 245768 | tf_op jit(solution)/shard_map/ppermute | solution.py:785
  131.2 4.5 %copy-start = (bf16[160,256]{1,0:T(8,128)(2,1)}, bf16[160,256]{1,0:T(8,128)(2,1)S(1)}, u32[]{:S(2)}) copy-start(bf16[160,256]{1,0:T(8,128)(2,1)S(1)} %fusion.2.refs_0_) | copy-start | bytes 245764
  131.2 7.4 %collective-permute-start.15 = (bf16[160,256]{1,0:T(8,128)(2,1)S(1)}, bf16[160,256]{1,0:T(8,128)(2,1)S(1)}, u32[]{:S(2)}, u32[]{:S(2)}) collective-permute-start(bf16[160,256]{1,0:T(8,128)(2,1)S(1)} %fusion.2.refs_0_), channel_id=1, source_target_pairs={{0,24},{4,28},{8,16},{12,20},{16,8},{20,12},{24,0},{28,4},{1,25},{... | collective-permute-start | bytes 245768 | tf_op jit(solution)/shard_map/ppermute | solution.py:785
  133.5 7.1 %collective-permute-start.14 = (bf16[160,256]{1,0:T(8,128)(2,1)S(1)}, bf16[160,256]{1,0:T(8,128)(2,1)S(1)}, u32[]{:S(2)}, u32[]{:S(2)}) collective-permute-start(bf16[160,256]{1,0:T(8,128)(2,1)S(1)} %fusion.2.refs_0_), channel_id=1, source_target_pairs={{0,16},{4,20},{8,24},{12,28},{16,0},{20,4},{24,8},{28,12},{1,17},{... | collective-permute-start | bytes 245768 | tf_op jit(solution)/shard_map/ppermute | solution.py:785
  133.5 7.1 %collective-permute-start.13 = (bf16[160,256]{1,0:T(8,128)(2,1)S(1)}, bf16[160,256]{1,0:T(8,128)(2,1)S(1)}, u32[]{:S(2)}, u32[]{:S(2)}) collective-permute-start(bf16[160,256]{1,0:T(8,128)(2,1)S(1)} %fusion.2.refs_0_), channel_id=1, source_target_pairs={{0,8},{4,12},{8,0},{12,4},{16,24},{20,28},{24,16},{28,20},{1,9},{5... | collective-permute-start | bytes 245768 | tf_op jit(solution)/shard_map/ppermute | solution.py:785
  135.7 5.5 %collective-permute-start.16 = (bf16[160,256]{1,0:T(8,128)(2,1)S(1)}, bf16[160,256]{1,0:T(8,128)(2,1)S(1)}, u32[]{:S(2)}, u32[]{:S(2)}) collective-permute-start(bf16[160,256]{1,0:T(8,128)(2,1)S(1)} %fusion.2.refs_0_), channel_id=1, source_target_pairs={{0,4},{4,0},{8,12},{12,8},{16,20},{20,16},{24,28},{28,24},{1,5},{5... | collective-permute-start | bytes 245768 | tf_op jit(solution)/shard_map/ppermute | solution.py:785
  138.6 3.5 %copy-start.1 = (bf16[160,256]{1,0:T(8,128)(2,1)}, bf16[160,256]{1,0:T(8,128)(2,1)S(1)}, u32[]{:S(2)}) copy-start(bf16[160,256]{1,0:T(8,128)(2,1)S(1)} %collective-permute-done.15.refs_3_) | copy-start | bytes 245764
  138.6 2.5 %collective-permute-start.19 = (bf16[160,256]{1,0:T(8,128)(2,1)S(1)}, bf16[160,256]{1,0:T(8,128)(2,1)S(1)}, u32[]{:S(2)}, u32[]{:S(2)}) collective-permute-start(bf16[160,256]{1,0:T(8,128)(2,1)S(1)} %collective-permute-done.15.refs_3_), channel_id=1, source_target_pairs={{0,4},{4,0},{8,12},{12,8},{16,20},{20,16},{24,28},{28,24},{1,5},{5... | collective-permute-start | bytes 245768 | tf_op jit(solution)/shard_map/ppermute | solution.py:785
  140.6 1.4 copy-start.2
  140.6 1.3 collective-permute-start.18
  140.6 1.4 copy-start.3
  140.6 1.4 collective-permute-start.17
  141.1 0.9 copy-start.4
  141.1 0.9 copy-start.5
  141.9 0.6 copy-start.6
  142.0 0.6 copy-start.7

commit v4 on v3

--- a/solution.py
+++ b/solution.py
@@ -35,6 +35,8 @@
 S = jax.ShapeDtypeStruct
 V = pltpu.VMEM
 MIB = 1 << 20
+INPUT_VMEM = 62 * MIB
+SECOND = 3
 SOURCE, TARGET, TIME, TYPE, BUCKET = range(5)
 LAYER_VMEM = 63 * MIB
 GROUP = 4
@@ -95,6 +97,8 @@
         self.part = self.trows + self.erows
         self.half = self.part // 2
         self.wide = D // blocks
+        self.second = self.half * SECOND // 10 // 16 * 16
+        self.first = self.half - self.second
 
     def type_rows(self, s):
         for f in range(self.blocks):
@@ -275,7 +279,7 @@
     ) = refs[:9]
     near, far, xg_hbm = refs[9:9 + nb], refs[9 + nb:9 + 2 * nb], refs[9 + 2 * nb]
     (
-        out_ref, dqkv_ref, skp_ref, keep_ref, send_ref,
+        out_ref, dqkv_ref, skp_ref, types_ref, keep_ref, send_ref,
         lst_r, lst_o, lst_c,
         wpk, gpack, gout, gnorm, gskip, xg, low, cot_ref, feat_ref, kinds_ref, mix_ref, idx_ref, emb_ref,
         wt, xcat, qt, rte, dn_buf, dkve_buf, mu,
@@ -331,6 +335,14 @@
     for copy in weights + small[3:]:
         copy.wait()
     cot_copy.start()
+    finish = [
+        pltpu.make_async_copy(
+            wpk.at[pl.ds(a, b - a), pl.ds(0, 3 * D)], types_ref.at[pl.ds(s * D + c, d - c)], osem.at[3 + f]
+        )
+        for s in range(TYPES) for f, a, b, c, d in lay.type_rows(s)
+    ]
+    for copy in finish:
+        copy.start()
 
     lane = lax.broadcasted_iota(jnp.int32, (D, 128), 1)
     rowi = lax.broadcasted_iota(jnp.int32, (D, 128), 0)
@@ -468,12 +480,9 @@
         return 0
 
     lax.fori_loop(0, N // NC // NODE_STEPS, node_steps, 0)
-    finish = [
-        pltpu.make_async_copy(cot_ref, out_ref, osem.at[0]),
-        pltpu.make_async_copy(skp, skp_ref, osem.at[1]),
-    ]
-    for copy in finish:
-        copy.start()
+    for i, (source, to) in enumerate(((cot_ref, out_ref), (skp, skp_ref))):
+        finish.append(pltpu.make_async_copy(source, to, osem.at[i]))
+        finish[-1].start()
 
     def gather_back(c):
         dn_buf[...] = nn(dnum[...], one_hot_rows(row(c, TARGET), N))
@@ -531,9 +540,12 @@
     for s in range(TYPES):
         drte = drte + nt(lay.get_type(wpk, s, D, 3 * D), dt[s * 256:(s + 1) * 256, :])
 
+    spots = [jnp.bitwise_xor(zi, j) for j in range(GROUP)]
+
     def put_edge(c0, value):
+        lanes = slice(c0 % WIDE, c0 % WIDE + value.shape[1])
         for f in range(lay.blocks):
-            gpack[f * lay.part + lay.trows:(f + 1) * lay.part, c0:c0 + value.shape[1]] = value[
+            gpack[spots[c0 // WIDE], f * lay.part + lay.trows:(f + 1) * lay.part, lanes] = value[
                 f * lay.erows:(f + 1) * lay.erows
             ].astype(bf16)
 
@@ -560,26 +572,23 @@
             [gnorm[:, f * lay.wide:(f + 1) * lay.wide], jnp.zeros((8, 256 - lay.wide), f32)], axis=1
         )
         small = jnp.concatenate([corner, mixg, jnp.zeros((lay.erows - 16, 256), f32)], axis=0)
-        gpack[f * lay.part + lay.trows:(f + 1) * lay.part, 768:] = small.astype(bf16)
+        gpack[spots[3], f * lay.part + lay.trows:(f + 1) * lay.part, :] = small.astype(bf16)
 
     done = 0
     for s in range(TYPES):
         g = nn(xcat[s * D:(s + 1) * D, :], low[...])
         g_kv = g[:, D:] + nn(rte[...], dt[s * 256:(s + 1) * 256, :])
-        value = jnp.concatenate([g[:, :D], g_kv, gout[s * D:(s + 1) * D, :]], axis=1).astype(bf16)
+        values = [g[:, :D], g_kv[:, :D], g_kv[:, D:], gout[s * D:(s + 1) * D, :]]
         for _, a, b, c, d in lay.type_rows(s):
-            gpack[a:b, :] = value[c:d]
+            for j in range(GROUP):
+                gpack[spots[j], a:b, :] = values[j][c:d].astype(bf16)
         while done < lay.blocks and (done + 1) * lay.trows <= (s + 1) * D:
             m = jnp.bitwise_xor(me, done)
             for i, (ref, side) in enumerate(((send_ref, 1 - core), (keep_ref, core))):
                 at = pl.ds(pl.multiple_of(done * lay.part + side * lay.half, 16), lay.half)
-                for j in range(GROUP):
-                    copy = pltpu.make_async_copy(
-                        gpack.at[at, pl.ds(j * WIDE, WIDE)], ref.at[m, jnp.bitwise_xor(zi, j)],
-                        gsem.at[(2 * done + i) * GROUP + j],
-                    )
-                    copy.start()
-                    finish.append(copy)
+                copy = pltpu.make_async_copy(gpack.at[:, at], ref.at[m], gsem.at[2 * done + i])
+                copy.start()
+                finish.append(copy)
             done += 1
     for copy in finish:
         copy.wait()
@@ -599,11 +608,11 @@
     edges = lambda rows, kind: V((rows, EDGES), kind)
     return pl.pallas_call(
         functools.partial(layer_kernel, lay),
-        out_shape=[S((N, D), bf16), S((N, 3 * D), bf16), S((D, N), f32), sums, sums],
+        out_shape=[S((N, D), bf16), S((N, 3 * D), bf16), S((D, N), f32), S((TYPES * D, 3 * D), bf16), sums, sums],
         in_specs=[SMEM, SMEM] + [ANY] * (2 * lay.blocks + 6),
-        out_specs=[ANY] * 5,
+        out_specs=[ANY] * 6,
         scratch_shapes=LISTS + [
-            V((lay.blocks * lay.part, 1024), bf16), V((lay.blocks * lay.part, 1024), bf16), V((TYPES * D, D), f32),
+            V((lay.blocks * lay.part, 1024), bf16), V((GROUP, lay.blocks * lay.part, WIDE), bf16), V((TYPES * D, D), f32),
             V((8, D), f32), V((8, 128), f32), edges(D, bf16), V((N, 3 * D), bf16), V((N, D), bf16), V((N, D), bf16),
             V(kinds.shape, jnp.int32), V(mix.shape, f32), V(idx.shape, jnp.int32), V((256, D), bf16),
             V((4 * D, TYPES * D), bf16), V((TYPES * D, N), bf16), V((D, N), bf16), V((D, 256), bf16),
@@ -614,7 +623,7 @@
             V((H, REL * SLOTS), f32), V((H, REL * SLOTS), f32),
             V((D + 16, N), f32), V((D + 16, N), bf16), V((N, 3 * D), f32), V((TYPES * 256, 2 * D), f32), V((D, N), f32),
             pltpu.SemaphoreType.DMA((2 * lay.blocks - 1,)), pltpu.SemaphoreType.DMA((8,)),
-            pltpu.SemaphoreType.DMA((3,)), pltpu.SemaphoreType.DMA((2 * lay.blocks * GROUP,)),
+            pltpu.SemaphoreType.DMA((3 + lay.blocks,)), pltpu.SemaphoreType.DMA((2 * lay.blocks,)),
         ],
         compiler_params=pltpu.CompilerParams(vmem_limit_bytes=LAYER_VMEM),
         cost_estimate=pl.CostEstimate(flops=60 * 10**9, bytes_accessed=16 * MIB, transcendentals=0),
@@ -622,34 +631,22 @@
     )(live, cnt, kinds, mix, idx, jnp.asarray(emb_table(), bf16), cot, feat, own, *near, *far, xg)
 
 
-def input_kernel(lay, *refs):
-    nb = lay.blocks - 1
-    kinds_ref, dqkv_ref, skp_ref, own_ref = refs[:4]
-    near, far = refs[4:4 + nb], refs[4 + nb:4 + 2 * nb]
-    out_ref, wpk, sems = refs[4 + 2 * nb:]
-    me, core, _ = position()
-    weights = lay.weight_copies(me, core, own_ref, near, far, wpk, sems)
-    for copy in weights:
-        copy.start()
+def input_kernel(kinds_ref, dqkv_ref, skp_ref, types_ref, out_ref):
     masks = (lax.broadcasted_iota(jnp.int32, (8, N), 0) == kinds_ref[...]).astype(f32)
-    for copy in weights:
-        copy.wait()
     for c in range(N // NC):
         at = slice(c * NC, (c + 1) * NC)
-        proj = pick(masks[:, at], [nt(lay.get_type(wpk, s, 0, 3 * D), dqkv_ref[at, :]) for s in range(TYPES)])
+        proj = pick(masks[:, at], [nt(types_ref[s * D:(s + 1) * D, :], dqkv_ref[at, :]) for s in range(TYPES)])
         out_ref[at, :] = (proj + skp_ref[:, at]).T.astype(bf16)
 
 
-def input_gradient(lay, kinds, dqkv, skp, own, near, far):
+def input_gradient(kinds, dqkv, skp, types):
     return pl.pallas_call(
-        functools.partial(input_kernel, lay),
+        input_kernel,
         out_shape=S((N, D), bf16),
-        in_specs=[VMEM] * 3 + [ANY] * (2 * lay.blocks - 1),
-        scratch_shapes=[V((lay.blocks * lay.part, 1024), bf16), pltpu.SemaphoreType.DMA((2 * lay.blocks - 1,))],
-        compiler_params=pltpu.CompilerParams(vmem_limit_bytes=63 * MIB),
+        compiler_params=pltpu.CompilerParams(vmem_limit_bytes=INPUT_VMEM),
         cost_estimate=pl.CostEstimate(flops=2 * N * D * D * 12, bytes_accessed=6 * MIB, transcendentals=0),
         name="input_gradient",
-    )(kinds, dqkv, skp, own, *near, *far)
+    )(kinds, dqkv, skp, types)
 
 
 def tree(terms):
@@ -658,42 +655,46 @@
     return terms[0]
 
 
-def add_core_kernel(blocks, keep_ref, got_ref, *refs):
-    outs, keep, got, isem, osem = refs[:blocks - 1], *refs[blocks - 1:]
+def add_core_kernel(lay, keep_ref, got_ref, *refs):
+    ways = ((lay.blocks, lambda ref, m: ref.at[m, :, pl.ds(0, lay.first)]),
+            (GROUP, lambda ref, m: ref.at[:, m, pl.ds(lay.first, lay.second)]))
+    jobs = [(way, m) for way in range(2) for m in range(1, ways[way][0])] + [(0, 0), (1, 0)]
+    outs, bufs, isem, osem = refs[:len(jobs)], refs[len(jobs):-2], *refs[-2:]
     loads = []
-    for m in range(1, blocks):
+    for k, (way, m) in enumerate(jobs):
         pair = [
-            pltpu.make_async_copy(keep_ref.at[m], keep.at[m - 1], isem.at[2 * m - 2]),
-            pltpu.make_async_copy(got_ref.at[m], got.at[m - 1], isem.at[2 * m - 1]),
+            pltpu.make_async_copy(ways[way][1](source, m), bufs[2 * way + i].at[m], isem.at[2 * k + i])
+            for i, source in enumerate((keep_ref, got_ref))
         ]
         for copy in pair:
             copy.start()
         loads.append(pair)
     stores = []
-    for m in range(1, blocks):
-        for copy in loads[m - 1]:
+    for k, (way, m) in enumerate(jobs):
+        for copy in loads[k]:
             copy.wait()
-        keep[m - 1] = (keep[m - 1].astype(f32) + got[m - 1].astype(f32)).astype(bf16)
-        store = pltpu.make_async_copy(keep.at[m - 1], outs[m - 1], osem.at[m - 1])
-        store.start()
-        stores.append(store)
+        keep, got = bufs[2 * way], bufs[2 * way + 1]
+        keep[m] = (keep[m].astype(f32) + got[m].astype(f32)).astype(bf16)
+        stores.append(pltpu.make_async_copy(keep.at[m], outs[k], osem.at[k]))
+        stores[-1].start()
     for copy in stores:
         copy.wait()
 
 
-def add_core(blocks, keep, got):
-    buf = V((blocks - 1, *keep.shape[1:]), bf16)
-    return pl.pallas_call(
-        functools.partial(add_core_kernel, blocks),
-        out_shape=[S(keep.shape[1:], bf16)] * (blocks - 1),
-        in_specs=[ANY, ANY],
-        out_specs=[ANY] * (blocks - 1),
-        scratch_shapes=[
-            buf, buf, pltpu.SemaphoreType.DMA((2 * blocks - 2,)), pltpu.SemaphoreType.DMA((blocks - 1,)),
-        ],
+def add_core(lay, keep, got):
+    shapes = [(lay.blocks, GROUP, lay.first, WIDE)] * 2 + [(GROUP, lay.blocks, lay.second, WIDE)] * 2
+    out_shape = [S(shape[1:], bf16) for shape in shapes[::2] for _ in range(shape[0] - 1)] + [S(shape[1:], bf16) for shape in shapes[::2]]
+    outs = pl.pallas_call(
+        functools.partial(add_core_kernel, lay),
+        out_shape=out_shape,
+        in_specs=[ANY] * 2,
+        out_specs=[ANY] * len(out_shape),
+        scratch_shapes=[V(shape, bf16) for shape in shapes]
+        + [pltpu.SemaphoreType.DMA((2 * len(out_shape),)), pltpu.SemaphoreType.DMA((len(out_shape),))],
         compiler_params=pltpu.CompilerParams(vmem_limit_bytes=63 * MIB),
         name="add_core",
     )(keep, got)
+    return [outs[-2], *outs[:lay.blocks - 1]], [outs[-1], *outs[lay.blocks - 1:-2]]
 
 
 def summed(terms):
@@ -792,17 +793,22 @@
     own, idx, xg, near[0] = lax.optimization_barrier((own, idx, xg, near[0]))
     far = [swap(x, "dp", 1) for x in near]
     mixes = [x.reshape(1, 68) for x in (mix_params, mix_first, mix_second, mix_avg)]
-    layer_out, dqkv, skp, keep, send = layer(
+    layer_out, dqkv, skp, types, keep, send = layer(
         lay, node_count, edge_count, kinds, mixes[0], idx, out_cot, node_feat,
         own, near, far, xg,
     )
     got = swap(send, "dp", 1)
-    chip = add_core(fsdp, keep, got)
-    parts = [summed([keep[0], got[0]])] + [swap(chip[m - 1], "fsdp", m) for m in range(1, fsdp)]
-    input_grad = input_gradient(lay, kinds, dqkv, skp, own, near, far)
-    input_grad, *parts = lax.optimization_barrier((input_grad, *parts))
-    pieces = [summed([x[k] for x in parts]) for k in range(GROUP)]
-    total = summed([pieces[0]] + [swap(pieces[k], "dp", 2 * k) for k in range(1, GROUP)])
+    chip_a, chip_b = add_core(lay, keep, got)
+    dqkv, *chip_a = lax.optimization_barrier((dqkv, *chip_a))
+    part_a = [chip_a[0]] + [swap(chip_a[m], "fsdp", m) for m in range(1, fsdp)]
+    part_b = [chip_b[0]] + [swap(chip_b[k], "dp", 2 * k) for k in range(1, GROUP)]
+    input_grad = input_gradient(kinds, dqkv, skp, types)
+    input_grad, *part_a = lax.optimization_barrier((input_grad, *part_a))
+    piece_a = [summed([x[k] for x in part_a]) for k in range(GROUP)]
+    piece_b = [summed([x[m] for x in part_b]) for m in range(fsdp)]
+    total_a = summed([piece_a[0]] + [swap(piece_a[k], "dp", 2 * k) for k in range(1, GROUP)])
+    total_b = summed([piece_b[0]] + [swap(piece_b[m], "fsdp", m) for m in range(1, fsdp)])
+    total = jnp.concatenate([total_a, total_b], axis=0)
     step = GROUP
     while step < lines:
         total = summed([total, swap(total, "dp", 2 * step)])

time: 147 us -> 140 us (0.952)
  Pallas kernels: 59.3 us -> 87.5 us
  starting transfers between devices: 53.6 us -> 30.6 us
  waiting for transfers between devices: 30.7 us -> 18.3 us
    pallas_call x1, Pallas kernels: 35 us -> 60.5 us  [layer(): pl.pallas_call(functools.partial(layer_kernel, lay), out_shape=[S((N, D),...]
    ppermute x20 -> x26, starting transfers between devices: 53.6 us -> 30.6 us  [swap(): return lax.ppermute(x, axis, [(i, i ^ mask) for i in range(size)])]
    ppermute x20 -> x26, waiting for transfers between devices: 30.7 us -> 18.3 us  [swap(): return lax.ppermute(x, axis, [(i, i ^ mask) for i in range(size)])]
    pallas_call x1, Pallas kernels: 6.33 us -> 9.8 us  [before(): pl.pallas_call(before_kernel, out_shape=(S((EDGES // EC * 8, EC), jnp.int...]
  transfers between devices with their start and end apart: 20 -> 26, of which waited for: 13 -> 14; matrix products, arithmetic and copies ran while one was open for 1% -> 0% of each run, Pallas kernels for 10% -> 12%
where the time goes in v4:
time: 140 us
  Pallas kernels  87.5 us (62%)
  starting transfers between devices  30.6 us (22%)
  waiting for transfers between devices  18.3 us (13%)
  between operations  1.69 us (1%)
  local copies, waits for them, and re-layouts  1.62 us (1%)
    pallas_call x1, Pallas kernels, layer(): pl.pallas_call(functools.partial(layer_kernel, lay), out_shape=[S((N, D),...  60.5 us
    ppermute x26, starting transfers between devices, swap(): return lax.ppermute(x, axis, [(i, i ^ mask) for i in range(size)])  30.6 us
    ppermute x26, waiting for transfers between devices, swap(): return lax.ppermute(x, axis, [(i, i ^ mask) for i in range(size)])  18.3 us
    pallas_call x1, Pallas kernels, before(): pl.pallas_call(before_kernel, out_shape=(S((EDGES // EC * 8, EC), jnp.int...  9.8 us
    pallas_call x1, Pallas kernels, update(): pl.pallas_call(functools.partial(update_kernel, jobs, len(states)), out_s...  5.32 us
    pallas_call x1, Pallas kernels, input_gradient(): pl.pallas_call(input_kernel, out_shape=S((N, D), bf16), compiler_params=p...  4.96 us
  transfers between devices with their start and end apart: 26, of which 14 were waited for; matrix products, arithmetic and copies ran while one was open for 0% of the time, Pallas kernels for 12%

profile of v4, /device:TPU:0, one launch (start us, length us, event | category | flops | bytes accessed | tf_op | source)
XLA Modules:
  0.0 139.9 jit_solution(12589830940729693693)
XLA Ops:
  0.7 1.9 %pack_half.1 = bf16[160,1024]{1,0:T(8,128)(2,1)} custom-call(f32[256,1024]{1,0:T(8,128)} %refs_8_.1, f32[64,768]{1,0:T(8,128)} %refs_12_.1, f32[8,64]{1,0:T(8,128)} %refs_16_.1), custom_call_target="tpu_custom_call" | custom-call | tf_op jit(solution)/shard_map/pack_half/pallas_call | solution.py:208
  2.6 4.0 %collective-permute-start.2 = (bf16[160,1024]{1,0:T(8,128)(2,1)}, bf16[160,1024]{1,0:T(8,128)(2,1)S(1)}, u32[]{:S(2)}, u32[]{:S(2)}) collective-permute-start(bf16[160,1024]{1,0:T(8,128)(2,1)} %pack_half.1), channel_id=1, source_target_pairs={{0,3},{1,2},{2,1},{3,0},{4,7},{5,6},{6,5},{7,4},{8,11},{9,10},{10,... | collective-permute-start | bytes 983048 | tf_op jit(solution)/shard_map/ppermute | solution.py:786
  6.5 0.5 collective-permute-start.1
  7.0 0.1 collective-permute-start
  7.2 2.2 %pack.1.refs_8_ = bf16[320,1024]{1,0:T(8,128)(2,1)} custom-call(f32[256,1024]{1,0:T(8,128)} %refs_8_.1, f32[64,768]{1,0:T(8,128)} %refs_12_.1, f32[8,64]{1,0:T(8,128)} %refs_16_.1), custom_call_target="tpu_custom_call" | custom-call | tf_op jit(solution)/shard_map/pack/pallas_call | solution.py:230
  9.4 9.8 %before.1 = (s32[136,512]{1,0:T(8,128)}, bf16[256,8704]{1,0:T(8,128)(2,1)}) custom-call(s32[8]{0:T(128)} %refs_1_.1, s32[1,1024]{1,0:T(1,128)} %bitcast.36, s32[8,1024]{1,0:T(8,128)} %src_ref.1, s32[8,1024]{1,0:T(8,128)} %dst_ref.1, s32[8,1024]{1,0:T(8,128)} %tim_ref.1, bf16[1024,256]{1,0:T(8,128)(2,1)} %refs_7_.1), custom_call_target="tpu_custom_call" | custom-call | flops 4563402752 | bytes 6291456 | tf_op jit(solution)/shard_map/before/pallas_call | solution.py:264
  19.2 2.5 %collective-permute-done.refs_9_ = bf16[160,1024]{1,0:T(8,128)(2,1)S(1)} collective-permute-done((bf16[160,1024]{1,0:T(8,128)(2,1)}, bf16[160,1024]{1,0:T(8,128)(2,1)S(1)}, u32[]{:S(2)}, u32[]{:S(2)}) %collective-permute-start) | collective-permute-done | bytes 327712 | tf_op jit(solution)/shard_map/ppermute | solution.py:786
  21.7 0.1 collective-permute-start.5
  21.8 0.0 copy-start.11
  21.8 0.5 collective-permute-start.4
  22.3 0.1 collective-permute-start.3
  23.1 0.4 collective-permute-done.5.refs_14_
  23.4 0.5 collective-permute-done.4.refs_13_
  23.9 0.5 collective-permute-done.3.refs_12_
  24.4 0.3 copy-done.14
  24.6 0.7 copy-done.15
  25.4 60.5 %layer.1 = (bf16[1024,256]{1,0:T(8,128)(2,1)}, bf16[1024,768]{1,0:T(8,128)(2,1)}, f32[256,1024]{1,0:T(8,128)}, bf16[1024,768]{1,0:T(8,128)(2,1)}, bf16[4,4,160,2...) custom-call(s32[1]{0:T(128)S(6)} %copy.43.refs_0_, s32[8]{0:T(128)} %refs_1_.1, s32[1,1024]{1,0:T(1,128)} %bitcast.37, ...), custom_call_target="tpu_custom_call" | custom-call | flops 60000002048 | bytes 16777216 | tf_op jit(solution)/shard_map/layer/pallas_call | solution.py:609
  85.9 7.4 %collective-permute-start.6 = (bf16[4,4,160,256]{3,2,1,0:T(8,128)(2,1)}, bf16[4,4,160,256]{3,2,1,0:T(8,128)(2,1)}, u32[]{:S(2)}, u32[]{:S(2)}) collective-permute-start(bf16[4,4,160,256]{3,2,1,0:T(8,128)(2,1)} %get-tuple-element.73), channel_id=1, source_target_pairs={{0,4},{4,0},{8,12},{12,8},{16,20},{20,16},{24,28},{28,24},{1,5},{5... | collective-permute-start | bytes 3932168 | tf_op jit(solution)/shard_map/ppermute | solution.py:786
  93.3 3.0 %collective-permute-done.6.got_ref = bf16[4,4,160,256]{3,2,1,0:T(8,128)(2,1)} collective-permute-done((bf16[4,4,160,256]{3,2,1,0:T(8,128)(2,1)}, bf16[4,4,160,256]{3,2,1,0:T(8,128)(2,1)}, u32[]{:S(2)}, u32[]{:S(2)}) %collective-permute-start.6) | collective-permute-done | bytes 1310752 | tf_op jit(solution)/shard_map/ppermute | solution.py:786
  96.3 2.7 %add_core.1 = (bf16[4,112,256]{2,1,0:T(8,128)(2,1)}, bf16[4,112,256]{2,1,0:T(8,128)(2,1)}, bf16[4,112,256]{2,1,0:T(8,128)(2,1)}, bf16[4,48,256]{2,1,0:T(8,128)(2...) custom-call(bf16[4,4,160,256]{3,2,1,0:T(8,128)(2,1)} %get-tuple-elem, ...), custom_call_target="tpu_custom_call" | custom-call | tf_op jit(solution)/shard_map/add_core/pallas_call | solution.py:687
  99.0 0.1 collective-permute-start.13
  99.1 0.1 collective-permute-start.14
  99.2 4.3 %collective-permute-start.15 = (bf16[4,48,256]{2,1,0:T(8,128)(2,1)}, bf16[4,48,256]{2,1,0:T(8,128)(2,1)S(1)}, u32[]{:S(2)}, u32[]{:S(2)}) collective-permute-start(bf16[4,48,256]{2,1,0:T(8,128)(2,1)} %get-tuple-element.93), channel_id=1, source_target_pairs={{0,24},{4,28},{8,16},{12,20},{16,8},{20,12},{24,0},{28,4},{1,25},{... | collective-permute-start | bytes 294920 | tf_op jit(solution)/shard_map/ppermute | solution.py:786
  103.5 2.0 %collective-permute-done.13 = bf16[4,48,256]{2,1,0:T(8,128)(2,1)S(1)} collective-permute-done((bf16[4,48,256]{2,1,0:T(8,128)(2,1)}, bf16[4,48,256]{2,1,0:T(8,128)(2,1)S(1)}, u32[]{:S(2)}, u32[]{:S(2)}) %collective-permute-start.13) | collective-permute-done | bytes 98336 | tf_op jit(solution)/shard_map/ppermute | solution.py:786
  105.5 1.5 %collective-permute-start.9 = (bf16[4,112,256]{2,1,0:T(8,128)(2,1)}, bf16[4,112,256]{2,1,0:T(8,128)(2,1)S(1)}, u32[]{:S(2)}, u32[]{:S(2)}) collective-permute-start(bf16[4,112,256]{2,1,0:T(8,128)(2,1)} %get-tuple-element.84), channel_id=1, source_target_pairs={{0,3},{1,2},{2,1},{3,0},{4,7},{5,6},{6,5},{7,4},{8,11},{9,10},{10,... | collective-permute-start | bytes 688136 | tf_op jit(solution)/shard_map/ppermute | solution.py:786
  107.0 5.0 %input_gradient.1 = bf16[1024,256]{1,0:T(8,128)(2,1)} custom-call(s32[1,1024]{1,0:T(1,128)} %bitcast.38, bf16[1024,768]{1,0:T(8,128)(2,1)} %get-tuple-element.78.dqkv_ref, f32[256,1024]{1,0:T(8,128)} %get-tuple-element.79.skp_ref, bf16[1024,768]{1,0:T(8,128)(2,1)} %get-tuple-element.80.types_ref), custom_call_target="tpu_custom_call" | custom-call | flops 1610612736 | bytes 6291456 | tf_op jit(solution)/shard_map/input_gradient/pallas_call | solution.py:643
  112.0 0.1 collective-permute-start.16
  112.1 1.5 %collective-permute-start.18 = (bf16[48,256]{1,0:T(8,128)(2,1)S(1)}, bf16[48,256]{1,0:T(8,128)(2,1)S(1)}, u32[]{:S(2)}, u32[]{:S(2)}) collective-permute-start(bf16[48,256]{1,0:T(8,128)(2,1)S(1)} %get-tuple-element.114), channel_id=1, source_target_pairs={{0,3},{1,2},{2,1},{3,0},{4,7},{5,6},{6,5},{7,4},{8,11},{9,10},{10,... | collective-permute-start | bytes 73736 | tf_op jit(solution)/shard_map/ppermute | solution.py:786
  113.6 1.9 %collective-permute-start.17 = (bf16[48,256]{1,0:T(8,128)(2,1)S(1)}, bf16[48,256]{1,0:T(8,128)(2,1)S(1)}, u32[]{:S(2)}, u32[]{:S(2)}) collective-permute-start(bf16[48,256]{1,0:T(8,128)(2,1)S(1)} %get-tuple-element.115), channel_id=1, source_target_pairs={{0,2},{1,3},{2,0},{3,1},{4,6},{5,7},{6,4},{7,5},{8,10},{9,11},{10,... | collective-permute-start | bytes 73736 | tf_op jit(solution)/shard_map/ppermute | solution.py:786
  115.6 0.6 collective-permute-done.8
  116.2 0.1 fusion.3
  116.3 0.1 collective-permute-start.10
  116.4 1.0 collective-permute-start.12
  117.4 2.4 %collective-permute-start.11 = (bf16[112,256]{1,0:T(8,128)(2,1)S(1)}, bf16[112,256]{1,0:T(8,128)(2,1)S(1)}, u32[]{:S(2)}, u32[]{:S(2)}) collective-permute-start(bf16[112,256]{1,0:T(8,128)(2,1)S(1)} %get-tuple-element.112), channel_id=1, source_target_pairs={{0,16},{4,20},{8,24},{12,28},{16,0},{20,4},{24,8},{28,12},{1,17},{... | collective-permute-start | bytes 172040 | tf_op jit(solution)/shard_map/ppermute | solution.py:786
  119.9 0.9 collective-permute-done.10
  120.8 1.7 %collective-permute-done.12 = bf16[112,256]{1,0:T(8,128)(2,1)S(1)} collective-permute-done((bf16[112,256]{1,0:T(8,128)(2,1)S(1)}, bf16[112,256]{1,0:T(8,128)(2,1)S(1)}, u32[]{:S(2)}, u32[]{:S(2)}) %collective-permute-start.12) | collective-permute-done | bytes 57376 | tf_op jit(solution)/shard_map/ppermute | solution.py:786
  122.5 1.7 %collective-permute-done.11 = bf16[112,256]{1,0:T(8,128)(2,1)S(1)} collective-permute-done((bf16[112,256]{1,0:T(8,128)(2,1)S(1)}, bf16[112,256]{1,0:T(8,128)(2,1)S(1)}, u32[]{:S(2)}, u32[]{:S(2)}) %collective-permute-start.11) | collective-permute-done | bytes 57376 | tf_op jit(solution)/shard_map/ppermute | solution.py:786
  124.2 0.1 fusion.1
  124.3 1.8 %collective-permute-start.21 = (bf16[160,256]{1,0:T(8,128)(2,1)S(1)}, bf16[160,256]{1,0:T(8,128)(2,1)S(1)}, u32[]{:S(2)}, u32[]{:S(2)}) collective-permute-start(bf16[160,256]{1,0:T(8,128)(2,1)S(1)} %pad_maximum_fusion.refs_0_), channel_id=1, source_target_pairs={{0,24},{4,28},{8,16},{12,20},{16,8},{20,12},{24,0},{28,4},{1,25},{... | collective-permute-start | bytes 245768 | tf_op jit(solution)/shard_map/ppermute | solution.py:786
  126.1 2.6 %collective-permute-start.19 = (bf16[160,256]{1,0:T(8,128)(2,1)S(1)}, bf16[160,256]{1,0:T(8,128)(2,1)S(1)}, u32[]{:S(2)}, u32[]{:S(2)}) collective-permute-start(bf16[160,256]{1,0:T(8,128)(2,1)S(1)} %pad_maximum_fusion.refs_0_), channel_id=1, source_target_pairs={{0,8},{4,12},{8,0},{12,4},{16,24},{20,28},{24,16},{28,20},{1,9},{5... | collective-permute-start | bytes 245768 | tf_op jit(solution)/shard_map/ppermute | solution.py:786
  128.8 1.9 %collective-permute-done.21.refs_3_ = bf16[160,256]{1,0:T(8,128)(2,1)S(1)} collective-permute-done((bf16[160,256]{1,0:T(8,128)(2,1)S(1)}, bf16[160,256]{1,0:T(8,128)(2,1)S(1)}, u32[]{:S(2)}, u32[]{:S(2)}) %collective-permute-start.21) | collective-permute-done | bytes 81952 | tf_op jit(solution)/shard_map/ppermute | solution.py:786
  130.6 1.7 %collective-permute-done.20.refs_2_ = bf16[160,256]{1,0:T(8,128)(2,1)S(1)} collective-permute-done((bf16[160,256]{1,0:T(8,128)(2,1)S(1)}, bf16[160,256]{1,0:T(8,128)(2,1)S(1)}, u32[]{:S(2)}, u32[]{:S(2)}) %collective-permute-start.20) | collective-permute-done | bytes 81952 | tf_op jit(solution)/shard_map/ppermute | solution.py:786
  132.4 0.5 collective-permute-start.23
  132.9 0.7 collective-permute-done.24.refs_6_
  133.6 0.2 collective-permute-done.23.refs_5_
  133.8 0.4 copy-done.8
  134.3 0.2 copy-done.9
  134.4 5.3 %update.1 = (f32[256,1024]{1,0:T(8,128)}, f32[256,1024]{1,0:T(8,128)}, f32[256,1024]{1,0:T(8,128)}, f32[256,1024]{1,0:T(8,128)}, f32[64,768]{1,0:T(8,128)}, /*in...) custom-call(bf16[160,256]{1,0:T(8,128)(2,1)} %copy-done, ...), custom_call_target="tpu_custom_call" | custom-call | tf_op jit(solution)/shard_map/update/pallas_call | solution.py:761
  (48 shorter events, 0.2 us)
Async XLA Ops:
  2.6 19.2 %collective-permute-start.2 = (bf16[160,1024]{1,0:T(8,128)(2,1)}, bf16[160,1024]{1,0:T(8,128)(2,1)S(1)}, u32[]{:S(2)}, u32[]{:S(2)}) collective-permute-start(bf16[160,1024]{1,0:T(8,128)(2,1)} %pack_half.1), channel_id=1, source_target_pairs={{0,3},{1,2},{2,1},{3,0},{4,7},{5,6},{6,5},{7,4},{8,11},{9,10},{10,... | collective-permute-start | bytes 983048 | tf_op jit(solution)/shard_map/ppermute | solution.py:786
  6.5 15.3 %collective-permute-start.1 = (bf16[160,1024]{1,0:T(8,128)(2,1)}, bf16[160,1024]{1,0:T(8,128)(2,1)S(1)}, u32[]{:S(2)}, u32[]{:S(2)}) collective-permute-start(bf16[160,1024]{1,0:T(8,128)(2,1)} %pack_half.1), channel_id=1, source_target_pairs={{0,2},{1,3},{2,0},{3,1},{4,6},{5,7},{6,4},{7,5},{8,10},{9,11},{10,... | collective-permute-start | bytes 983048 | tf_op jit(solution)/shard_map/ppermute | solution.py:786
  7.0 14.7 %collective-permute-start = (bf16[160,1024]{1,0:T(8,128)(2,1)}, bf16[160,1024]{1,0:T(8,128)(2,1)S(1)}, u32[]{:S(2)}, u32[]{:S(2)}) collective-permute-start(bf16[160,1024]{1,0:T(8,128)(2,1)} %pack_half.1), channel_id=1, source_target_pairs={{0,1},{1,0},{2,3},{3,2},{4,5},{5,4},{6,7},{7,6},{8,9},{9,8},{10,11... | collective-permute-start | bytes 983048 | tf_op jit(solution)/shard_map/ppermute | solution.py:786
  21.7 3.6 %copy-start.12 = (bf16[160,1024]{1,0:T(8,128)(2,1)}, bf16[160,1024]{1,0:T(8,128)(2,1)S(1)}, u32[]{:S(2)}) copy-start(bf16[160,1024]{1,0:T(8,128)(2,1)S(1)} %collective-permute-done.refs_9_) | copy-start | bytes 983044
  21.7 3.6 %copy-start.10 = (bf16[160,1024]{1,0:T(8,128)(2,1)}, bf16[160,1024]{1,0:T(8,128)(2,1)S(1)}, u32[]{:S(2)}) copy-start(bf16[160,1024]{1,0:T(8,128)(2,1)S(1)} %collective-permute-done.2.refs_11_) | copy-start | bytes 983044
  21.7 1.7 %collective-permute-start.5 = (bf16[160,1024]{1,0:T(8,128)(2,1)S(1)}, bf16[160,1024]{1,0:T(8,128)(2,1)S(1)}, u32[]{:S(2)}, u32[]{:S(2)}) collective-permute-start(bf16[160,1024]{1,0:T(8,128)(2,1)S(1)} %collective-permute-done.2.refs_11_), channel_id=1, source_target_pairs={{0,4},{4,0},{8,12},{12,8},{16,20},{20,16},{24,28},{28,24},{1,5},{5... | collective-permute-start | bytes 983048 | tf_op jit(solution)/shard_map/ppermute | solution.py:786
  21.8 3.5 %copy-start.11 = (bf16[160,1024]{1,0:T(8,128)(2,1)}, bf16[160,1024]{1,0:T(8,128)(2,1)S(1)}, u32[]{:S(2)}) copy-start(bf16[160,1024]{1,0:T(8,128)(2,1)S(1)} %collective-permute-done.1.refs_10_) | copy-start | bytes 983044
  21.8 2.1 %collective-permute-start.4 = (bf16[160,1024]{1,0:T(8,128)(2,1)S(1)}, bf16[160,1024]{1,0:T(8,128)(2,1)S(1)}, u32[]{:S(2)}, u32[]{:S(2)}) collective-permute-start(bf16[160,1024]{1,0:T(8,128)(2,1)S(1)} %collective-permute-done.1.refs_10_), channel_id=1, source_target_pairs={{0,4},{4,0},{8,12},{12,8},{16,20},{20,16},{24,28},{28,24},{1,5},{5... | collective-permute-start | bytes 983048 | tf_op jit(solution)/shard_map/ppermute | solution.py:786
  22.3 2.0 %collective-permute-start.3 = (bf16[160,1024]{1,0:T(8,128)(2,1)S(1)}, bf16[160,1024]{1,0:T(8,128)(2,1)S(1)}, u32[]{:S(2)}, u32[]{:S(2)}) collective-permute-start(bf16[160,1024]{1,0:T(8,128)(2,1)S(1)} %collective-permute-done.refs_9_), channel_id=1, source_target_pairs={{0,4},{4,0},{8,12},{12,8},{16,20},{20,16},{24,28},{28,24},{1,5},{5... | collective-permute-start | bytes 983048 | tf_op jit(solution)/shard_map/ppermute | solution.py:786
  23.4 0.9 copy-start.13
  23.9 0.7 copy-start.14
  24.6 0.7 copy-start.15
  85.9 10.4 %collective-permute-start.6 = (bf16[4,4,160,256]{3,2,1,0:T(8,128)(2,1)}, bf16[4,4,160,256]{3,2,1,0:T(8,128)(2,1)}, u32[]{:S(2)}, u32[]{:S(2)}) collective-permute-start(bf16[4,4,160,256]{3,2,1,0:T(8,128)(2,1)} %get-tuple-element.73), channel_id=1, source_target_pairs={{0,4},{4,0},{8,12},{12,8},{16,20},{20,16},{24,28},{28,24},{1,5},{5... | collective-permute-start | bytes 3932168 | tf_op jit(solution)/shard_map/ppermute | solution.py:786
  99.0 6.5 %collective-permute-start.13 = (bf16[4,48,256]{2,1,0:T(8,128)(2,1)}, bf16[4,48,256]{2,1,0:T(8,128)(2,1)S(1)}, u32[]{:S(2)}, u32[]{:S(2)}) collective-permute-start(bf16[4,48,256]{2,1,0:T(8,128)(2,1)} %get-tuple-element.91), channel_id=1, source_target_pairs={{0,8},{4,12},{8,0},{12,4},{16,24},{20,28},{24,16},{28,20},{1,9},{5... | collective-permute-start | bytes 294920 | tf_op jit(solution)/shard_map/ppermute | solution.py:786
  99.1 12.8 %collective-permute-start.14 = (bf16[4,48,256]{2,1,0:T(8,128)(2,1)}, bf16[4,48,256]{2,1,0:T(8,128)(2,1)S(1)}, u32[]{:S(2)}, u32[]{:S(2)}) collective-permute-start(bf16[4,48,256]{2,1,0:T(8,128)(2,1)} %get-tuple-element.92), channel_id=1, source_target_pairs={{0,16},{4,20},{8,24},{12,28},{16,0},{20,4},{24,8},{28,12},{1,17},{... | collective-permute-start | bytes 294920 | tf_op jit(solution)/shard_map/ppermute | solution.py:786
  99.2 12.8 %collective-permute-start.15 = (bf16[4,48,256]{2,1,0:T(8,128)(2,1)}, bf16[4,48,256]{2,1,0:T(8,128)(2,1)S(1)}, u32[]{:S(2)}, u32[]{:S(2)}) collective-permute-start(bf16[4,48,256]{2,1,0:T(8,128)(2,1)} %get-tuple-element.93), channel_id=1, source_target_pairs={{0,24},{4,28},{8,16},{12,20},{16,8},{20,12},{24,0},{28,4},{1,25},{... | collective-permute-start | bytes 294920 | tf_op jit(solution)/shard_map/ppermute | solution.py:786
  103.5 10.1 %collective-permute-start.7 = (bf16[4,112,256]{2,1,0:T(8,128)(2,1)}, bf16[4,112,256]{2,1,0:T(8,128)(2,1)S(1)}, u32[]{:S(2)}, u32[]{:S(2)}) collective-permute-start(bf16[4,112,256]{2,1,0:T(8,128)(2,1)} %get-tuple-element.82), channel_id=1, source_target_pairs={{0,1},{1,0},{2,3},{3,2},{4,5},{5,4},{6,7},{7,6},{8,9},{9,8},{10,11... | collective-permute-start | bytes 688136 | tf_op jit(solution)/shard_map/ppermute | solution.py:786
  103.5 12.7 %collective-permute-start.8 = (bf16[4,112,256]{2,1,0:T(8,128)(2,1)}, bf16[4,112,256]{2,1,0:T(8,128)(2,1)S(1)}, u32[]{:S(2)}, u32[]{:S(2)}) collective-permute-start(bf16[4,112,256]{2,1,0:T(8,128)(2,1)} %get-tuple-element.83), channel_id=1, source_target_pairs={{0,2},{1,3},{2,0},{3,1},{4,6},{5,7},{6,4},{7,5},{8,10},{9,11},{10,... | collective-permute-start | bytes 688136 | tf_op jit(solution)/shard_map/ppermute | solution.py:786
  105.5 10.6 %collective-permute-start.9 = (bf16[4,112,256]{2,1,0:T(8,128)(2,1)}, bf16[4,112,256]{2,1,0:T(8,128)(2,1)S(1)}, u32[]{:S(2)}, u32[]{:S(2)}) collective-permute-start(bf16[4,112,256]{2,1,0:T(8,128)(2,1)} %get-tuple-element.84), channel_id=1, source_target_pairs={{0,3},{1,2},{2,1},{3,0},{4,7},{5,6},{6,5},{7,4},{8,11},{9,10},{10,... | collective-permute-start | bytes 688136 | tf_op jit(solution)/shard_map/ppermute | solution.py:786
  107.0 5.0 %copy-start.2 = (bf16[4,48,256]{2,1,0:T(8,128)(2,1)S(1)}, bf16[4,48,256]{2,1,0:T(8,128)(2,1)}, u32[]{:S(2)}) copy-start(bf16[4,48,256]{2,1,0:T(8,128)(2,1)} %get-tuple-element.90) | copy-start | bytes 294916
  107.0 9.2 %copy-start.1 = (bf16[4,112,256]{2,1,0:T(8,128)(2,1)S(1)}, bf16[4,112,256]{2,1,0:T(8,128)(2,1)}, u32[]{:S(2)}) copy-start(bf16[4,112,256]{2,1,0:T(8,128)(2,1)} %get-tuple-element.86) | copy-start | bytes 688132
  112.0 5.4 %collective-permute-start.16 = (bf16[48,256]{1,0:T(8,128)(2,1)S(1)}, bf16[48,256]{1,0:T(8,128)(2,1)S(1)}, u32[]{:S(2)}, u32[]{:S(2)}) collective-permute-start(bf16[48,256]{1,0:T(8,128)(2,1)S(1)} %get-tuple-element.113), channel_id=1, source_target_pairs={{0,1},{1,0},{2,3},{3,2},{4,5},{5,4},{6,7},{7,6},{8,9},{9,8},{10,11... | collective-permute-start | bytes 73736 | tf_op jit(solution)/shard_map/ppermute | solution.py:786
  112.1 7.8 %collective-permute-start.18 = (bf16[48,256]{1,0:T(8,128)(2,1)S(1)}, bf16[48,256]{1,0:T(8,128)(2,1)S(1)}, u32[]{:S(2)}, u32[]{:S(2)}) collective-permute-start(bf16[48,256]{1,0:T(8,128)(2,1)S(1)} %get-tuple-element.114), channel_id=1, source_target_pairs={{0,3},{1,2},{2,1},{3,0},{4,7},{5,6},{6,5},{7,4},{8,11},{9,10},{10,... | collective-permute-start | bytes 73736 | tf_op jit(solution)/shard_map/ppermute | solution.py:786
  113.6 6.2 %collective-permute-start.17 = (bf16[48,256]{1,0:T(8,128)(2,1)S(1)}, bf16[48,256]{1,0:T(8,128)(2,1)S(1)}, u32[]{:S(2)}, u32[]{:S(2)}) collective-permute-start(bf16[48,256]{1,0:T(8,128)(2,1)S(1)} %get-tuple-element.115), channel_id=1, source_target_pairs={{0,2},{1,3},{2,0},{3,1},{4,6},{5,7},{6,4},{7,5},{8,10},{9,11},{10,... | collective-permute-start | bytes 73736 | tf_op jit(solution)/shard_map/ppermute | solution.py:786
  116.3 4.5 %collective-permute-start.10 = (bf16[112,256]{1,0:T(8,128)(2,1)S(1)}, bf16[112,256]{1,0:T(8,128)(2,1)S(1)}, u32[]{:S(2)}, u32[]{:S(2)}) collective-permute-start(bf16[112,256]{1,0:T(8,128)(2,1)S(1)} %get-tuple-element.110), channel_id=1, source_target_pairs={{0,8},{4,12},{8,0},{12,4},{16,24},{20,28},{24,16},{28,20},{1,9},{5... | collective-permute-start | bytes 172040 | tf_op jit(solution)/shard_map/ppermute | solution.py:786
  116.4 6.1 %collective-permute-start.12 = (bf16[112,256]{1,0:T(8,128)(2,1)S(1)}, bf16[112,256]{1,0:T(8,128)(2,1)S(1)}, u32[]{:S(2)}, u32[]{:S(2)}) collective-permute-start(bf16[112,256]{1,0:T(8,128)(2,1)S(1)} %get-tuple-element.111), channel_id=1, source_target_pairs={{0,24},{4,28},{8,16},{12,20},{16,8},{20,12},{24,0},{28,4},{1,25},{... | collective-permute-start | bytes 172040 | tf_op jit(solution)/shard_map/ppermute | solution.py:786
  117.4 6.8 %collective-permute-start.11 = (bf16[112,256]{1,0:T(8,128)(2,1)S(1)}, bf16[112,256]{1,0:T(8,128)(2,1)S(1)}, u32[]{:S(2)}, u32[]{:S(2)}) collective-permute-start(bf16[112,256]{1,0:T(8,128)(2,1)S(1)} %get-tuple-element.112), channel_id=1, source_target_pairs={{0,16},{4,20},{8,24},{12,28},{16,0},{20,4},{24,8},{28,12},{1,17},{... | collective-permute-start | bytes 172040 | tf_op jit(solution)/shard_map/ppermute | solution.py:786
  124.3 9.5 %copy-start = (bf16[160,256]{1,0:T(8,128)(2,1)}, bf16[160,256]{1,0:T(8,128)(2,1)S(1)}, u32[]{:S(2)}) copy-start(bf16[160,256]{1,0:T(8,128)(2,1)S(1)} %pad_maximum_fusion.refs_0_) | copy-start | bytes 245764
  124.3 6.3 %collective-permute-start.21 = (bf16[160,256]{1,0:T(8,128)(2,1)S(1)}, bf16[160,256]{1,0:T(8,128)(2,1)S(1)}, u32[]{:S(2)}, u32[]{:S(2)}) collective-permute-start(bf16[160,256]{1,0:T(8,128)(2,1)S(1)} %pad_maximum_fusion.refs_0_), channel_id=1, source_target_pairs={{0,24},{4,28},{8,16},{12,20},{16,8},{20,12},{24,0},{28,4},{1,25},{... | collective-permute-start | bytes 245768 | tf_op jit(solution)/shard_map/ppermute | solution.py:786
  126.1 6.2 %collective-permute-start.20 = (bf16[160,256]{1,0:T(8,128)(2,1)S(1)}, bf16[160,256]{1,0:T(8,128)(2,1)S(1)}, u32[]{:S(2)}, u32[]{:S(2)}) collective-permute-start(bf16[160,256]{1,0:T(8,128)(2,1)S(1)} %pad_maximum_fusion.refs_0_), channel_id=1, source_target_pairs={{0,16},{4,20},{8,24},{12,28},{16,0},{20,4},{24,8},{28,12},{1,17},{... | collective-permute-start | bytes 245768 | tf_op jit(solution)/shard_map/ppermute | solution.py:786
  126.1 6.2 %collective-permute-start.19 = (bf16[160,256]{1,0:T(8,128)(2,1)S(1)}, bf16[160,256]{1,0:T(8,128)(2,1)S(1)}, u32[]{:S(2)}, u32[]{:S(2)}) collective-permute-start(bf16[160,256]{1,0:T(8,128)(2,1)S(1)} %pad_maximum_fusion.refs_0_), channel_id=1, source_target_pairs={{0,8},{4,12},{8,0},{12,4},{16,24},{20,28},{24,16},{28,20},{1,9},{5... | collective-permute-start | bytes 245768 | tf_op jit(solution)/shard_map/ppermute | solution.py:786
  128.8 4.1 %collective-permute-start.22 = (bf16[160,256]{1,0:T(8,128)(2,1)S(1)}, bf16[160,256]{1,0:T(8,128)(2,1)S(1)}, u32[]{:S(2)}, u32[]{:S(2)}) collective-permute-start(bf16[160,256]{1,0:T(8,128)(2,1)S(1)} %pad_maximum_fusion.refs_0_), channel_id=1, source_target_pairs={{0,4},{4,0},{8,12},{12,8},{16,20},{20,16},{24,28},{28,24},{1,5},{5... | collective-permute-start | bytes 245768 | tf_op jit(solution)/shard_map/ppermute | solution.py:786
  130.6 3.2 %copy-start.3 = (bf16[160,256]{1,0:T(8,128)(2,1)}, bf16[160,256]{1,0:T(8,128)(2,1)S(1)}, u32[]{:S(2)}) copy-start(bf16[160,256]{1,0:T(8,128)(2,1)S(1)} %collective-permute-done.21.refs_3_) | copy-start | bytes 245764
  130.6 2.2 %collective-permute-start.25 = (bf16[160,256]{1,0:T(8,128)(2,1)S(1)}, bf16[160,256]{1,0:T(8,128)(2,1)S(1)}, u32[]{:S(2)}, u32[]{:S(2)}) collective-permute-start(bf16[160,256]{1,0:T(8,128)(2,1)S(1)} %collective-permute-done.21.refs_3_), channel_id=1, source_target_pairs={{0,4},{4,0},{8,12},{12,8},{16,20},{20,16},{24,28},{28,24},{1,5},{5... | collective-permute-start | bytes 245768 | tf_op jit(solution)/shard_map/ppermute | solution.py:786
  132.4 1.5 %copy-start.4 = (bf16[160,256]{1,0:T(8,128)(2,1)}, bf16[160,256]{1,0:T(8,128)(2,1)S(1)}, u32[]{:S(2)}) copy-start(bf16[160,256]{1,0:T(8,128)(2,1)S(1)} %collective-permute-done.20.refs_2_) | copy-start | bytes 245764
  132.4 1.3 collective-permute-start.24
  132.4 1.4 %copy-start.5 = (bf16[160,256]{1,0:T(8,128)(2,1)}, bf16[160,256]{1,0:T(8,128)(2,1)S(1)}, u32[]{:S(2)}) copy-start(bf16[160,256]{1,0:T(8,128)(2,1)S(1)} %collective-permute-done.19.refs_1_) | copy-start | bytes 245764
  132.4 1.4 %collective-permute-start.23 = (bf16[160,256]{1,0:T(8,128)(2,1)S(1)}, bf16[160,256]{1,0:T(8,128)(2,1)S(1)}, u32[]{:S(2)}, u32[]{:S(2)}) collective-permute-start(bf16[160,256]{1,0:T(8,128)(2,1)S(1)} %collective-permute-done.19.refs_1_), channel_id=1, source_target_pairs={{0,4},{4,0},{8,12},{12,8},{16,20},{20,16},{24,28},{28,24},{1,5},{5... | collective-permute-start | bytes 245768 | tf_op jit(solution)/shard_map/ppermute | solution.py:786
  132.9 0.9 copy-start.6
  132.9 0.9 copy-start.7
  133.6 0.6 copy-start.8
  133.8 0.6 copy-start.9

commit v5 on v4

--- a/solution.py
+++ b/solution.py
@@ -16,7 +16,7 @@
 NSUB = EC // SUB
 NC = 256
 NODE_STEPS = 4
-EDGES = REL * SLOTS + EC
+EDGES = REL * SLOTS
 bf16 = jnp.bfloat16
 f32 = jnp.float32
 norm_eps = 1e-5
@@ -154,7 +154,7 @@
     total = lax.fori_loop(0, REL, odd, paired)
     for extra in range(2 * NSUB):
         put(total + extra, 0, 0, 0)
-    return paired // NSUB, (total + NSUB - 1) // NSUB
+    return paired // NSUB, (total + NSUB - 1) // NSUB, total
 
 
 def rows_of(ref, lst_r, lst_o, c):
@@ -166,8 +166,8 @@
     return jnp.concatenate(pieces, axis=1)
 
 
-def place(c):
-    return pl.ds(pl.multiple_of(c * EC, EC), EC)
+def place(c, span=EC):
+    return pl.ds(pl.multiple_of(c * EC, EC), span)
 
 
 LISTS = [pltpu.SMEM((REL * SLOTS // SUB + 2 * NSUB,), jnp.int32)] * 3
@@ -236,7 +236,7 @@
 
 
 def before_kernel(cnt_ref, kinds_ref, src_ref, dst_ref, tim_ref, feat_ref, idx_ref, xg_ref, typ_ref, lst_r, lst_o, lst_c):
-    _, chunks = list_blocks(cnt_ref, lst_r, lst_o, lst_c)
+    _, chunks, _ = list_blocks(cnt_ref, lst_r, lst_o, lst_c)
     src = src_ref[...]
     for j in range(SLOTS // 128):
         idx = src[:, j * 128:(j + 1) * 128]
@@ -257,7 +257,12 @@
         xg_ref[:, place(c)] = nn(ft, one_hot_rows(src, N)).astype(bf16)
         return 0
 
-    lax.fori_loop(0, chunks, one, 0)
+    def two(c, _):
+        one(2 * c, 0)
+        one(2 * c + 1, 0)
+        return 0
+
+    lax.fori_loop(0, (chunks + 1) // 2, two, 0)
 
 
 def before(cnt, kinds, src, dst, tim, feat):
@@ -304,7 +309,7 @@
     cot_copy = pltpu.make_async_copy(cot_hbm, cot_ref, xsem.at[2])
 
     ident = eye()
-    whole, chunks = list_blocks(cnt_ref, lst_r, lst_o, lst_c)
+    whole, chunks, total = list_blocks(cnt_ref, lst_r, lst_o, lst_c)
 
     def row(c, k):
         return idx_ref[pl.ds(pl.multiple_of(c * 8, 8), 8), :][k:k + 1]
@@ -371,11 +376,11 @@
     wet = nt(ident, lay.get_edge(wpk, 512, 768)).astype(bf16)
     rte[...] = nt(wet, emb_ref[...]).astype(bf16)
 
-    def mu_of(c):
-        return jnp.concatenate([mu[lst_r[c * NSUB + k]] for k in range(NSUB)], axis=1)
-
-    def blocks_of(c, wide):
-        return [(lst_r[c * NSUB + k * (wide // SUB)], slice(k * wide, (k + 1) * wide)) for k in range(EC // wide)]
+    def mu_of(c, span):
+        return jnp.concatenate([mu[lst_r[c * NSUB + k]] for k in range(span // SUB)], axis=1)
+
+    def blocks_of(c, wide, span):
+        return [(lst_r[c * NSUB + k * (wide // SUB)], slice(k * wide, (k + 1) * wide)) for k in range(span // wide)]
 
     def lookup(c):
         rt = nn(rte[...], one_hot_rows(row(c, TIME), 256))
@@ -390,38 +395,50 @@
         xm = jnp.concatenate([jnp.where(cu == s, xe, zero) for s in range(TYPES)], axis=0)
         kve[:, place(c)] = nn(wt[D:3 * D, :], xm).astype(bf16)
 
-    def forward(wide, c, _):
-        at = place(c)
+    def forward(wide, more, c, _, span=EC):
+        at = place(c, span)
         kv_e = kve[:, at]
         q_e = qe[:, at].astype(f32)
         ks, ms = [], []
-        for r, sl in blocks_of(c, wide):
+        for r, sl in blocks_of(c, wide, span):
             ks.append(nn(bdat[r], kv_e[:D, sl]))
             ms.append(nn(bdmt[r], kv_e[D:, sl]))
         ka = jnp.concatenate(ks, axis=1)
         me_ = jnp.concatenate(ms, axis=1)
-        xe = lookup(c + 1)
+        xe = lookup(c + 1) if more else None
         xg[:, at] = ka.astype(bf16)
         msg[:, at] = me_.astype(bf16)
         raw = head_sum(ka * q_e)
         raws[:, at] = raw
         lanes = lax.broadcasted_iota(jnp.int32, (H, SUB), 1)
-        w = jnp.exp(raw * mu_of(c))
+        w = jnp.exp(raw * mu_of(c, span))
         w = jnp.concatenate(
-            [jnp.where(lanes < lst_c[c * NSUB + k], w[:, k * SUB:(k + 1) * SUB], 0.0) for k in range(NSUB)], axis=1
+            [jnp.where(lanes < lst_c[c * NSUB + k], w[:, k * SUB:(k + 1) * SUB], 0.0) for k in range(span // SUB)], axis=1
         )
         wexp[:, at] = w
         wm = (head_wide(w) * me_).astype(bf16)
-        lookup_q(c + 1)
-        num[...] += nt(jnp.concatenate([wm, hi_lo(w)], axis=0), one_hot_rows(row(c, TARGET), N))
-        project(c + 1, xe)
+        if more:
+            lookup_q(c + 1)
+        num[...] += nt(jnp.concatenate([wm, hi_lo(w)], axis=0), one_hot_rows(row(c, TARGET)[:, :span], N))
+        if more:
+            project(c + 1, xe)
         return 0
 
     xg_copy.wait()
     project(0, lookup(0))
     lookup_q(0)
-    lax.fori_loop(0, whole, functools.partial(forward, 2 * SUB), 0)
-    lax.fori_loop(whole, chunks, functools.partial(forward, SUB), 0)
+    whole, last = jnp.minimum(whole, chunks - 1), chunks - 1
+    lax.fori_loop(0, whole, functools.partial(forward, 2 * SUB, True), 0)
+    lax.fori_loop(whole, last, functools.partial(forward, SUB, True), 0)
+    few = total - last * NSUB <= NSUB // 2
+
+    @pl.when(few)
+    def _():
+        forward(SUB, False, last, 0, EC // 2)
+
+    @pl.when(jnp.logical_not(few))
+    def _():
+        forward(SUB, False, last, 0)
 
     cot_copy.wait()
     nwt = nt(ident, lay.get_norm(wpk)).astype(bf16)
@@ -487,28 +504,29 @@
     def gather_back(c):
         dn_buf[...] = nn(dnum[...], one_hot_rows(row(c, TARGET), N))
 
-    def scatter_back(c):
-        dkve = dkve_buf[...]
-        dqkv[:, D:] += nt(one_hot_rows(row(c, SOURCE), N), dkve)
-        dtkv[...] += nt(one_hot_rows(row(c, BUCKET), 1024), dkve)
-
-    def backward(wide, c, _):
-        at = place(c)
+    def scatter_back(c, span=EC):
+        dkve = dkve_buf[:, :span]
+        dqkv[:, D:] += nt(one_hot_rows(row(c, SOURCE)[:, :span], N), dkve)
+        dtkv[...] += nt(one_hot_rows(row(c, BUCKET)[:, :span], 1024), dkve)
+
+    def backward(wide, more, c, _, span=EC):
+        at = place(c, span)
         scatter_back(jnp.maximum(c - 1, 0))
-        dn_e = dn_buf[:D]
+        dn_e = dn_buf[:D, :span]
         w = wexp[:, at]
-        dw = head_sum(dn_e * msg[:, at].astype(f32)) + dn_buf[D:D + H] + dn_buf[D + H:]
+        dw = head_sum(dn_e * msg[:, at].astype(f32)) + dn_buf[D:D + H, :span] + dn_buf[D + H:, :span]
         ds = dw * w
         dsr = ds * raws[:, at]
-        ss = head_wide(ds * mu_of(c))
+        ss = head_wide(ds * mu_of(c, span))
         dka = (ss * qe[:, at].astype(f32)).astype(bf16)
         dms = (head_wide(w) * dn_e).astype(bf16)
         dqe = (ss * xg[:, at].astype(f32)).astype(bf16)
-        gather_back(c + 1)
-        for r, sl in blocks_of(c, wide):
+        if more:
+            gather_back(c + 1)
+        for r, sl in blocks_of(c, wide, span):
             dkve_buf[0:D, sl] = nn(bda[r], dka[:, sl]).astype(bf16)
             dkve_buf[D:, sl] = nn(bdm[r], dms[:, sl]).astype(bf16)
-        for r, sl in blocks_of(c, wide):
+        for r, sl in blocks_of(c, wide, span):
             at_k = pl.ds(pl.multiple_of(c * EC + sl.start, SUB), wide)
             gak = nt(kve[0:D, at_k], dka[:, sl])
             gmk = nt(kve[D:, at_k], dms[:, sl])
@@ -517,19 +535,29 @@
             gm[r, 0:128] += gmk[0:128, 0:128]
             gm[r, 128:] += gmk[128:, 128:]
             dmu[r] += sum(dsr[:, k:k + 128] for k in range(sl.start, sl.stop, 128))
-        dqkv[:, :D] += nt(one_hot_rows(row(c, TARGET), N), dqe)
+        dqkv[:, :D] += nt(one_hot_rows(row(c, TARGET)[:, :span], N), dqe)
         return 0
 
     gather_back(0)
     def backward_pair(c, _):
-        backward(2 * SUB, 2 * c, 0)
-        backward(2 * SUB, 2 * c + 1, 0)
+        backward(2 * SUB, True, 2 * c, 0)
+        backward(2 * SUB, True, 2 * c + 1, 0)
         return 0
 
     lax.fori_loop(0, whole // 2, backward_pair, 0)
-    lax.fori_loop(whole // 2 * 2, whole, functools.partial(backward, 2 * SUB), 0)
-    lax.fori_loop(whole, chunks, functools.partial(backward, SUB), 0)
-    scatter_back(chunks - 1)
+    lax.fori_loop(whole // 2 * 2, whole, functools.partial(backward, 2 * SUB, True), 0)
+    lax.fori_loop(whole, last, functools.partial(backward, SUB, True), 0)
+
+    @pl.when(few)
+    def _():
+        backward(SUB, False, last, 0, EC // 2)
+        scatter_back(last, EC // 2)
+
+    @pl.when(jnp.logical_not(few))
+    def _():
+        backward(SUB, False, last, 0)
+        scatter_back(last)
+
 
     low[...] = dqkv[...].astype(bf16)
     last = pltpu.make_async_copy(low, dqkv_ref, osem.at[2])

time: 140 us -> 138 us (0.986)
  Pallas kernels: 87.5 us -> 84.5 us
    pallas_call x1, Pallas kernels: 60.5 us -> 58.9 us  [layer(): pl.pallas_call(functools.partial(layer_kernel, lay), out_shape=[S((N, D),...]
  transfers between devices with their start and end apart: 26 -> 26, of which waited for: 14 -> 13; matrix products, arithmetic and copies ran while one was open for 0% -> 0% of each run, Pallas kernels for 12% -> 11%
where the time goes in v5:
time: 138 us; the launch traced here: 139 us
  Pallas kernels  84.5 us (61%)
  starting transfers between devices  31.8 us (23%)
  waiting for transfers between devices  19.4 us (14%)
  between operations  1.68 us (1%)
  local copies, waits for them, and re-layouts  1.62 us (1%)
    pallas_call x1, Pallas kernels, layer(): pl.pallas_call(functools.partial(layer_kernel, lay), out_shape=[S((N, D),...  58.9 us
    ppermute x26, starting transfers between devices, swap(): return lax.ppermute(x, axis, [(i, i ^ mask) for i in range(size)])  31.8 us
    ppermute x26, waiting for transfers between devices, swap(): return lax.ppermute(x, axis, [(i, i ^ mask) for i in range(size)])  19.4 us
    pallas_call x1, Pallas kernels, before(): pl.pallas_call(before_kernel, out_shape=(S((EDGES // EC * 8, EC), jnp.int...  8.47 us
    pallas_call x1, Pallas kernels, update(): pl.pallas_call(functools.partial(update_kernel, jobs, len(states)), out_s...  5.32 us
    pallas_call x1, Pallas kernels, input_gradient(): pl.pallas_call(input_kernel, out_shape=S((N, D), bf16), compiler_params=p...  4.95 us
  transfers between devices with their start and end apart: 26, of which 13 were waited for; matrix products, arithmetic and copies ran while one was open for 0% of the time, Pallas kernels for 11%

profile of v5, /device:TPU:0, one launch (start us, length us, event | category | flops | bytes accessed | tf_op | source)
XLA Modules:
  0.0 139.3 jit_solution(4693461830924248666)
XLA Ops:
  0.7 1.9 %pack_half.1 = bf16[160,1024]{1,0:T(8,128)(2,1)} custom-call(f32[256,1024]{1,0:T(8,128)} %refs_8_.1, f32[64,768]{1,0:T(8,128)} %refs_12_.1, f32[8,64]{1,0:T(8,128)} %refs_16_.1), custom_call_target="tpu_custom_call" | custom-call | tf_op jit(solution)/shard_map/pack_half/pallas_call | solution.py:208
  2.6 4.0 %collective-permute-start.2 = (bf16[160,1024]{1,0:T(8,128)(2,1)}, bf16[160,1024]{1,0:T(8,128)(2,1)S(1)}, u32[]{:S(2)}, u32[]{:S(2)}) collective-permute-start(bf16[160,1024]{1,0:T(8,128)(2,1)} %pack_half.1), channel_id=1, source_target_pairs={{0,3},{1,2},{2,1},{3,0},{4,7},{5,6},{6,5},{7,4},{8,11},{9,10},{10,... | collective-permute-start | bytes 983048 | tf_op jit(solution)/shard_map/ppermute | solution.py:814
  6.5 0.5 collective-permute-start.1
  7.0 0.1 collective-permute-start
  7.2 2.2 %pack.1.refs_8_ = bf16[320,1024]{1,0:T(8,128)(2,1)} custom-call(f32[256,1024]{1,0:T(8,128)} %refs_8_.1, f32[64,768]{1,0:T(8,128)} %refs_12_.1, f32[8,64]{1,0:T(8,128)} %refs_16_.1), custom_call_target="tpu_custom_call" | custom-call | tf_op jit(solution)/shard_map/pack/pallas_call | solution.py:230
  9.4 8.5 %before.1 = (s32[128,512]{1,0:T(8,128)}, bf16[256,8192]{1,0:T(8,128)(2,1)}) custom-call(s32[8]{0:T(128)} %refs_1_.1, s32[1,1024]{1,0:T(1,128)} %bitcast.36, s32[8,1024]{1,0:T(8,128)} %src_ref.1, s32[8,1024]{1,0:T(8,128)} %dst_ref.1, s32[8,1024]{1,0:T(8,128)} %tim_ref.1, bf16[1024,256]{1,0:T(8,128)(2,1)} %refs_7_.1), custom_call_target="tpu_custom_call" | custom-call | flops 4294967296 | bytes 6291456 | tf_op jit(solution)/shard_map/before/pallas_call | solution.py:269
  17.9 3.9 %collective-permute-done.refs_9_ = bf16[160,1024]{1,0:T(8,128)(2,1)S(1)} collective-permute-done((bf16[160,1024]{1,0:T(8,128)(2,1)}, bf16[160,1024]{1,0:T(8,128)(2,1)S(1)}, u32[]{:S(2)}, u32[]{:S(2)}) %collective-permute-start) | collective-permute-done | bytes 327712 | tf_op jit(solution)/shard_map/ppermute | solution.py:814
  21.7 0.1 collective-permute-start.5
  21.8 0.5 collective-permute-start.4
  22.3 0.1 collective-permute-start.3
  23.1 0.4 collective-permute-done.5.refs_14_
  23.4 0.5 collective-permute-done.4.refs_13_
  23.9 0.5 collective-permute-done.3.refs_12_
  24.4 0.3 copy-done.14
  24.6 0.7 copy-done.15
  25.4 58.9 %layer.1 = (bf16[1024,256]{1,0:T(8,128)(2,1)}, bf16[1024,768]{1,0:T(8,128)(2,1)}, f32[256,1024]{1,0:T(8,128)}, bf16[1024,768]{1,0:T(8,128)(2,1)}, bf16[4,4,160,2...) custom-call(s32[1]{0:T(128)S(6)} %copy.43.refs_0_, s32[8]{0:T(128)} %refs_1_.1, s32[1,1024]{1,0:T(1,128)} %bitcast.37, ...), custom_call_target="tpu_custom_call" | custom-call | flops 60000002048 | bytes 16777216 | tf_op jit(solution)/shard_map/layer/pallas_call | solution.py:637
  84.3 0.8 collective-permute-start.6
  85.1 3.0 %collective-permute-done.6.got_ref = bf16[4,4,160,256]{3,2,1,0:T(8,128)(2,1)} collective-permute-done((bf16[4,4,160,256]{3,2,1,0:T(8,128)(2,1)}, bf16[4,4,160,256]{3,2,1,0:T(8,128)(2,1)}, u32[]{:S(2)}, u32[]{:S(2)}) %collective-permute-start.6) | collective-permute-done | bytes 1310752 | tf_op jit(solution)/shard_map/ppermute | solution.py:814
  88.1 2.7 %add_core.1 = (bf16[4,112,256]{2,1,0:T(8,128)(2,1)}, bf16[4,112,256]{2,1,0:T(8,128)(2,1)}, bf16[4,112,256]{2,1,0:T(8,128)(2,1)}, bf16[4,48,256]{2,1,0:T(8,128)(2...) custom-call(bf16[4,4,160,256]{3,2,1,0:T(8,128)(2,1)} %get-tuple-elem, ...), custom_call_target="tpu_custom_call" | custom-call | tf_op jit(solution)/shard_map/add_core/pallas_call | solution.py:715
  90.8 0.1 collective-permute-start.13
  90.9 0.1 collective-permute-start.14
  91.0 4.3 %collective-permute-start.15 = (bf16[4,48,256]{2,1,0:T(8,128)(2,1)}, bf16[4,48,256]{2,1,0:T(8,128)(2,1)S(1)}, u32[]{:S(2)}, u32[]{:S(2)}) collective-permute-start(bf16[4,48,256]{2,1,0:T(8,128)(2,1)} %get-tuple-element.93), channel_id=1, source_target_pairs={{0,24},{4,28},{8,16},{12,20},{16,8},{20,12},{24,0},{28,4},{1,25},{... | collective-permute-start | bytes 294920 | tf_op jit(solution)/shard_map/ppermute | solution.py:814
  95.3 3.9 %collective-permute-start.7 = (bf16[4,112,256]{2,1,0:T(8,128)(2,1)}, bf16[4,112,256]{2,1,0:T(8,128)(2,1)S(1)}, u32[]{:S(2)}, u32[]{:S(2)}) collective-permute-start(bf16[4,112,256]{2,1,0:T(8,128)(2,1)} %get-tuple-element.82), channel_id=1, source_target_pairs={{0,1},{1,0},{2,3},{3,2},{4,5},{5,4},{6,7},{7,6},{8,9},{9,8},{10,11... | collective-permute-start | bytes 688136 | tf_op jit(solution)/shard_map/ppermute | solution.py:814
  99.2 3.9 %collective-permute-start.8 = (bf16[4,112,256]{2,1,0:T(8,128)(2,1)}, bf16[4,112,256]{2,1,0:T(8,128)(2,1)S(1)}, u32[]{:S(2)}, u32[]{:S(2)}) collective-permute-start(bf16[4,112,256]{2,1,0:T(8,128)(2,1)} %get-tuple-element.83), channel_id=1, source_target_pairs={{0,2},{1,3},{2,0},{3,1},{4,6},{5,7},{6,4},{7,5},{8,10},{9,11},{10,... | collective-permute-start | bytes 688136 | tf_op jit(solution)/shard_map/ppermute | solution.py:814
  103.1 1.5 %collective-permute-start.9 = (bf16[4,112,256]{2,1,0:T(8,128)(2,1)}, bf16[4,112,256]{2,1,0:T(8,128)(2,1)S(1)}, u32[]{:S(2)}, u32[]{:S(2)}) collective-permute-start(bf16[4,112,256]{2,1,0:T(8,128)(2,1)} %get-tuple-element.84), channel_id=1, source_target_pairs={{0,3},{1,2},{2,1},{3,0},{4,7},{5,6},{6,5},{7,4},{8,11},{9,10},{10,... | collective-permute-start | bytes 688136 | tf_op jit(solution)/shard_map/ppermute | solution.py:814
  104.6 5.0 %input_gradient.1 = bf16[1024,256]{1,0:T(8,128)(2,1)} custom-call(s32[1,1024]{1,0:T(1,128)} %bitcast.38, bf16[1024,768]{1,0:T(8,128)(2,1)} %get-tuple-element.78.dqkv_ref, f32[256,1024]{1,0:T(8,128)} %get-tuple-element.79.skp_ref, bf16[1024,768]{1,0:T(8,128)(2,1)} %get-tuple-element.80.types_ref), custom_call_target="tpu_custom_call" | custom-call | flops 1610612736 | bytes 6291456 | tf_op jit(solution)/shard_map/input_gradient/pallas_call | solution.py:671
  109.6 1.0 collective-permute-start.16
  110.6 1.7 %collective-permute-start.18 = (bf16[48,256]{1,0:T(8,128)(2,1)S(1)}, bf16[48,256]{1,0:T(8,128)(2,1)S(1)}, u32[]{:S(2)}, u32[]{:S(2)}) collective-permute-start(bf16[48,256]{1,0:T(8,128)(2,1)S(1)} %get-tuple-element.114), channel_id=1, source_target_pairs={{0,3},{1,2},{2,1},{3,0},{4,7},{5,6},{6,5},{7,4},{8,11},{9,10},{10,... | collective-permute-start | bytes 73736 | tf_op jit(solution)/shard_map/ppermute | solution.py:814
  112.3 0.9 collective-permute-start.17
  113.2 1.1 collective-permute-done.9
  114.3 0.1 fusion.3
  114.3 0.1 collective-permute-start.10
  114.4 0.7 collective-permute-start.12
  115.2 2.7 %collective-permute-start.11 = (bf16[112,256]{1,0:T(8,128)(2,1)S(1)}, bf16[112,256]{1,0:T(8,128)(2,1)S(1)}, u32[]{:S(2)}, u32[]{:S(2)}) collective-permute-start(bf16[112,256]{1,0:T(8,128)(2,1)S(1)} %get-tuple-element.112), channel_id=1, source_target_pairs={{0,16},{4,20},{8,24},{12,28},{16,0},{20,4},{24,8},{28,12},{1,17},{... | collective-permute-start | bytes 172040 | tf_op jit(solution)/shard_map/ppermute | solution.py:814
  117.9 0.6 collective-permute-done.10
  118.6 2.0 %collective-permute-done.12 = bf16[112,256]{1,0:T(8,128)(2,1)S(1)} collective-permute-done((bf16[112,256]{1,0:T(8,128)(2,1)S(1)}, bf16[112,256]{1,0:T(8,128)(2,1)S(1)}, u32[]{:S(2)}, u32[]{:S(2)}) %collective-permute-start.12) | collective-permute-done | bytes 57376 | tf_op jit(solution)/shard_map/ppermute | solution.py:814
  120.6 3.7 %collective-permute-done.11 = bf16[112,256]{1,0:T(8,128)(2,1)S(1)} collective-permute-done((bf16[112,256]{1,0:T(8,128)(2,1)S(1)}, bf16[112,256]{1,0:T(8,128)(2,1)S(1)}, u32[]{:S(2)}, u32[]{:S(2)}) %collective-permute-start.11) | collective-permute-done | bytes 57376 | tf_op jit(solution)/shard_map/ppermute | solution.py:814
  124.3 0.1 fusion.1
  124.4 0.2 collective-permute-start.21
  124.6 4.3 %collective-permute-start.19 = (bf16[160,256]{1,0:T(8,128)(2,1)S(1)}, bf16[160,256]{1,0:T(8,128)(2,1)S(1)}, u32[]{:S(2)}, u32[]{:S(2)}) collective-permute-start(bf16[160,256]{1,0:T(8,128)(2,1)S(1)} %pad_maximum_fusion.refs_0_), channel_id=1, source_target_pairs={{0,8},{4,12},{8,0},{12,4},{16,24},{20,28},{24,16},{28,20},{1,9},{5... | collective-permute-start | bytes 245768 | tf_op jit(solution)/shard_map/ppermute | solution.py:814
  128.8 2.0 %collective-permute-done.21.refs_3_ = bf16[160,256]{1,0:T(8,128)(2,1)S(1)} collective-permute-done((bf16[160,256]{1,0:T(8,128)(2,1)S(1)}, bf16[160,256]{1,0:T(8,128)(2,1)S(1)}, u32[]{:S(2)}, u32[]{:S(2)}) %collective-permute-start.21) | collective-permute-done | bytes 81952 | tf_op jit(solution)/shard_map/ppermute | solution.py:814
  130.8 0.8 collective-permute-done.20.refs_2_
  131.7 0.5 collective-permute-start.23
  132.2 0.7 collective-permute-done.24.refs_6_
  133.0 0.2 collective-permute-done.23.refs_5_
  133.2 0.4 copy-done.8
  133.6 0.2 copy-done.9
  133.8 5.3 %update.1 = (f32[256,1024]{1,0:T(8,128)}, f32[256,1024]{1,0:T(8,128)}, f32[256,1024]{1,0:T(8,128)}, f32[256,1024]{1,0:T(8,128)}, f32[64,768]{1,0:T(8,128)}, /*in...) custom-call(bf16[160,256]{1,0:T(8,128)(2,1)} %copy-done, ...), custom_call_target="tpu_custom_call" | custom-call | tf_op jit(solution)/shard_map/update/pallas_call | solution.py:789
  (48 shorter events, 0.2 us)
Async XLA Ops:
  2.6 19.2 %collective-permute-start.2 = (bf16[160,1024]{1,0:T(8,128)(2,1)}, bf16[160,1024]{1,0:T(8,128)(2,1)S(1)}, u32[]{:S(2)}, u32[]{:S(2)}) collective-permute-start(bf16[160,1024]{1,0:T(8,128)(2,1)} %pack_half.1), channel_id=1, source_target_pairs={{0,3},{1,2},{2,1},{3,0},{4,7},{5,6},{6,5},{7,4},{8,11},{9,10},{10,... | collective-permute-start | bytes 983048 | tf_op jit(solution)/shard_map/ppermute | solution.py:814
  6.5 15.3 %collective-permute-start.1 = (bf16[160,1024]{1,0:T(8,128)(2,1)}, bf16[160,1024]{1,0:T(8,128)(2,1)S(1)}, u32[]{:S(2)}, u32[]{:S(2)}) collective-permute-start(bf16[160,1024]{1,0:T(8,128)(2,1)} %pack_half.1), channel_id=1, source_target_pairs={{0,2},{1,3},{2,0},{3,1},{4,6},{5,7},{6,4},{7,5},{8,10},{9,11},{10,... | collective-permute-start | bytes 983048 | tf_op jit(solution)/shard_map/ppermute | solution.py:814
  7.0 14.7 %collective-permute-start = (bf16[160,1024]{1,0:T(8,128)(2,1)}, bf16[160,1024]{1,0:T(8,128)(2,1)S(1)}, u32[]{:S(2)}, u32[]{:S(2)}) collective-permute-start(bf16[160,1024]{1,0:T(8,128)(2,1)} %pack_half.1), channel_id=1, source_target_pairs={{0,1},{1,0},{2,3},{3,2},{4,5},{5,4},{6,7},{7,6},{8,9},{9,8},{10,11... | collective-permute-start | bytes 983048 | tf_op jit(solution)/shard_map/ppermute | solution.py:814
  21.7 3.6 %copy-start.12 = (bf16[160,1024]{1,0:T(8,128)(2,1)}, bf16[160,1024]{1,0:T(8,128)(2,1)S(1)}, u32[]{:S(2)}) copy-start(bf16[160,1024]{1,0:T(8,128)(2,1)S(1)} %collective-permute-done.refs_9_) | copy-start | bytes 983044
  21.7 3.6 %copy-start.10 = (bf16[160,1024]{1,0:T(8,128)(2,1)}, bf16[160,1024]{1,0:T(8,128)(2,1)S(1)}, u32[]{:S(2)}) copy-start(bf16[160,1024]{1,0:T(8,128)(2,1)S(1)} %collective-permute-done.2.refs_11_) | copy-start | bytes 983044
  21.7 1.7 %collective-permute-start.5 = (bf16[160,1024]{1,0:T(8,128)(2,1)S(1)}, bf16[160,1024]{1,0:T(8,128)(2,1)S(1)}, u32[]{:S(2)}, u32[]{:S(2)}) collective-permute-start(bf16[160,1024]{1,0:T(8,128)(2,1)S(1)} %collective-permute-done.2.refs_11_), channel_id=1, source_target_pairs={{0,4},{4,0},{8,12},{12,8},{16,20},{20,16},{24,28},{28,24},{1,5},{5... | collective-permute-start | bytes 983048 | tf_op jit(solution)/shard_map/ppermute | solution.py:814
  21.8 3.5 %copy-start.11 = (bf16[160,1024]{1,0:T(8,128)(2,1)}, bf16[160,1024]{1,0:T(8,128)(2,1)S(1)}, u32[]{:S(2)}) copy-start(bf16[160,1024]{1,0:T(8,128)(2,1)S(1)} %collective-permute-done.1.refs_10_) | copy-start | bytes 983044
  21.8 2.1 %collective-permute-start.4 = (bf16[160,1024]{1,0:T(8,128)(2,1)S(1)}, bf16[160,1024]{1,0:T(8,128)(2,1)S(1)}, u32[]{:S(2)}, u32[]{:S(2)}) collective-permute-start(bf16[160,1024]{1,0:T(8,128)(2,1)S(1)} %collective-permute-done.1.refs_10_), channel_id=1, source_target_pairs={{0,4},{4,0},{8,12},{12,8},{16,20},{20,16},{24,28},{28,24},{1,5},{5... | collective-permute-start | bytes 983048 | tf_op jit(solution)/shard_map/ppermute | solution.py:814
  22.3 2.0 %collective-permute-start.3 = (bf16[160,1024]{1,0:T(8,128)(2,1)S(1)}, bf16[160,1024]{1,0:T(8,128)(2,1)S(1)}, u32[]{:S(2)}, u32[]{:S(2)}) collective-permute-start(bf16[160,1024]{1,0:T(8,128)(2,1)S(1)} %collective-permute-done.refs_9_), channel_id=1, source_target_pairs={{0,4},{4,0},{8,12},{12,8},{16,20},{20,16},{24,28},{28,24},{1,5},{5... | collective-permute-start | bytes 983048 | tf_op jit(solution)/shard_map/ppermute | solution.py:814
  23.4 0.9 copy-start.13
  23.9 0.7 copy-start.14
  24.6 0.7 copy-start.15
  84.3 3.8 %collective-permute-start.6 = (bf16[4,4,160,256]{3,2,1,0:T(8,128)(2,1)}, bf16[4,4,160,256]{3,2,1,0:T(8,128)(2,1)}, u32[]{:S(2)}, u32[]{:S(2)}) collective-permute-start(bf16[4,4,160,256]{3,2,1,0:T(8,128)(2,1)} %get-tuple-element.73), channel_id=1, source_target_pairs={{0,4},{4,0},{8,12},{12,8},{16,20},{20,16},{24,28},{28,24},{1,5},{5... | collective-permute-start | bytes 3932168 | tf_op jit(solution)/shard_map/ppermute | solution.py:814
  90.8 12.3 %collective-permute-start.13 = (bf16[4,48,256]{2,1,0:T(8,128)(2,1)}, bf16[4,48,256]{2,1,0:T(8,128)(2,1)S(1)}, u32[]{:S(2)}, u32[]{:S(2)}) collective-permute-start(bf16[4,48,256]{2,1,0:T(8,128)(2,1)} %get-tuple-element.91), channel_id=1, source_target_pairs={{0,8},{4,12},{8,0},{12,4},{16,24},{20,28},{24,16},{28,20},{1,9},{5... | collective-permute-start | bytes 294920 | tf_op jit(solution)/shard_map/ppermute | solution.py:814
  90.9 18.7 %collective-permute-start.14 = (bf16[4,48,256]{2,1,0:T(8,128)(2,1)}, bf16[4,48,256]{2,1,0:T(8,128)(2,1)S(1)}, u32[]{:S(2)}, u32[]{:S(2)}) collective-permute-start(bf16[4,48,256]{2,1,0:T(8,128)(2,1)} %get-tuple-element.92), channel_id=1, source_target_pairs={{0,16},{4,20},{8,24},{12,28},{16,0},{20,4},{24,8},{28,12},{1,17},{... | collective-permute-start | bytes 294920 | tf_op jit(solution)/shard_map/ppermute | solution.py:814
  91.0 18.6 %collective-permute-start.15 = (bf16[4,48,256]{2,1,0:T(8,128)(2,1)}, bf16[4,48,256]{2,1,0:T(8,128)(2,1)S(1)}, u32[]{:S(2)}, u32[]{:S(2)}) collective-permute-start(bf16[4,48,256]{2,1,0:T(8,128)(2,1)} %get-tuple-element.93), channel_id=1, source_target_pairs={{0,24},{4,28},{8,16},{12,20},{16,8},{20,12},{24,0},{28,4},{1,25},{... | collective-permute-start | bytes 294920 | tf_op jit(solution)/shard_map/ppermute | solution.py:814
  95.3 17.0 %collective-permute-start.7 = (bf16[4,112,256]{2,1,0:T(8,128)(2,1)}, bf16[4,112,256]{2,1,0:T(8,128)(2,1)S(1)}, u32[]{:S(2)}, u32[]{:S(2)}) collective-permute-start(bf16[4,112,256]{2,1,0:T(8,128)(2,1)} %get-tuple-element.82), channel_id=1, source_target_pairs={{0,1},{1,0},{2,3},{3,2},{4,5},{5,4},{6,7},{7,6},{8,9},{9,8},{10,11... | collective-permute-start | bytes 688136 | tf_op jit(solution)/shard_map/ppermute | solution.py:814
  99.2 14.0 %collective-permute-start.8 = (bf16[4,112,256]{2,1,0:T(8,128)(2,1)}, bf16[4,112,256]{2,1,0:T(8,128)(2,1)S(1)}, u32[]{:S(2)}, u32[]{:S(2)}) collective-permute-start(bf16[4,112,256]{2,1,0:T(8,128)(2,1)} %get-tuple-element.83), channel_id=1, source_target_pairs={{0,2},{1,3},{2,0},{3,1},{4,6},{5,7},{6,4},{7,5},{8,10},{9,11},{10,... | collective-permute-start | bytes 688136 | tf_op jit(solution)/shard_map/ppermute | solution.py:814
  103.1 11.1 %collective-permute-start.9 = (bf16[4,112,256]{2,1,0:T(8,128)(2,1)}, bf16[4,112,256]{2,1,0:T(8,128)(2,1)S(1)}, u32[]{:S(2)}, u32[]{:S(2)}) collective-permute-start(bf16[4,112,256]{2,1,0:T(8,128)(2,1)} %get-tuple-element.84), channel_id=1, source_target_pairs={{0,3},{1,2},{2,1},{3,0},{4,7},{5,6},{6,5},{7,4},{8,11},{9,10},{10,... | collective-permute-start | bytes 688136 | tf_op jit(solution)/shard_map/ppermute | solution.py:814
  104.6 5.0 %copy-start.2 = (bf16[4,48,256]{2,1,0:T(8,128)(2,1)S(1)}, bf16[4,48,256]{2,1,0:T(8,128)(2,1)}, u32[]{:S(2)}) copy-start(bf16[4,48,256]{2,1,0:T(8,128)(2,1)} %get-tuple-element.90) | copy-start | bytes 294916
  104.6 9.7 %copy-start.1 = (bf16[4,112,256]{2,1,0:T(8,128)(2,1)S(1)}, bf16[4,112,256]{2,1,0:T(8,128)(2,1)}, u32[]{:S(2)}) copy-start(bf16[4,112,256]{2,1,0:T(8,128)(2,1)} %get-tuple-element.86) | copy-start | bytes 688132
  109.6 5.5 %collective-permute-start.16 = (bf16[48,256]{1,0:T(8,128)(2,1)S(1)}, bf16[48,256]{1,0:T(8,128)(2,1)S(1)}, u32[]{:S(2)}, u32[]{:S(2)}) collective-permute-start(bf16[48,256]{1,0:T(8,128)(2,1)S(1)} %get-tuple-element.113), channel_id=1, source_target_pairs={{0,1},{1,0},{2,3},{3,2},{4,5},{5,4},{6,7},{7,6},{8,9},{9,8},{10,11... | collective-permute-start | bytes 73736 | tf_op jit(solution)/shard_map/ppermute | solution.py:814
  110.6 7.3 %collective-permute-start.18 = (bf16[48,256]{1,0:T(8,128)(2,1)S(1)}, bf16[48,256]{1,0:T(8,128)(2,1)S(1)}, u32[]{:S(2)}, u32[]{:S(2)}) collective-permute-start(bf16[48,256]{1,0:T(8,128)(2,1)S(1)} %get-tuple-element.114), channel_id=1, source_target_pairs={{0,3},{1,2},{2,1},{3,0},{4,7},{5,6},{6,5},{7,4},{8,11},{9,10},{10,... | collective-permute-start | bytes 73736 | tf_op jit(solution)/shard_map/ppermute | solution.py:814
  112.3 5.6 %collective-permute-start.17 = (bf16[48,256]{1,0:T(8,128)(2,1)S(1)}, bf16[48,256]{1,0:T(8,128)(2,1)S(1)}, u32[]{:S(2)}, u32[]{:S(2)}) collective-permute-start(bf16[48,256]{1,0:T(8,128)(2,1)S(1)} %get-tuple-element.115), channel_id=1, source_target_pairs={{0,2},{1,3},{2,0},{3,1},{4,6},{5,7},{6,4},{7,5},{8,10},{9,11},{10,... | collective-permute-start | bytes 73736 | tf_op jit(solution)/shard_map/ppermute | solution.py:814
  114.3 4.2 %collective-permute-start.10 = (bf16[112,256]{1,0:T(8,128)(2,1)S(1)}, bf16[112,256]{1,0:T(8,128)(2,1)S(1)}, u32[]{:S(2)}, u32[]{:S(2)}) collective-permute-start(bf16[112,256]{1,0:T(8,128)(2,1)S(1)} %get-tuple-element.110), channel_id=1, source_target_pairs={{0,8},{4,12},{8,0},{12,4},{16,24},{20,28},{24,16},{28,20},{1,9},{5... | collective-permute-start | bytes 172040 | tf_op jit(solution)/shard_map/ppermute | solution.py:814
  114.4 6.1 %collective-permute-start.12 = (bf16[112,256]{1,0:T(8,128)(2,1)S(1)}, bf16[112,256]{1,0:T(8,128)(2,1)S(1)}, u32[]{:S(2)}, u32[]{:S(2)}) collective-permute-start(bf16[112,256]{1,0:T(8,128)(2,1)S(1)} %get-tuple-element.111), channel_id=1, source_target_pairs={{0,24},{4,28},{8,16},{12,20},{16,8},{20,12},{24,0},{28,4},{1,25},{... | collective-permute-start | bytes 172040 | tf_op jit(solution)/shard_map/ppermute | solution.py:814
  115.2 9.1 %collective-permute-start.11 = (bf16[112,256]{1,0:T(8,128)(2,1)S(1)}, bf16[112,256]{1,0:T(8,128)(2,1)S(1)}, u32[]{:S(2)}, u32[]{:S(2)}) collective-permute-start(bf16[112,256]{1,0:T(8,128)(2,1)S(1)} %get-tuple-element.112), channel_id=1, source_target_pairs={{0,16},{4,20},{8,24},{12,28},{16,0},{20,4},{24,8},{28,12},{1,17},{... | collective-permute-start | bytes 172040 | tf_op jit(solution)/shard_map/ppermute | solution.py:814
  124.4 8.8 %copy-start = (bf16[160,256]{1,0:T(8,128)(2,1)}, bf16[160,256]{1,0:T(8,128)(2,1)S(1)}, u32[]{:S(2)}) copy-start(bf16[160,256]{1,0:T(8,128)(2,1)S(1)} %pad_maximum_fusion.refs_0_) | copy-start | bytes 245764
  124.4 6.5 %collective-permute-start.21 = (bf16[160,256]{1,0:T(8,128)(2,1)S(1)}, bf16[160,256]{1,0:T(8,128)(2,1)S(1)}, u32[]{:S(2)}, u32[]{:S(2)}) collective-permute-start(bf16[160,256]{1,0:T(8,128)(2,1)S(1)} %pad_maximum_fusion.refs_0_), channel_id=1, source_target_pairs={{0,24},{4,28},{8,16},{12,20},{16,8},{20,12},{24,0},{28,4},{1,25},{... | collective-permute-start | bytes 245768 | tf_op jit(solution)/shard_map/ppermute | solution.py:814
  124.6 7.1 %collective-permute-start.20 = (bf16[160,256]{1,0:T(8,128)(2,1)S(1)}, bf16[160,256]{1,0:T(8,128)(2,1)S(1)}, u32[]{:S(2)}, u32[]{:S(2)}) collective-permute-start(bf16[160,256]{1,0:T(8,128)(2,1)S(1)} %pad_maximum_fusion.refs_0_), channel_id=1, source_target_pairs={{0,16},{4,20},{8,24},{12,28},{16,0},{20,4},{24,8},{28,12},{1,17},{... | collective-permute-start | bytes 245768 | tf_op jit(solution)/shard_map/ppermute | solution.py:814
  124.6 7.1 %collective-permute-start.19 = (bf16[160,256]{1,0:T(8,128)(2,1)S(1)}, bf16[160,256]{1,0:T(8,128)(2,1)S(1)}, u32[]{:S(2)}, u32[]{:S(2)}) collective-permute-start(bf16[160,256]{1,0:T(8,128)(2,1)S(1)} %pad_maximum_fusion.refs_0_), channel_id=1, source_target_pairs={{0,8},{4,12},{8,0},{12,4},{16,24},{20,28},{24,16},{28,20},{1,9},{5... | collective-permute-start | bytes 245768 | tf_op jit(solution)/shard_map/ppermute | solution.py:814
  128.8 3.4 %collective-permute-start.22 = (bf16[160,256]{1,0:T(8,128)(2,1)S(1)}, bf16[160,256]{1,0:T(8,128)(2,1)S(1)}, u32[]{:S(2)}, u32[]{:S(2)}) collective-permute-start(bf16[160,256]{1,0:T(8,128)(2,1)S(1)} %pad_maximum_fusion.refs_0_), channel_id=1, source_target_pairs={{0,4},{4,0},{8,12},{12,8},{16,20},{20,16},{24,28},{28,24},{1,5},{5... | collective-permute-start | bytes 245768 | tf_op jit(solution)/shard_map/ppermute | solution.py:814
  130.8 2.3 %copy-start.3 = (bf16[160,256]{1,0:T(8,128)(2,1)}, bf16[160,256]{1,0:T(8,128)(2,1)S(1)}, u32[]{:S(2)}) copy-start(bf16[160,256]{1,0:T(8,128)(2,1)S(1)} %collective-permute-done.21.refs_3_) | copy-start | bytes 245764
  130.8 1.4 collective-permute-start.25
  131.7 1.5 %copy-start.4 = (bf16[160,256]{1,0:T(8,128)(2,1)}, bf16[160,256]{1,0:T(8,128)(2,1)S(1)}, u32[]{:S(2)}) copy-start(bf16[160,256]{1,0:T(8,128)(2,1)S(1)} %collective-permute-done.20.refs_2_) | copy-start | bytes 245764
  131.7 1.3 collective-permute-start.24
  131.7 1.4 %copy-start.5 = (bf16[160,256]{1,0:T(8,128)(2,1)}, bf16[160,256]{1,0:T(8,128)(2,1)S(1)}, u32[]{:S(2)}) copy-start(bf16[160,256]{1,0:T(8,128)(2,1)S(1)} %collective-permute-done.19.refs_1_) | copy-start | bytes 245764
  131.7 1.4 %collective-permute-start.23 = (bf16[160,256]{1,0:T(8,128)(2,1)S(1)}, bf16[160,256]{1,0:T(8,128)(2,1)S(1)}, u32[]{:S(2)}, u32[]{:S(2)}) collective-permute-start(bf16[160,256]{1,0:T(8,128)(2,1)S(1)} %collective-permute-done.19.refs_1_), channel_id=1, source_target_pairs={{0,4},{4,0},{8,12},{12,8},{16,20},{20,16},{24,28},{28,24},{1,5},{5... | collective-permute-start | bytes 245768 | tf_op jit(solution)/shard_map/ppermute | solution.py:814
  132.2 0.9 copy-start.6
  132.2 0.9 copy-start.7
  133.0 0.6 copy-start.8
  133.1 0.6 copy-start.9

commit v6 on v5

--- a/solution.py
+++ b/solution.py
@@ -504,14 +504,20 @@
     def gather_back(c):
         dn_buf[...] = nn(dnum[...], one_hot_rows(row(c, TARGET), N))
 
+    def scatter_nodes(c, dkve):
+        dqkv[:, D:] += nt(one_hot_rows(row(c, SOURCE)[:, :dkve.shape[1]], N), dkve)
+
+    def scatter_times(c, dkve):
+        dtkv[...] += nt(one_hot_rows(row(c, BUCKET)[:, :dkve.shape[1]], 1024), dkve)
+
     def scatter_back(c, span=EC):
-        dkve = dkve_buf[:, :span]
-        dqkv[:, D:] += nt(one_hot_rows(row(c, SOURCE)[:, :span], N), dkve)
-        dtkv[...] += nt(one_hot_rows(row(c, BUCKET)[:, :span], 1024), dkve)
+        scatter_times(c, dkve_buf[:, :span])
+        scatter_nodes(c, dkve_buf[:, :span])
 
     def backward(wide, more, c, _, span=EC):
         at = place(c, span)
-        scatter_back(jnp.maximum(c - 1, 0))
+        before, dkve = jnp.maximum(c - 1, 0), dkve_buf[...]
+        scatter_times(before, dkve)
         dn_e = dn_buf[:D, :span]
         w = wexp[:, at]
         dw = head_sum(dn_e * msg[:, at].astype(f32)) + dn_buf[D:D + H, :span] + dn_buf[D + H:, :span]
@@ -521,8 +527,6 @@
         dka = (ss * qe[:, at].astype(f32)).astype(bf16)
         dms = (head_wide(w) * dn_e).astype(bf16)
         dqe = (ss * xg[:, at].astype(f32)).astype(bf16)
-        if more:
-            gather_back(c + 1)
         for r, sl in blocks_of(c, wide, span):
             dkve_buf[0:D, sl] = nn(bda[r], dka[:, sl]).astype(bf16)
             dkve_buf[D:, sl] = nn(bdm[r], dms[:, sl]).astype(bf16)
@@ -536,6 +540,9 @@
             gm[r, 128:] += gmk[128:, 128:]
             dmu[r] += sum(dsr[:, k:k + 128] for k in range(sl.start, sl.stop, 128))
         dqkv[:, :D] += nt(one_hot_rows(row(c, TARGET)[:, :span], N), dqe)
+        scatter_nodes(before, dkve)
+        if more:
+            gather_back(c + 1)
         return 0
 
     gather_back(0)

time: 138 us -> 142 us (1.029); the launches traced: 139 us -> 140 us
  starting transfers between devices: 31.8 us -> 25.1 us
  Pallas kernels: 84.5 us -> 91.1 us
    ppermute x26, starting transfers between devices: 31.8 us -> 25.1 us  [swap(): return lax.ppermute(x, axis, [(i, i ^ mask) for i in range(size)])]
    pallas_call x1, Pallas kernels: 58.9 us -> 64.7 us  [layer(): pl.pallas_call(functools.partial(layer_kernel, lay), out_shape=[S((N, D),...]
  transfers between devices with their start and end apart: 26 -> 26, of which waited for: 13 -> 14; matrix products, arithmetic and copies ran while one was open for 0% -> 0% of each run, Pallas kernels for 11% -> 12%
where the time goes in v6:
time: 142 us; the launch traced here: 140 us
  Pallas kernels  91.1 us (64%)
  starting transfers between devices  25.1 us (18%)
  waiting for transfers between devices  20.3 us (14%)
  between operations  1.68 us (1%)
  local copies, waits for them, and re-layouts  1.62 us (1%)
    pallas_call x1, Pallas kernels, layer(): pl.pallas_call(functools.partial(layer_kernel, lay), out_shape=[S((N, D),...  64.7 us
    ppermute x26, starting transfers between devices, swap(): return lax.ppermute(x, axis, [(i, i ^ mask) for i in range(size)])  25.1 us
    ppermute x26, waiting for transfers between devices, swap(): return lax.ppermute(x, axis, [(i, i ^ mask) for i in range(size)])  20.3 us
    pallas_call x1, Pallas kernels, before(): pl.pallas_call(before_kernel, out_shape=(S((EDGES // EC * 8, EC), jnp.int...  9.26 us
    pallas_call x1, Pallas kernels, update(): pl.pallas_call(functools.partial(update_kernel, jobs, len(states)), out_s...  5.32 us
    pallas_call x1, Pallas kernels, input_gradient(): pl.pallas_call(input_kernel, out_shape=S((N, D), bf16), compiler_params=p...  4.95 us
  transfers between devices with their start and end apart: 26, of which 14 were waited for; matrix products, arithmetic and copies ran while one was open for 0% of the time, Pallas kernels for 12%

profile of v6, /device:TPU:0, one launch (start us, length us, event | category | flops | bytes accessed | tf_op | source)
XLA Modules:
  0.0 140.1 jit_solution(11129174225241837832)
XLA Ops:
  0.7 1.9 %pack_half.1 = bf16[160,1024]{1,0:T(8,128)(2,1)} custom-call(f32[256,1024]{1,0:T(8,128)} %refs_8_.1, f32[64,768]{1,0:T(8,128)} %refs_12_.1, f32[8,64]{1,0:T(8,128)} %refs_16_.1), custom_call_target="tpu_custom_call" | custom-call | tf_op jit(solution)/shard_map/pack_half/pallas_call | solution.py:208
  2.6 4.0 %collective-permute-start.2 = (bf16[160,1024]{1,0:T(8,128)(2,1)}, bf16[160,1024]{1,0:T(8,128)(2,1)S(1)}, u32[]{:S(2)}, u32[]{:S(2)}) collective-permute-start(bf16[160,1024]{1,0:T(8,128)(2,1)} %pack_half.1), channel_id=1, source_target_pairs={{0,3},{1,2},{2,1},{3,0},{4,7},{5,6},{6,5},{7,4},{8,11},{9,10},{10,... | collective-permute-start | bytes 983048 | tf_op jit(solution)/shard_map/ppermute | solution.py:821
  6.5 0.5 collective-permute-start.1
  7.0 0.1 collective-permute-start
  7.2 2.2 %pack.1.refs_8_ = bf16[320,1024]{1,0:T(8,128)(2,1)} custom-call(f32[256,1024]{1,0:T(8,128)} %refs_8_.1, f32[64,768]{1,0:T(8,128)} %refs_12_.1, f32[8,64]{1,0:T(8,128)} %refs_16_.1), custom_call_target="tpu_custom_call" | custom-call | tf_op jit(solution)/shard_map/pack/pallas_call | solution.py:230
  9.4 9.3 %before.1 = (s32[128,512]{1,0:T(8,128)}, bf16[256,8192]{1,0:T(8,128)(2,1)}) custom-call(s32[8]{0:T(128)} %refs_1_.1, s32[1,1024]{1,0:T(1,128)} %bitcast.36, s32[8,1024]{1,0:T(8,128)} %src_ref.1, s32[8,1024]{1,0:T(8,128)} %dst_ref.1, s32[8,1024]{1,0:T(8,128)} %tim_ref.1, bf16[1024,256]{1,0:T(8,128)(2,1)} %refs_7_.1), custom_call_target="tpu_custom_call" | custom-call | flops 4294967296 | bytes 6291456 | tf_op jit(solution)/shard_map/before/pallas_call | solution.py:269
  18.7 3.1 %collective-permute-done.refs_9_ = bf16[160,1024]{1,0:T(8,128)(2,1)S(1)} collective-permute-done((bf16[160,1024]{1,0:T(8,128)(2,1)}, bf16[160,1024]{1,0:T(8,128)(2,1)S(1)}, u32[]{:S(2)}, u32[]{:S(2)}) %collective-permute-start) | collective-permute-done | bytes 327712 | tf_op jit(solution)/shard_map/ppermute | solution.py:821
  21.7 0.1 collective-permute-start.5
  21.8 0.5 collective-permute-start.4
  22.3 0.1 collective-permute-start.3
  23.1 0.4 collective-permute-done.5.refs_14_
  23.4 0.5 collective-permute-done.4.refs_13_
  23.9 0.5 collective-permute-done.3.refs_12_
  24.4 0.3 copy-done.14
  24.6 0.7 copy-done.15
  25.4 64.7 %layer.1 = (bf16[1024,256]{1,0:T(8,128)(2,1)}, bf16[1024,768]{1,0:T(8,128)(2,1)}, f32[256,1024]{1,0:T(8,128)}, bf16[1024,768]{1,0:T(8,128)(2,1)}, bf16[4,4,160,2...) custom-call(s32[1]{0:T(128)S(6)} %copy.43.refs_0_, s32[8]{0:T(128)} %refs_1_.1, s32[1,1024]{1,0:T(1,128)} %bitcast.37, ...), custom_call_target="tpu_custom_call" | custom-call | flops 60000002048 | bytes 16777216 | tf_op jit(solution)/shard_map/layer/pallas_call | solution.py:644
  90.1 0.1 collective-permute-start.6
  90.2 3.4 %collective-permute-done.6.got_ref = bf16[4,4,160,256]{3,2,1,0:T(8,128)(2,1)} collective-permute-done((bf16[4,4,160,256]{3,2,1,0:T(8,128)(2,1)}, bf16[4,4,160,256]{3,2,1,0:T(8,128)(2,1)}, u32[]{:S(2)}, u32[]{:S(2)}) %collective-permute-start.6) | collective-permute-done | bytes 1310752 | tf_op jit(solution)/shard_map/ppermute | solution.py:821
  93.6 2.7 %add_core.1 = (bf16[4,112,256]{2,1,0:T(8,128)(2,1)}, bf16[4,112,256]{2,1,0:T(8,128)(2,1)}, bf16[4,112,256]{2,1,0:T(8,128)(2,1)}, bf16[4,48,256]{2,1,0:T(8,128)(2...) custom-call(bf16[4,4,160,256]{3,2,1,0:T(8,128)(2,1)} %get-tuple-elem, ...), custom_call_target="tpu_custom_call" | custom-call | tf_op jit(solution)/shard_map/add_core/pallas_call | solution.py:722
  96.3 0.1 collective-permute-start.13
  96.4 0.1 collective-permute-start.14
  96.4 4.3 %collective-permute-start.15 = (bf16[4,48,256]{2,1,0:T(8,128)(2,1)}, bf16[4,48,256]{2,1,0:T(8,128)(2,1)S(1)}, u32[]{:S(2)}, u32[]{:S(2)}) collective-permute-start(bf16[4,48,256]{2,1,0:T(8,128)(2,1)} %get-tuple-element.93), channel_id=1, source_target_pairs={{0,24},{4,28},{8,16},{12,20},{16,8},{20,12},{24,0},{28,4},{1,25},{... | collective-permute-start | bytes 294920 | tf_op jit(solution)/shard_map/ppermute | solution.py:821
  100.7 1.0 collective-permute-start.7
  101.8 0.8 collective-permute-done.13
  102.6 1.7 %collective-permute-start.9 = (bf16[4,112,256]{2,1,0:T(8,128)(2,1)}, bf16[4,112,256]{2,1,0:T(8,128)(2,1)S(1)}, u32[]{:S(2)}, u32[]{:S(2)}) collective-permute-start(bf16[4,112,256]{2,1,0:T(8,128)(2,1)} %get-tuple-element.84), channel_id=1, source_target_pairs={{0,3},{1,2},{2,1},{3,0},{4,7},{5,6},{6,5},{7,4},{8,11},{9,10},{10,... | collective-permute-start | bytes 688136 | tf_op jit(solution)/shard_map/ppermute | solution.py:821
  104.2 5.0 %input_gradient.1 = bf16[1024,256]{1,0:T(8,128)(2,1)} custom-call(s32[1,1024]{1,0:T(1,128)} %bitcast.38, bf16[1024,768]{1,0:T(8,128)(2,1)} %get-tuple-element.78.dqkv_ref, f32[256,1024]{1,0:T(8,128)} %get-tuple-element.79.skp_ref, bf16[1024,768]{1,0:T(8,128)(2,1)} %get-tuple-element.80.types_ref), custom_call_target="tpu_custom_call" | custom-call | flops 1610612736 | bytes 6291456 | tf_op jit(solution)/shard_map/input_gradient/pallas_call | solution.py:678
  109.2 1.1 collective-permute-start.16
  110.4 0.4 collective-permute-start.18
  110.8 2.0 %collective-permute-start.17 = (bf16[48,256]{1,0:T(8,128)(2,1)S(1)}, bf16[48,256]{1,0:T(8,128)(2,1)S(1)}, u32[]{:S(2)}, u32[]{:S(2)}) collective-permute-start(bf16[48,256]{1,0:T(8,128)(2,1)S(1)} %get-tuple-element.115), channel_id=1, source_target_pairs={{0,2},{1,3},{2,0},{3,1},{4,6},{5,7},{6,4},{7,5},{8,10},{9,11},{10,... | collective-permute-start | bytes 73736 | tf_op jit(solution)/shard_map/ppermute | solution.py:821
  112.8 1.6 %collective-permute-done.8 = bf16[4,112,256]{2,1,0:T(8,128)(2,1)S(1)} collective-permute-done((bf16[4,112,256]{2,1,0:T(8,128)(2,1)}, bf16[4,112,256]{2,1,0:T(8,128)(2,1)S(1)}, u32[]{:S(2)}, u32[]{:S(2)}) %collective-permute-start.8) | collective-permute-done | bytes 229408 | tf_op jit(solution)/shard_map/ppermute | solution.py:821
  114.5 0.1 fusion.3
  114.6 0.4 collective-permute-start.10
  114.9 3.3 %collective-permute-start.12 = (bf16[112,256]{1,0:T(8,128)(2,1)S(1)}, bf16[112,256]{1,0:T(8,128)(2,1)S(1)}, u32[]{:S(2)}, u32[]{:S(2)}) collective-permute-start(bf16[112,256]{1,0:T(8,128)(2,1)S(1)} %get-tuple-element.111), channel_id=1, source_target_pairs={{0,24},{4,28},{8,16},{12,20},{16,8},{20,12},{24,0},{28,4},{1,25},{... | collective-permute-start | bytes 172040 | tf_op jit(solution)/shard_map/ppermute | solution.py:821
  118.2 0.5 collective-permute-start.11
  118.8 0.6 collective-permute-done.10
  119.4 2.2 %collective-permute-done.12 = bf16[112,256]{1,0:T(8,128)(2,1)S(1)} collective-permute-done((bf16[112,256]{1,0:T(8,128)(2,1)S(1)}, bf16[112,256]{1,0:T(8,128)(2,1)S(1)}, u32[]{:S(2)}, u32[]{:S(2)}) %collective-permute-start.12) | collective-permute-done | bytes 57376 | tf_op jit(solution)/shard_map/ppermute | solution.py:821
  121.6 2.4 %collective-permute-done.11 = bf16[112,256]{1,0:T(8,128)(2,1)S(1)} collective-permute-done((bf16[112,256]{1,0:T(8,128)(2,1)S(1)}, bf16[112,256]{1,0:T(8,128)(2,1)S(1)}, u32[]{:S(2)}, u32[]{:S(2)}) %collective-permute-start.11) | collective-permute-done | bytes 57376 | tf_op jit(solution)/shard_map/ppermute | solution.py:821
  124.0 1.8 %collective-permute-start.21 = (bf16[160,256]{1,0:T(8,128)(2,1)S(1)}, bf16[160,256]{1,0:T(8,128)(2,1)S(1)}, u32[]{:S(2)}, u32[]{:S(2)}) collective-permute-start(bf16[160,256]{1,0:T(8,128)(2,1)S(1)} %pad_maximum_fusion.refs_0_), channel_id=1, source_target_pairs={{0,24},{4,28},{8,16},{12,20},{16,8},{20,12},{24,0},{28,4},{1,25},{... | collective-permute-start | bytes 245768 | tf_op jit(solution)/shard_map/ppermute | solution.py:821
  125.8 0.3 collective-permute-start.20
  126.1 2.4 %collective-permute-start.19 = (bf16[160,256]{1,0:T(8,128)(2,1)S(1)}, bf16[160,256]{1,0:T(8,128)(2,1)S(1)}, u32[]{:S(2)}, u32[]{:S(2)}) collective-permute-start(bf16[160,256]{1,0:T(8,128)(2,1)S(1)} %pad_maximum_fusion.refs_0_), channel_id=1, source_target_pairs={{0,8},{4,12},{8,0},{12,4},{16,24},{20,28},{24,16},{28,20},{1,9},{5... | collective-permute-start | bytes 245768 | tf_op jit(solution)/shard_map/ppermute | solution.py:821
  128.5 2.3 %collective-permute-done.21.refs_3_ = bf16[160,256]{1,0:T(8,128)(2,1)S(1)} collective-permute-done((bf16[160,256]{1,0:T(8,128)(2,1)S(1)}, bf16[160,256]{1,0:T(8,128)(2,1)S(1)}, u32[]{:S(2)}, u32[]{:S(2)}) %collective-permute-start.21) | collective-permute-done | bytes 81952 | tf_op jit(solution)/shard_map/ppermute | solution.py:821
  130.8 1.7 %collective-permute-done.20.refs_2_ = bf16[160,256]{1,0:T(8,128)(2,1)S(1)} collective-permute-done((bf16[160,256]{1,0:T(8,128)(2,1)S(1)}, bf16[160,256]{1,0:T(8,128)(2,1)S(1)}, u32[]{:S(2)}, u32[]{:S(2)}) %collective-permute-start.20) | collective-permute-done | bytes 81952 | tf_op jit(solution)/shard_map/ppermute | solution.py:821
  132.5 0.5 collective-permute-start.23
  133.0 0.7 collective-permute-done.24.refs_6_
  133.8 0.2 collective-permute-done.23.refs_5_
  134.0 0.4 copy-done.8
  134.4 0.2 copy-done.9
  134.6 5.3 %update.1 = (f32[256,1024]{1,0:T(8,128)}, f32[256,1024]{1,0:T(8,128)}, f32[256,1024]{1,0:T(8,128)}, f32[256,1024]{1,0:T(8,128)}, f32[64,768]{1,0:T(8,128)}, /*in...) custom-call(bf16[160,256]{1,0:T(8,128)(2,1)} %copy-done, ...), custom_call_target="tpu_custom_call" | custom-call | tf_op jit(solution)/shard_map/update/pallas_call | solution.py:796
  (48 shorter events, 0.2 us)
Async XLA Ops:
  2.6 19.2 %collective-permute-start.2 = (bf16[160,1024]{1,0:T(8,128)(2,1)}, bf16[160,1024]{1,0:T(8,128)(2,1)S(1)}, u32[]{:S(2)}, u32[]{:S(2)}) collective-permute-start(bf16[160,1024]{1,0:T(8,128)(2,1)} %pack_half.1), channel_id=1, source_target_pairs={{0,3},{1,2},{2,1},{3,0},{4,7},{5,6},{6,5},{7,4},{8,11},{9,10},{10,... | collective-permute-start | bytes 983048 | tf_op jit(solution)/shard_map/ppermute | solution.py:821
  6.5 15.3 %collective-permute-start.1 = (bf16[160,1024]{1,0:T(8,128)(2,1)}, bf16[160,1024]{1,0:T(8,128)(2,1)S(1)}, u32[]{:S(2)}, u32[]{:S(2)}) collective-permute-start(bf16[160,1024]{1,0:T(8,128)(2,1)} %pack_half.1), channel_id=1, source_target_pairs={{0,2},{1,3},{2,0},{3,1},{4,6},{5,7},{6,4},{7,5},{8,10},{9,11},{10,... | collective-permute-start | bytes 983048 | tf_op jit(solution)/shard_map/ppermute | solution.py:821
  7.0 14.7 %collective-permute-start = (bf16[160,1024]{1,0:T(8,128)(2,1)}, bf16[160,1024]{1,0:T(8,128)(2,1)S(1)}, u32[]{:S(2)}, u32[]{:S(2)}) collective-permute-start(bf16[160,1024]{1,0:T(8,128)(2,1)} %pack_half.1), channel_id=1, source_target_pairs={{0,1},{1,0},{2,3},{3,2},{4,5},{5,4},{6,7},{7,6},{8,9},{9,8},{10,11... | collective-permute-start | bytes 983048 | tf_op jit(solution)/shard_map/ppermute | solution.py:821
  21.7 3.6 %copy-start.12 = (bf16[160,1024]{1,0:T(8,128)(2,1)}, bf16[160,1024]{1,0:T(8,128)(2,1)S(1)}, u32[]{:S(2)}) copy-start(bf16[160,1024]{1,0:T(8,128)(2,1)S(1)} %collective-permute-done.refs_9_) | copy-start | bytes 983044
  21.7 3.6 %copy-start.10 = (bf16[160,1024]{1,0:T(8,128)(2,1)}, bf16[160,1024]{1,0:T(8,128)(2,1)S(1)}, u32[]{:S(2)}) copy-start(bf16[160,1024]{1,0:T(8,128)(2,1)S(1)} %collective-permute-done.2.refs_11_) | copy-start | bytes 983044
  21.7 1.7 %collective-permute-start.5 = (bf16[160,1024]{1,0:T(8,128)(2,1)S(1)}, bf16[160,1024]{1,0:T(8,128)(2,1)S(1)}, u32[]{:S(2)}, u32[]{:S(2)}) collective-permute-start(bf16[160,1024]{1,0:T(8,128)(2,1)S(1)} %collective-permute-done.2.refs_11_), channel_id=1, source_target_pairs={{0,4},{4,0},{8,12},{12,8},{16,20},{20,16},{24,28},{28,24},{1,5},{5... | collective-permute-start | bytes 983048 | tf_op jit(solution)/shard_map/ppermute | solution.py:821
  21.8 3.5 %copy-start.11 = (bf16[160,1024]{1,0:T(8,128)(2,1)}, bf16[160,1024]{1,0:T(8,128)(2,1)S(1)}, u32[]{:S(2)}) copy-start(bf16[160,1024]{1,0:T(8,128)(2,1)S(1)} %collective-permute-done.1.refs_10_) | copy-start | bytes 983044
  21.8 2.1 %collective-permute-start.4 = (bf16[160,1024]{1,0:T(8,128)(2,1)S(1)}, bf16[160,1024]{1,0:T(8,128)(2,1)S(1)}, u32[]{:S(2)}, u32[]{:S(2)}) collective-permute-start(bf16[160,1024]{1,0:T(8,128)(2,1)S(1)} %collective-permute-done.1.refs_10_), channel_id=1, source_target_pairs={{0,4},{4,0},{8,12},{12,8},{16,20},{20,16},{24,28},{28,24},{1,5},{5... | collective-permute-start | bytes 983048 | tf_op jit(solution)/shard_map/ppermute | solution.py:821
  22.3 2.0 %collective-permute-start.3 = (bf16[160,1024]{1,0:T(8,128)(2,1)S(1)}, bf16[160,1024]{1,0:T(8,128)(2,1)S(1)}, u32[]{:S(2)}, u32[]{:S(2)}) collective-permute-start(bf16[160,1024]{1,0:T(8,128)(2,1)S(1)} %collective-permute-done.refs_9_), channel_id=1, source_target_pairs={{0,4},{4,0},{8,12},{12,8},{16,20},{20,16},{24,28},{28,24},{1,5},{5... | collective-permute-start | bytes 983048 | tf_op jit(solution)/shard_map/ppermute | solution.py:821
  23.4 0.9 copy-start.13
  23.9 0.7 copy-start.14
  24.6 0.7 copy-start.15
  90.1 3.4 %collective-permute-start.6 = (bf16[4,4,160,256]{3,2,1,0:T(8,128)(2,1)}, bf16[4,4,160,256]{3,2,1,0:T(8,128)(2,1)}, u32[]{:S(2)}, u32[]{:S(2)}) collective-permute-start(bf16[4,4,160,256]{3,2,1,0:T(8,128)(2,1)} %get-tuple-element.73), channel_id=1, source_target_pairs={{0,4},{4,0},{8,12},{12,8},{16,20},{20,16},{24,28},{28,24},{1,5},{5... | collective-permute-start | bytes 3932168 | tf_op jit(solution)/shard_map/ppermute | solution.py:821
  96.3 6.3 %collective-permute-start.13 = (bf16[4,48,256]{2,1,0:T(8,128)(2,1)}, bf16[4,48,256]{2,1,0:T(8,128)(2,1)S(1)}, u32[]{:S(2)}, u32[]{:S(2)}) collective-permute-start(bf16[4,48,256]{2,1,0:T(8,128)(2,1)} %get-tuple-element.91), channel_id=1, source_target_pairs={{0,8},{4,12},{8,0},{12,4},{16,24},{20,28},{24,16},{28,20},{1,9},{5... | collective-permute-start | bytes 294920 | tf_op jit(solution)/shard_map/ppermute | solution.py:821
  96.4 12.8 %collective-permute-start.14 = (bf16[4,48,256]{2,1,0:T(8,128)(2,1)}, bf16[4,48,256]{2,1,0:T(8,128)(2,1)S(1)}, u32[]{:S(2)}, u32[]{:S(2)}) collective-permute-start(bf16[4,48,256]{2,1,0:T(8,128)(2,1)} %get-tuple-element.92), channel_id=1, source_target_pairs={{0,16},{4,20},{8,24},{12,28},{16,0},{20,4},{24,8},{28,12},{1,17},{... | collective-permute-start | bytes 294920 | tf_op jit(solution)/shard_map/ppermute | solution.py:821
  96.4 12.8 %collective-permute-start.15 = (bf16[4,48,256]{2,1,0:T(8,128)(2,1)}, bf16[4,48,256]{2,1,0:T(8,128)(2,1)S(1)}, u32[]{:S(2)}, u32[]{:S(2)}) collective-permute-start(bf16[4,48,256]{2,1,0:T(8,128)(2,1)} %get-tuple-element.93), channel_id=1, source_target_pairs={{0,24},{4,28},{8,16},{12,20},{16,8},{20,12},{24,0},{28,4},{1,25},{... | collective-permute-start | bytes 294920 | tf_op jit(solution)/shard_map/ppermute | solution.py:821
  100.7 10.0 %collective-permute-start.7 = (bf16[4,112,256]{2,1,0:T(8,128)(2,1)}, bf16[4,112,256]{2,1,0:T(8,128)(2,1)S(1)}, u32[]{:S(2)}, u32[]{:S(2)}) collective-permute-start(bf16[4,112,256]{2,1,0:T(8,128)(2,1)} %get-tuple-element.82), channel_id=1, source_target_pairs={{0,1},{1,0},{2,3},{3,2},{4,5},{5,4},{6,7},{7,6},{8,9},{9,8},{10,11... | collective-permute-start | bytes 688136 | tf_op jit(solution)/shard_map/ppermute | solution.py:821
  101.8 12.7 %collective-permute-start.8 = (bf16[4,112,256]{2,1,0:T(8,128)(2,1)}, bf16[4,112,256]{2,1,0:T(8,128)(2,1)S(1)}, u32[]{:S(2)}, u32[]{:S(2)}) collective-permute-start(bf16[4,112,256]{2,1,0:T(8,128)(2,1)} %get-tuple-element.83), channel_id=1, source_target_pairs={{0,2},{1,3},{2,0},{3,1},{4,6},{5,7},{6,4},{7,5},{8,10},{9,11},{10,... | collective-permute-start | bytes 688136 | tf_op jit(solution)/shard_map/ppermute | solution.py:821
  102.6 11.9 %collective-permute-start.9 = (bf16[4,112,256]{2,1,0:T(8,128)(2,1)}, bf16[4,112,256]{2,1,0:T(8,128)(2,1)S(1)}, u32[]{:S(2)}, u32[]{:S(2)}) collective-permute-start(bf16[4,112,256]{2,1,0:T(8,128)(2,1)} %get-tuple-element.84), channel_id=1, source_target_pairs={{0,3},{1,2},{2,1},{3,0},{4,7},{5,6},{6,5},{7,4},{8,11},{9,10},{10,... | collective-permute-start | bytes 688136 | tf_op jit(solution)/shard_map/ppermute | solution.py:821
  104.2 5.0 %copy-start.2 = (bf16[4,48,256]{2,1,0:T(8,128)(2,1)S(1)}, bf16[4,48,256]{2,1,0:T(8,128)(2,1)}, u32[]{:S(2)}) copy-start(bf16[4,48,256]{2,1,0:T(8,128)(2,1)} %get-tuple-element.90) | copy-start | bytes 294916
  104.2 10.2 %copy-start.1 = (bf16[4,112,256]{2,1,0:T(8,128)(2,1)S(1)}, bf16[4,112,256]{2,1,0:T(8,128)(2,1)}, u32[]{:S(2)}) copy-start(bf16[4,112,256]{2,1,0:T(8,128)(2,1)} %get-tuple-element.86) | copy-start | bytes 688132
  109.2 9.0 %collective-permute-start.16 = (bf16[48,256]{1,0:T(8,128)(2,1)S(1)}, bf16[48,256]{1,0:T(8,128)(2,1)S(1)}, u32[]{:S(2)}, u32[]{:S(2)}) collective-permute-start(bf16[48,256]{1,0:T(8,128)(2,1)S(1)} %get-tuple-element.113), channel_id=1, source_target_pairs={{0,1},{1,0},{2,3},{3,2},{4,5},{5,4},{6,7},{7,6},{8,9},{9,8},{10,11... | collective-permute-start | bytes 73736 | tf_op jit(solution)/shard_map/ppermute | solution.py:821
  110.4 8.4 %collective-permute-start.18 = (bf16[48,256]{1,0:T(8,128)(2,1)S(1)}, bf16[48,256]{1,0:T(8,128)(2,1)S(1)}, u32[]{:S(2)}, u32[]{:S(2)}) collective-permute-start(bf16[48,256]{1,0:T(8,128)(2,1)S(1)} %get-tuple-element.114), channel_id=1, source_target_pairs={{0,3},{1,2},{2,1},{3,0},{4,7},{5,6},{6,5},{7,4},{8,11},{9,10},{10,... | collective-permute-start | bytes 73736 | tf_op jit(solution)/shard_map/ppermute | solution.py:821
  110.8 8.0 %collective-permute-start.17 = (bf16[48,256]{1,0:T(8,128)(2,1)S(1)}, bf16[48,256]{1,0:T(8,128)(2,1)S(1)}, u32[]{:S(2)}, u32[]{:S(2)}) collective-permute-start(bf16[48,256]{1,0:T(8,128)(2,1)S(1)} %get-tuple-element.115), channel_id=1, source_target_pairs={{0,2},{1,3},{2,0},{3,1},{4,6},{5,7},{6,4},{7,5},{8,10},{9,11},{10,... | collective-permute-start | bytes 73736 | tf_op jit(solution)/shard_map/ppermute | solution.py:821
  114.6 4.9 %collective-permute-start.10 = (bf16[112,256]{1,0:T(8,128)(2,1)S(1)}, bf16[112,256]{1,0:T(8,128)(2,1)S(1)}, u32[]{:S(2)}, u32[]{:S(2)}) collective-permute-start(bf16[112,256]{1,0:T(8,128)(2,1)S(1)} %get-tuple-element.110), channel_id=1, source_target_pairs={{0,8},{4,12},{8,0},{12,4},{16,24},{20,28},{24,16},{28,20},{1,9},{5... | collective-permute-start | bytes 172040 | tf_op jit(solution)/shard_map/ppermute | solution.py:821
  114.9 6.6 %collective-permute-start.12 = (bf16[112,256]{1,0:T(8,128)(2,1)S(1)}, bf16[112,256]{1,0:T(8,128)(2,1)S(1)}, u32[]{:S(2)}, u32[]{:S(2)}) collective-permute-start(bf16[112,256]{1,0:T(8,128)(2,1)S(1)} %get-tuple-element.111), channel_id=1, source_target_pairs={{0,24},{4,28},{8,16},{12,20},{16,8},{20,12},{24,0},{28,4},{1,25},{... | collective-permute-start | bytes 172040 | tf_op jit(solution)/shard_map/ppermute | solution.py:821
  118.2 5.7 %collective-permute-start.11 = (bf16[112,256]{1,0:T(8,128)(2,1)S(1)}, bf16[112,256]{1,0:T(8,128)(2,1)S(1)}, u32[]{:S(2)}, u32[]{:S(2)}) collective-permute-start(bf16[112,256]{1,0:T(8,128)(2,1)S(1)} %get-tuple-element.112), channel_id=1, source_target_pairs={{0,16},{4,20},{8,24},{12,28},{16,0},{20,4},{24,8},{28,12},{1,17},{... | collective-permute-start | bytes 172040 | tf_op jit(solution)/shard_map/ppermute | solution.py:821
  124.0 9.9 %copy-start = (bf16[160,256]{1,0:T(8,128)(2,1)}, bf16[160,256]{1,0:T(8,128)(2,1)S(1)}, u32[]{:S(2)}) copy-start(bf16[160,256]{1,0:T(8,128)(2,1)S(1)} %pad_maximum_fusion.refs_0_) | copy-start | bytes 245764
  124.0 6.7 %collective-permute-start.21 = (bf16[160,256]{1,0:T(8,128)(2,1)S(1)}, bf16[160,256]{1,0:T(8,128)(2,1)S(1)}, u32[]{:S(2)}, u32[]{:S(2)}) collective-permute-start(bf16[160,256]{1,0:T(8,128)(2,1)S(1)} %pad_maximum_fusion.refs_0_), channel_id=1, source_target_pairs={{0,24},{4,28},{8,16},{12,20},{16,8},{20,12},{24,0},{28,4},{1,25},{... | collective-permute-start | bytes 245768 | tf_op jit(solution)/shard_map/ppermute | solution.py:821
  125.8 6.7 %collective-permute-start.20 = (bf16[160,256]{1,0:T(8,128)(2,1)S(1)}, bf16[160,256]{1,0:T(8,128)(2,1)S(1)}, u32[]{:S(2)}, u32[]{:S(2)}) collective-permute-start(bf16[160,256]{1,0:T(8,128)(2,1)S(1)} %pad_maximum_fusion.refs_0_), channel_id=1, source_target_pairs={{0,16},{4,20},{8,24},{12,28},{16,0},{20,4},{24,8},{28,12},{1,17},{... | collective-permute-start | bytes 245768 | tf_op jit(solution)/shard_map/ppermute | solution.py:821
  126.1 6.4 %collective-permute-start.19 = (bf16[160,256]{1,0:T(8,128)(2,1)S(1)}, bf16[160,256]{1,0:T(8,128)(2,1)S(1)}, u32[]{:S(2)}, u32[]{:S(2)}) collective-permute-start(bf16[160,256]{1,0:T(8,128)(2,1)S(1)} %pad_maximum_fusion.refs_0_), channel_id=1, source_target_pairs={{0,8},{4,12},{8,0},{12,4},{16,24},{20,28},{24,16},{28,20},{1,9},{5... | collective-permute-start | bytes 245768 | tf_op jit(solution)/shard_map/ppermute | solution.py:821
  128.5 4.5 %collective-permute-start.22 = (bf16[160,256]{1,0:T(8,128)(2,1)S(1)}, bf16[160,256]{1,0:T(8,128)(2,1)S(1)}, u32[]{:S(2)}, u32[]{:S(2)}) collective-permute-start(bf16[160,256]{1,0:T(8,128)(2,1)S(1)} %pad_maximum_fusion.refs_0_), channel_id=1, source_target_pairs={{0,4},{4,0},{8,12},{12,8},{16,20},{20,16},{24,28},{28,24},{1,5},{5... | collective-permute-start | bytes 245768 | tf_op jit(solution)/shard_map/ppermute | solution.py:821
  130.7 3.2 %copy-start.3 = (bf16[160,256]{1,0:T(8,128)(2,1)}, bf16[160,256]{1,0:T(8,128)(2,1)S(1)}, u32[]{:S(2)}) copy-start(bf16[160,256]{1,0:T(8,128)(2,1)S(1)} %collective-permute-done.21.refs_3_) | copy-start | bytes 245764
  130.8 2.3 %collective-permute-start.25 = (bf16[160,256]{1,0:T(8,128)(2,1)S(1)}, bf16[160,256]{1,0:T(8,128)(2,1)S(1)}, u32[]{:S(2)}, u32[]{:S(2)}) collective-permute-start(bf16[160,256]{1,0:T(8,128)(2,1)S(1)} %collective-permute-done.21.refs_3_), channel_id=1, source_target_pairs={{0,4},{4,0},{8,12},{12,8},{16,20},{20,16},{24,28},{28,24},{1,5},{5... | collective-permute-start | bytes 245768 | tf_op jit(solution)/shard_map/ppermute | solution.py:821
  132.5 1.5 %copy-start.4 = (bf16[160,256]{1,0:T(8,128)(2,1)}, bf16[160,256]{1,0:T(8,128)(2,1)S(1)}, u32[]{:S(2)}) copy-start(bf16[160,256]{1,0:T(8,128)(2,1)S(1)} %collective-permute-done.20.refs_2_) | copy-start | bytes 245764
  132.5 1.3 collective-permute-start.24
  132.5 1.4 %copy-start.5 = (bf16[160,256]{1,0:T(8,128)(2,1)}, bf16[160,256]{1,0:T(8,128)(2,1)S(1)}, u32[]{:S(2)}) copy-start(bf16[160,256]{1,0:T(8,128)(2,1)S(1)} %collective-permute-done.19.refs_1_) | copy-start | bytes 245764
  132.5 1.4 %collective-permute-start.23 = (bf16[160,256]{1,0:T(8,128)(2,1)S(1)}, bf16[160,256]{1,0:T(8,128)(2,1)S(1)}, u32[]{:S(2)}, u32[]{:S(2)}) collective-permute-start(bf16[160,256]{1,0:T(8,128)(2,1)S(1)} %collective-permute-done.19.refs_1_), channel_id=1, source_target_pairs={{0,4},{4,0},{8,12},{12,8},{16,20},{20,16},{24,28},{28,24},{1,5},{5... | collective-permute-start | bytes 245768 | tf_op jit(solution)/shard_map/ppermute | solution.py:821
  133.0 0.9 copy-start.6
  133.0 0.9 copy-start.7
  133.8 0.6 copy-start.8
  133.9 0.6 copy-start.9
